TPU v7x, 32 devices: a whole 2x2x4 slice. The times are simulated.
32 devices in a mesh: section: 4 (over y, x), seq: 4 (over z), head: 2 (over core).
Axes of the slice: x: 2, y: 2, z: 4, core: 2. Of those that a mesh axis runs over, the one named last changes fastest.
Arguments:
- queries: bfloat16 [4096, 4096], P(('section', 'seq'), 'head'), may hold values from -180 to 180
- keys: bfloat16 [4096, 1024], P(('section', 'seq'), 'head'), may hold values from -6 to 6
- values: bfloat16 [4096, 1024], P(('section', 'seq'), 'head'), may hold values from -6 to 6
- query_pooling_weight: float32 [4, 4096], P(None, 'head'), may hold values from -3 to 3
- key_pooling_weight: float32 [4, 1024], P(None, 'head'), may hold values from -3 to 3
- value_pooling_weight: float32 [4, 1024], P(None, 'head'), may hold values from -3 to 3
- up_weight: float32 [4, 4096], P(None, 'head'), may hold values from -8 to 8
- out_gain: float32 [4096], P('head'), may hold values from 0.1 to 1.9
Outputs:
- attended: bfloat16 [4096, 4096], P(('section', 'seq'), 'head')
All inputs are finite; a program needn't handle non-finite values.
Results may differ from a plain program's by a relative error of at most 0.0067.
Values may be sent and summed in bfloat16 or wider, within the bound.
No kernel may reach another device: no remote copies, remote signals or barrier semaphores. Data moves between devices by JAX's collectives and lax.ppermute only.
A program may use at most 128 MiB of HBM per device.

v0:
```python
import jax
import jax.numpy as jnp
from jax import lax
from jax.sharding import PartitionSpec as P

HEAD_SIZE = 128
D = 4096
POOL_FACTOR = 4
WINDOW_LENGTH = 512


def passed_along(value, axis, steps):
    count = lax.axis_size(axis)
    initial, last = (max(0, -steps), min(count, count - steps))
    return lax.ppermute(value, axis, [(source, source + steps) for source in range(initial, last)])


def pool_rows(source, weights):
    grouped = source.reshape(source.shape[0] // weights.shape[0], weights.shape[0], source.shape[1])
    return jnp.sum(grouped * weights[None], axis=1).astype(jnp.bfloat16)


def window_attention(queries, keys_all, values_all, first_token, reach_count):
    tokens = queries.shape[0]
    kv_heads = keys_all.shape[1] // HEAD_SIZE
    group_length = queries.shape[1] // (kv_heads * HEAD_SIZE)
    shaped_q = queries.reshape(tokens, kv_heads, group_length, HEAD_SIZE)
    shaped_k = keys_all.reshape(-1, kv_heads, HEAD_SIZE)
    shaped_v = values_all.reshape(-1, kv_heads, HEAD_SIZE)
    scores = jnp.einsum(
        "qhgd,khd->hgqk", shaped_q, shaped_k, preferred_element_type=jnp.float32
    ) * HEAD_SIZE ** (-0.5)
    query_pos = first_token + jnp.arange(tokens)
    key_pos = first_token - reach_count * tokens + jnp.arange(keys_all.shape[0])
    allowed = (
        (key_pos[None, :] <= query_pos[:, None])
        & (key_pos[None, :] > query_pos[:, None] - WINDOW_LENGTH)
        & (key_pos[None, :] >= 0)
    )
    scores = jnp.where(allowed, scores, -jnp.inf)
    highest = jnp.max(scores, axis=-1, keepdims=True)
    weights = jnp.exp(scores - highest)
    normalizer = jnp.sum(weights, axis=-1)
    blended = jnp.einsum(
        "hgqk,khd->qhgd", weights.astype(jnp.bfloat16), shaped_v, preferred_element_type=jnp.float32
    )
    return (blended / jnp.transpose(normalizer, (2, 0, 1))[..., None]).reshape(tokens, -1)


def empty_state(query_count, kv_heads, group_length):
    running_max = jnp.full((kv_heads, group_length, query_count), -jnp.inf, jnp.float32)
    running_sum = jnp.zeros((kv_heads, group_length, query_count), jnp.float32)
    running_acc = jnp.zeros((kv_heads, group_length, query_count, HEAD_SIZE), jnp.float32)
    return (running_max, running_sum, running_acc)


def coarse_update(state, query_rows, query_pos, block_keys, block_values, key_pos):
    running_max, running_sum, running_acc = state
    kv_heads = block_keys.shape[1] // HEAD_SIZE
    group_length = query_rows.shape[1] // (kv_heads * HEAD_SIZE)
    shaped_q = query_rows.reshape(query_rows.shape[0], kv_heads, group_length, HEAD_SIZE)
    shaped_k = block_keys.reshape(-1, kv_heads, HEAD_SIZE)
    shaped_v = block_values.reshape(-1, kv_heads, HEAD_SIZE)
    scores = jnp.einsum(
        "qhgd,khd->hgqk", shaped_q, shaped_k, preferred_element_type=jnp.float32
    ) * HEAD_SIZE ** (-0.5)
    scores = jnp.where(key_pos[None, :] <= query_pos[:, None], scores, -jnp.inf)
    newest = jnp.maximum(running_max, jnp.max(scores, axis=-1))
    anchor = jnp.where(newest == -jnp.inf, 0.0, newest)
    weights = jnp.exp(scores - anchor[..., None])
    rescale = jnp.exp(running_max - anchor)
    running_sum = running_sum * rescale + jnp.sum(weights, axis=-1)
    running_acc = running_acc * rescale[..., None] + jnp.einsum(
        "hgqk,khd->hgqd", weights.astype(jnp.bfloat16), shaped_v, preferred_element_type=jnp.float32
    )
    return (newest, running_sum, running_acc)


def guarded_update(single, query_rows, query_pos, block_keys, block_values, key_pos):

    def update_state(carried):
        return coarse_update(carried, query_rows, query_pos, block_keys, block_values, key_pos)

    def keep_state(carried):
        return carried

    return lax.cond(jnp.min(key_pos) <= jnp.max(query_pos), update_state, keep_state, single)


def fold_blocks(state_sets, piece, query_sets, position_fn):
    piece_keys, piece_values = piece
    row_count = piece_keys.shape[0]
    block_rows = row_count
    while block_rows > 2048 and block_rows % 2 == 0:
        block_rows = block_rows // 2
    block_count = row_count // block_rows

    def one_block(step_index, states):
        starting_row = step_index * block_rows
        block_keys = lax.dynamic_slice_in_dim(piece_keys, starting_row, block_rows, 0)
        block_values = lax.dynamic_slice_in_dim(piece_values, starting_row, block_rows, 0)
        key_pos = position_fn(starting_row + jnp.arange(block_rows))
        updated = []
        for query_set, single in zip(query_sets, states):
            updated.append(
                guarded_update(
                    single, query_set[0], query_set[1], block_keys, block_values, key_pos
                )
            )
        return tuple(updated)

    return lax.fori_loop(0, block_count, one_block, state_sets)


def finish_state(state):
    running_max, running_sum, running_acc = state
    safe_sum = jnp.where(running_sum > 0.0, running_sum, 1.0)
    result = running_acc / safe_sum[..., None]
    return jnp.transpose(result, (2, 0, 1, 3)).reshape(result.shape[2], -1)


def per_device(
    queries,
    keys,
    values,
    query_pooling_weight,
    key_pooling_weight,
    value_pooling_weight,
    up_weight,
    out_gain,
):
    tokens = queries.shape[0]
    pooled_rows = tokens // POOL_FACTOR
    kv_heads = keys.shape[1] // HEAD_SIZE
    group_length = queries.shape[1] // (kv_heads * HEAD_SIZE)
    seq_count = lax.axis_size("seq")
    section_count = lax.axis_size("section")
    section_index = lax.axis_index("section")
    seq_index = lax.axis_index("seq")
    position = section_index * seq_count + seq_index
    first_token = position * tokens
    pooled_query_rows = pool_rows(queries, query_pooling_weight)
    pooled_key_rows = pool_rows(keys, key_pooling_weight)
    pooled_value_rows = pool_rows(values, value_pooling_weight)
    reach_count = -(-(WINDOW_LENGTH - 1) // tokens)
    older_keys = []
    older_values = []
    carried_query = jnp.zeros((1, queries.shape[1]), jnp.bfloat16)
    for offset in range(reach_count, 0, -1):
        arrived = passed_along((keys, values, pooled_query_rows[-1:]), ("section", "seq"), offset)
        older_keys.append(arrived[0])
        older_values.append(arrived[1])
        if offset == 1:
            carried_query = arrived[2]
    keys_all = jnp.concatenate(older_keys + [keys], axis=0)
    values_all = jnp.concatenate(older_values + [values], axis=0)
    fine_part = window_attention(queries, keys_all, values_all, first_token, reach_count)
    shifted_q = jnp.concatenate([carried_query, pooled_query_rows[:-1]], axis=0)
    moved = (
        lax.all_to_all(shifted_q, "section", split_axis=1, concat_axis=0, tiled=True),
        lax.all_to_all(pooled_key_rows, "section", split_axis=1, concat_axis=0, tiled=True),
        lax.all_to_all(pooled_value_rows, "section", split_axis=1, concat_axis=0, tiled=True),
    )
    local_rows = jnp.arange(section_count * pooled_rows)
    moved_pos = (
        (local_rows // pooled_rows * seq_count + seq_index) * pooled_rows
        + local_rows % pooled_rows
        - 1
    )
    query_sets = ((moved[0], moved_pos),)
    initial = (empty_state(section_count * pooled_rows, kv_heads // section_count, group_length),)
    group_rows = section_count * pooled_rows

    def regrouped_position(global_rows):
        seq_part = global_rows // group_rows
        section_part = global_rows % group_rows // pooled_rows
        return (section_part * seq_count + seq_part) * pooled_rows + global_rows % pooled_rows

    states = fold_blocks(
        initial,
        (
            lax.all_gather(moved[1], "seq", axis=0, tiled=True),
            lax.all_gather(moved[2], "seq", axis=0, tiled=True),
        ),
        query_sets,
        regrouped_position,
    )
    coarse_part = lax.all_to_all(
        finish_state(states[0]), "section", split_axis=0, concat_axis=1, tiled=True
    )
    expanded_rows = (coarse_part[:, None, :] * up_weight[None]).reshape(tokens, -1)
    combined = fine_part + expanded_rows
    squares = lax.psum(jnp.sum(combined * combined, axis=1), "head")
    scaled = combined * lax.rsqrt(squares / D + 1e-05)[:, None] * out_gain[None]
    return scaled.astype(jnp.bfloat16)


def solution(mesh):
    return jax.shard_map(
        per_device,
        mesh=mesh,
        in_specs=(
            P(("section", "seq"), "head"),
            P(("section", "seq"), "head"),
            P(("section", "seq"), "head"),
            P(None, "head"),
            P(None, "head"),
            P(None, "head"),
            P(None, "head"),
            P("head"),
        ),
        out_specs=P(("section", "seq"), "head"),
        check_vma=False,
    )
```

profile of v0, /device:TPU:0, one launch (start us, length us, event | category | flops | bytes accessed | tf_op | source)
XLA Modules:
  0.0 130.2 jit_solution(9529463733394160281)
XLA Ops:
  0.0 1.8 %copy.49 = bf16[256,512]{0,1:T(8,128)(2,1)} copy(bf16[256,512]{1,0:T(8,128)(2,1)} %param.11) | data formatting | bytes 524288 | tf_op args[1]
  1.9 5.8 %collective-permute-start.3 = (bf16[256,512]{0,1:T(8,128)(2,1)}, bf16[256,512]{0,1:T(8,128)(2,1)}, u32[]{:S(2)}, u32[]{:S(2)}) collective-permute-start(bf16[256,512]{0,1:T(8,128)(2,1)} %copy.49), channel_id=1, source_target_pairs={{0,2},{2,4},{4,6},{6,8},{8,10},{10,12},{12,14},{14,16},{16,18},{18... | collective-permute-start | bytes 786440 | tf_op jit(solution)/shard_map/ppermute | solution.py:15
  7.6 4.5 %collective-permute-start.2 = (bf16[256,512]{0,1:T(8,128)(2,1)}, bf16[256,512]{0,1:T(8,128)(2,1)}, u32[]{:S(2)}, u32[]{:S(2)}) collective-permute-start(bf16[256,512]{0,1:T(8,128)(2,1)} %copy.49), channel_id=1, source_target_pairs={{0,4},{2,6},{4,8},{6,10},{8,12},{10,14},{12,16},{14,18},{16,20},{1... | collective-permute-start | bytes 786440 | tf_op jit(solution)/shard_map/ppermute | solution.py:15
  12.1 3.8 %collective-permute-start.1 = (bf16[256,512]{1,0:T(8,128)(2,1)}, bf16[256,512]{1,0:T(8,128)(2,1)}, u32[]{:S(2)}, u32[]{:S(2)}) collective-permute-start(bf16[256,512]{1,0:T(8,128)(2,1)} %param.12), channel_id=1, source_target_pairs={{0,2},{2,4},{4,6},{6,8},{8,10},{10,12},{12,14},{14,16},{16,18},{18... | collective-permute-start | bytes 786440 | tf_op jit(solution)/shard_map/ppermute | solution.py:15
  15.9 2.9 %collective-permute-start = (bf16[256,512]{1,0:T(8,128)(2,1)}, bf16[256,512]{1,0:T(8,128)(2,1)}, u32[]{:S(2)}, u32[]{:S(2)}) collective-permute-start(bf16[256,512]{1,0:T(8,128)(2,1)} %param.12), channel_id=1, source_target_pairs={{0,4},{2,6},{4,8},{6,10},{8,12},{10,14},{12,16},{14,18},{16,20},{1... | collective-permute-start | bytes 786440 | tf_op jit(solution)/shard_map/ppermute | solution.py:15
  18.8 1.7 %reshape.137 = f32[64,4,2048]{2,1,0:T(4,128)S(1)} reshape(bf16[256,2048]{1,0:T(8,128)(2,1)} %param.10) | data formatting | bytes 3145728 | tf_op jit(solution)/shard_map/convert_element_type | solution.py:20
  20.5 2.2 %multiply_reduce_fusion.1 = bf16[64,2048]{1,0:T(8,128)(2,1)S(1)} fusion(f32[64,4,2048]{2,1,0:T(4,128)S(1)} %reshape.137, f32[4,2048]{1,0:T(4,128)} %param.13), kind=kLoop, calls=%fused_computation.34 | loop fusion | flops 917504 | bytes 2392064 | tf_op jit(solution)/shard_map/reduce_sum | solution.py:20
  23.5 4.4 %collective-permute-start.4 = (bf16[1,2048]{1,0:T(2,128)(2,1)S(1)}, bf16[1,2048]{1,0:T(2,128)(2,1)S(1)}, u32[]{:S(2)}, u32[]{:S(2)}) collective-permute-start(bf16[1,2048]{1,0:T(2,128)(2,1)S(1)} %slice.8), channel_id=1, source_target_pairs={{0,2},{2,4},{4,6},{6,8},{8,10},{10,12},{12,14},{14,16},{16,18},{18... | collective-permute-start | bytes 12296 | tf_op jit(solution)/shard_map/ppermute | solution.py:15
  29.1 3.3 %all-to-all-start.1 = ((bf16[64,4,128]{2,0,1:T(8,128)(2,1)}), bf16[64,4,128]{2,0,1:T(8,128)(2,1)S(1)}, u32[]{:S(2)}, u32[]{:S(2)}) async-start(bf16[64,4,128]{2,0,1:T(8,128)(2,1)} %copy_bitcast_fusion.2), calls=%async_computation.1 | async-start | bytes 131072 | tf_op jit(solution)/shard_map/all_to_all | solution.py:161
  32.4 1.1 reshape.139
  38.4 7.7 %all-to-all-done.1 = bf16[64,4,128]{2,0,1:T(8,128)(2,1)S(1)} async-done(((bf16[64,4,128]{2,0,1:T(8,128)(2,1)}), bf16[64,4,128]{2,0,1:T(8,128)(2,1)S(1)}, u32[]{:S(2)}, u32[]{:S(2)}) %all-to-all-start.1) | async-done | bytes 65568 | tf_op jit(solution)/shard_map/all_to_all | solution.py:161
  46.1 3.3 %all-to-all-start.2 = ((bf16[64,4,128]{2,0,1:T(8,128)(2,1)}), bf16[64,4,128]{2,0,1:T(8,128)(2,1)S(1)}, u32[]{:S(2)}, u32[]{:S(2)}) async-start(bf16[64,4,128]{2,0,1:T(8,128)(2,1)} %copy_bitcast_fusion.1), calls=%async_computation.2 | async-start | bytes 131072 | tf_op jit(solution)/shard_map/all_to_all | solution.py:162
  50.3 4.1 %all-to-all-done.2 = bf16[64,4,128]{2,0,1:T(8,128)(2,1)S(1)} async-done(((bf16[64,4,128]{2,0,1:T(8,128)(2,1)}), bf16[64,4,128]{2,0,1:T(8,128)(2,1)S(1)}, u32[]{:S(2)}, u32[]{:S(2)}) %all-to-all-start.2) | async-done | bytes 65568 | tf_op jit(solution)/shard_map/all_to_all | solution.py:162
  54.4 3.4 %all-to-all-start = ((bf16[64,4,512]{2,0,1:T(8,128)(2,1)}), bf16[64,4,512]{2,0,1:T(8,128)(2,1)S(1)}, u32[]{:S(2)}, u32[]{:S(2)}) async-start(bf16[64,4,512]{2,0,1:T(8,128)(2,1)} %bitcast.102), calls=%async_computation | async-start | bytes 524288 | tf_op jit(solution)/shard_map/all_to_all | solution.py:160
  57.8 14.0 %all_gather.6 = bf16[1024,128]{1,0:T(8,128)(2,1)S(1)} all-gather(bf16[256,128]{1,0:T(8,128)(2,1)S(1)} %bitcast.112), channel_id=1, replica_groups=mesh['section'=4,'seq'=4,'head'=2] {'seq'}, dimensions={0}, use_global_device_ids=true | all-gather | bytes 327680 | tf_op jit(solution)/shard_map/all_gather | solution.py:182
  71.8 13.8 %all_gather.7 = bf16[1024,128]{1,0:T(8,128)(2,1)S(1)} all-gather(bf16[256,128]{1,0:T(8,128)(2,1)S(1)} %bitcast.113), channel_id=1, replica_groups=mesh['section'=4,'seq'=4,'head'=2] {'seq'}, dimensions={0}, use_global_device_ids=true | all-gather | bytes 327680 | tf_op jit(solution)/shard_map/all_gather | solution.py:183
  85.6 3.3 %conditional.1 = ((f32[1,4,256]{2,1,0:T(4,128)S(1)}, f32[1,4,256,128]{3,2,1,0:T(8,128)S(1)})) conditional(s32[]{:T(128)} %convert_element_type.50, (f32[1,4,256]{2,1,0:T(4,128)S(1)}, f32[1,4,256,128]{3,2,1,0:T(8,128)S(1)}) %tuple.19, (s32[1024]{0:T(1024)S(1)}, s32[256]{0:T(256)S(1)}, bf16[4,64,512]{2,1,0:T(8,128)(2,1)S(1)}, ...), branch_computations={%region_7.8_spmd, %region_8.11_spmd} | conditional | flops 548935680 | bytes 16045080 | solution.py:87
  87.6 1.3 %fusion.10 = f32[1,4,256,128]{3,2,1,0:T(8,128)S(1)} fusion(f32[1024,256,4]{1,0,2:T(8,128)S(1)} %get-tuple-element.98, f32[4,256]{1,0:T(4,128)S(1)} %get-tuple-element.96, pred[256,1024]{0,1:T(8,128)(4,1)S(1)} %broadcast_compare_fusion, f32[1,4,256,128]{3,2,1,0:T(8,128)S(1)} %get-tuple-element.75, bf16[1024,128]{1,0:T(8,128)(2,1)S(1)} %get-tuple-element.76, ...), kind=kOutput, calls=%fused_computation.9 | convolution fusion | flops 272891904 | bytes 5775360 | tf_op jit(solution)/shard_map/while/body/eval_jaxpr/cond/branch_1_fun/hgqk,khd->hgqd/dot_general | solution.py:73
  90.5 4.7 %all-to-all-start.3 = ((f32[4,64,512]{2,1,0:T(8,128)}), f32[4,64,512]{2,1,0:T(8,128)S(1)}, u32[]{:S(2)}, u32[]{:S(2)}) async-start(f32[4,64,512]{2,1,0:T(8,128)} %all_to_all.58), calls=%async_computation.3 | async-start | bytes 1048576 | tf_op jit(solution)/shard_map/all_to_all | solution.py:188
  95.2 1.2 pad_maximum_fusion.1
  96.4 2.3 %fusion.25 = (f32[4,4,256]{2,1,0:T(4,128)S(1)}, f32[4,768,256,4]{2,1,3,0:T(8,128)S(1)}) fusion(pred[256,768]{0,1:T(8,128)(4,1)S(1)} %and_and_fusion, bf16[768,4,128,1]{0,2,3,1:T(8,128)(2,1)S(1)} %bitcast.104, bf16[256,4,4,128]{3,2,1,0:T(4,128)(2,1)S(1)} %reshape.135), kind=kOutput, calls=%fused_computation.28 | convolution fusion | flops 814739456 | bytes 14630912 | tf_op jit(solution)/shard_map/qhgd,khd->hgqk/dot_general | solution.py:30
  98.7 2.6 %fusion.23 = f32[4,4,256]{2,1,0:T(4,128)S(1)} fusion(f32[4,768,256,4]{2,1,3,0:T(8,128)S(1)} %get-tuple-element.100, f32[4,4,256]{2,1,0:T(4,128)S(1)} %get-tuple-element.99, pred[256,768]{0,1:T(8,128)(4,1)S(1)} %and_and_fusion), kind=kLoop, calls=%fused_computation.26 | loop fusion | flops 12578816 | bytes 12812288 | tf_op jit(solution)/shard_map/reduce_sum | solution.py:43
  101.3 1.9 %copy-done = f32[4,768,256,4]{2,1,3,0:T(8,128)} copy-done((f32[4,768,256,4]{2,1,3,0:T(8,128)}, f32[4,768,256,4]{2,1,3,0:T(8,128)S(1)}, u32[]{:S(2)}) %copy-start) | copy-done | bytes 12582936
  103.2 1.1 pad_maximum_fusion
  104.3 1.2 copy.48
  106.1 2.8 %mul.151 = f32[256,4,4,128]{3,2,1,0:T(4,128)} reshape(f32[64,4,2048]{2,1,0:T(4,128)S(1)} %broadcast_multiply_fusion) | data formatting | bytes 4194304 | tf_op jit(solution)/shard_map/mul | solution.py:191
  108.9 1.7 %mul.150 = f32[256,2048]{1,0:T(8,128)} reshape(f32[64,4,2048]{2,1,0:T(4,128)S(1)} %broadcast_multiply_fusion) | data formatting | bytes 4194304 | tf_op jit(solution)/shard_map/mul | solution.py:191
  110.6 1.9 %copy.61 = f32[256,4,4,128]{0,3,2,1:T(8,128)S(1)} copy(f32[256,4,4,128]{3,2,1,0:T(4,128)} %mul.151) | data formatting | bytes 4194304 | tf_op jit(solution)/shard_map/mul | solution.py:191
  112.6 9.2 %multiply_reduce_fusion = (f32[256]{0:T(256)S(1)}, f32[256,4,4,128]{0,3,2,1:T(8,128)}) fusion(f32[256,4,4,128]{0,3,2,1:T(8,128)S(1)} %copy.61, f32[256,4,4]{0,2,1:T(4,128)S(1)} %bitcast.114, bf16[768,4,128,1]{0,2,3,1:T(8,128)(2,1)S(1)} %bitcast.111, f32[4,768,256,4]{2,1,3,0:T(8,128)} %copy-done, f32[4,4,256]{2,1,0:T(4,128)S(1)} %get-tuple-element.99, ...), kind=kOutput, calls=%fused_computation.33 | convolution fusion | flops 819986176 | bytes 17794048 | tf_op jit(solution)/shard_map/hgqk,khd->qhgd/dot_general | solution.py:44
  121.8 3.1 %copy.60 = f32[256,2048]{1,0:T(8,128)} copy(f32[256,2048]{0,1:T(8,128)} %bitcast.105) | data formatting | bytes 4194304 | tf_op jit(solution)/shard_map/reshape | solution.py:47
  124.9 2.4 %psum.7 = f32[256]{0:T(256)S(1)} all-reduce(f32[256]{0:T(256)S(1)} %get-tuple-element.101), channel_id=1, replica_groups=mesh['section'=4,'seq'=4,'head'=2] {'head'}, use_global_device_ids=true, to_apply=%region_12.13 | all-reduce | flops 256 | bytes 2048 | tf_op jit(solution)/shard_map/psum | solution.py:193
  127.4 2.9 %multiply_convert_fusion = bf16[256,2048]{1,0:T(8,128)(2,1)} fusion(f32[256,2048]{1,0:T(8,128)} %copy.60, f32[256,2048]{1,0:T(8,128)S(1)} %copy-done.1, f32[2048]{0:T(1024)S(1)} %copy-done.11, f32[256]{0:T(256)S(1)} %add_rsqrt_fusion), kind=kLoop, calls=%fused_computation.32 | loop fusion | flops 2097152 | bytes 5252096 | tf_op jit(solution)/shard_map/convert_element_type | solution.py:195
  (62 shorter events, 10.5 us)
Async XLA Ops:
  0.0 27.9 %copy-start.5 = (bf16[256,512]{1,0:T(8,128)(2,1)S(1)}, bf16[256,512]{1,0:T(8,128)(2,1)}, u32[]{:S(2)}) copy-start(bf16[256,512]{1,0:T(8,128)(2,1)} %param.11) | copy-start | bytes 786436
  0.0 28.1 %copy-start.9 = (f32[4,512]{1,0:T(4,128)S(1)}, f32[4,512]{1,0:T(4,128)}, u32[]{:S(2)}) copy-start(f32[4,512]{1,0:T(4,128)} %param.14) | copy-start | bytes 24580
  0.0 33.6 %copy-start.10 = (f32[4,512]{1,0:T(4,128)S(1)}, f32[4,512]{1,0:T(4,128)}, u32[]{:S(2)}) copy-start(f32[4,512]{1,0:T(4,128)} %param.15) | copy-start | bytes 24580
  1.9 33.0 %copy-start.2 = (bf16[256,2048]{1,0:T(8,128)(2,1)S(1)}, bf16[256,2048]{1,0:T(8,128)(2,1)}, u32[]{:S(2)}) copy-start(bf16[256,2048]{1,0:T(8,128)(2,1)} %param.10) | copy-start | bytes 3145732
  1.9 93.3 %collective-permute-start.3 = (bf16[256,512]{0,1:T(8,128)(2,1)}, bf16[256,512]{0,1:T(8,128)(2,1)}, u32[]{:S(2)}, u32[]{:S(2)}) collective-permute-start(bf16[256,512]{0,1:T(8,128)(2,1)} %copy.49), channel_id=1, source_target_pairs={{0,2},{2,4},{4,6},{6,8},{8,10},{10,12},{12,14},{14,16},{16,18},{18... | collective-permute-start | bytes 786440 | tf_op jit(solution)/shard_map/ppermute | solution.py:15
  7.6 87.6 %collective-permute-start.2 = (bf16[256,512]{0,1:T(8,128)(2,1)}, bf16[256,512]{0,1:T(8,128)(2,1)}, u32[]{:S(2)}, u32[]{:S(2)}) collective-permute-start(bf16[256,512]{0,1:T(8,128)(2,1)} %copy.49), channel_id=1, source_target_pairs={{0,4},{2,6},{4,8},{6,10},{8,12},{10,14},{12,16},{14,18},{16,20},{1... | collective-permute-start | bytes 786440 | tf_op jit(solution)/shard_map/ppermute | solution.py:15
  12.1 91.1 %collective-permute-start.1 = (bf16[256,512]{1,0:T(8,128)(2,1)}, bf16[256,512]{1,0:T(8,128)(2,1)}, u32[]{:S(2)}, u32[]{:S(2)}) collective-permute-start(bf16[256,512]{1,0:T(8,128)(2,1)} %param.12), channel_id=1, source_target_pairs={{0,2},{2,4},{4,6},{6,8},{8,10},{10,12},{12,14},{14,16},{16,18},{18... | collective-permute-start | bytes 786440 | tf_op jit(solution)/shard_map/ppermute | solution.py:15
  15.9 87.3 %collective-permute-start = (bf16[256,512]{1,0:T(8,128)(2,1)}, bf16[256,512]{1,0:T(8,128)(2,1)}, u32[]{:S(2)}, u32[]{:S(2)}) collective-permute-start(bf16[256,512]{1,0:T(8,128)(2,1)} %param.12), channel_id=1, source_target_pairs={{0,4},{2,6},{4,8},{6,10},{8,12},{10,14},{12,16},{14,18},{16,20},{1... | collective-permute-start | bytes 786440 | tf_op jit(solution)/shard_map/ppermute | solution.py:15
  22.8 0.7 copy-start.3
  23.5 25.9 %collective-permute-start.4 = (bf16[1,2048]{1,0:T(2,128)(2,1)S(1)}, bf16[1,2048]{1,0:T(2,128)(2,1)S(1)}, u32[]{:S(2)}, u32[]{:S(2)}) collective-permute-start(bf16[1,2048]{1,0:T(2,128)(2,1)S(1)} %slice.8), channel_id=1, source_target_pairs={{0,2},{2,4},{4,6},{6,8},{8,10},{10,12},{12,14},{14,16},{16,18},{18... | collective-permute-start | bytes 12296 | tf_op jit(solution)/shard_map/ppermute | solution.py:15
  27.9 21.6 %copy-start.4 = (bf16[64,2048]{1,0:T(8,128)(2,1)S(1)}, bf16[64,2048]{1,0:T(8,128)(2,1)}, u32[]{:S(2)}) copy-start(bf16[64,2048]{1,0:T(8,128)(2,1)} %copy-done.3) | copy-start | bytes 786436
  29.1 17.1 %all-to-all-start.1 = ((bf16[64,4,128]{2,0,1:T(8,128)(2,1)}), bf16[64,4,128]{2,0,1:T(8,128)(2,1)S(1)}, u32[]{:S(2)}, u32[]{:S(2)}) async-start(bf16[64,4,128]{2,0,1:T(8,128)(2,1)} %copy_bitcast_fusion.2), calls=%async_computation.1 | async-start | bytes 131072 | tf_op jit(solution)/shard_map/all_to_all | solution.py:161
  46.1 8.2 %all-to-all-start.2 = ((bf16[64,4,128]{2,0,1:T(8,128)(2,1)}), bf16[64,4,128]{2,0,1:T(8,128)(2,1)S(1)}, u32[]{:S(2)}, u32[]{:S(2)}) async-start(bf16[64,4,128]{2,0,1:T(8,128)(2,1)} %copy_bitcast_fusion.1), calls=%async_computation.2 | async-start | bytes 131072 | tf_op jit(solution)/shard_map/all_to_all | solution.py:162
  54.4 31.2 %all-to-all-start = ((bf16[64,4,512]{2,0,1:T(8,128)(2,1)}), bf16[64,4,512]{2,0,1:T(8,128)(2,1)S(1)}, u32[]{:S(2)}, u32[]{:S(2)}) async-start(bf16[64,4,512]{2,0,1:T(8,128)(2,1)} %bitcast.102), calls=%async_computation | async-start | bytes 524288 | tf_op jit(solution)/shard_map/all_to_all | solution.py:160
  90.5 14.9 %all-to-all-start.3 = ((f32[4,64,512]{2,1,0:T(8,128)}), f32[4,64,512]{2,1,0:T(8,128)S(1)}, u32[]{:S(2)}, u32[]{:S(2)}) async-start(f32[4,64,512]{2,1,0:T(8,128)} %all_to_all.58), calls=%async_computation.3 | async-start | bytes 1048576 | tf_op jit(solution)/shard_map/all_to_all | solution.py:188
  98.6 4.6 %copy-start = (f32[4,768,256,4]{2,1,3,0:T(8,128)}, f32[4,768,256,4]{2,1,3,0:T(8,128)S(1)}, u32[]{:S(2)}) copy-start(f32[4,768,256,4]{2,1,3,0:T(8,128)S(1)} %get-tuple-element.100) | copy-start | bytes 37748740
  98.7 4.6 %copy-start.6 = (bf16[256,512]{1,0:T(8,128)(2,1)S(1)}, bf16[256,512]{1,0:T(8,128)(2,1)}, u32[]{:S(2)}) copy-start(bf16[256,512]{1,0:T(8,128)(2,1)} %param.12) | copy-start | bytes 786436
  103.2 2.3 %copy-start.8 = (f32[4,2048]{1,0:T(4,128)S(1)}, f32[4,2048]{1,0:T(4,128)}, u32[]{:S(2)}) copy-start(f32[4,2048]{1,0:T(4,128)} %param.16) | copy-start | bytes 98308
  108.9 3.7 %copy-start.7 = (bf16[768,512]{0,1:T(8,128)(2,1)S(1)}, bf16[768,512]{0,1:T(8,128)(2,1)}, u32[]{:S(2)}) copy-start(bf16[768,512]{0,1:T(8,128)(2,1)} %copy.48) | copy-start | bytes 2359300
  121.8 5.5 %copy-start.1 = (f32[256,2048]{1,0:T(8,128)S(1)}, f32[256,2048]{1,0:T(8,128)}, u32[]{:S(2)}) copy-start(f32[256,2048]{1,0:T(8,128)} %mul.150) | copy-start | bytes 6291460
  121.8 5.5 %copy-start.11 = (f32[2048]{0:T(1024)S(1)}, f32[2048]{0:T(1024)}, u32[]{:S(2)}) copy-start(f32[2048]{0:T(1024)} %param.17) | copy-start | bytes 24580
where the time goes:
time: 131 us; the launch traced here: 130 us
  starting transfers between devices  35.9 us (27%)
  blocking collectives  30.2 us (23%)
  local copies, waits for them, and re-layouts  22.5 us (17%)
  other arithmetic  14.4 us (11%)
  matrix products  13.6 us (10%)
  waiting for transfers between devices  11.9 us (9%)
  between operations  1.65 us (1%)
    ppermute x5, starting transfers between devices, passed_along(): lax.ppermute(value, axis, [(source, source + steps) for source in range(i...  21.3 us
    all_gather x1, blocking collectives, per_device(): lax.all_gather(moved[1], 'seq', axis=0, tiled=True)  14 us
    all_gather x1, blocking collectives, per_device(): lax.all_gather(moved[2], 'seq', axis=0, tiled=True)  13.8 us
    dot_general x1, matrix products, window_attention(): jnp.einsum('hgqk,khd->qhgd', weights.astype(jnp.bfloat16), shaped_v, pref...  9.22 us
    all_to_all x1, waiting for transfers between devices, per_device(): lax.all_to_all(pooled_key_rows, 'section', split_axis=1, concat_axis=0, t...  7.74 us
    mul x4, local copies, waits for them, and re-layouts, per_device(): coarse_part[:, None, :] * up_weight[None]  6.48 us
    all_to_all x1, starting transfers between devices, per_device(): lax.all_to_all(finish_state(states[0]), 'section', split_axis=0, concat_a...  4.65 us
    unnamed x25, local copies, waits for them, and re-layouts  4.52 us
  transfers between devices with their start and end apart: 9, of which 2 were waited for; matrix products, arithmetic and copies ran while one was open for 17% of the time, Pallas kernels for 0%

commit v1 on v0

v1 whole, which is shorter than its diff:
```python
import functools
import math

import jax
import jax.numpy as jnp
from jax import lax
from jax.experimental import pallas as pl
from jax.experimental.pallas import tpu as pltpu
from jax.sharding import PartitionSpec as P

HEAD_SIZE = 128
POOL_FACTOR = 4
WINDOW_LENGTH = 512
KEY_CHUNK = 1024
MASKED = -1e30
EXP2_SCALE = HEAD_SIZE ** (-0.5) * math.log2(math.e)
NT = (((1,), (1,)), ((), ()))
NN = (((1,), (0,)), ((), ()))


def params(mib=48):
    return pltpu.CompilerParams(vmem_limit_bytes=mib * 1024 * 1024)


def cost(flops, nbytes, exps=0):
    return pl.CostEstimate(flops=int(flops), bytes_accessed=int(nbytes), transcendentals=int(exps))


def dot(a, b, dims):
    return lax.dot_general(a, b, dims, preferred_element_type=jnp.float32)


def passed_along(value, axis, steps):
    count = lax.axis_size(axis)
    return lax.ppermute(value, axis, [(source, source + steps) for source in range(count - steps)])


def selection(pooled, tokens, first):
    row = lax.broadcasted_iota(jnp.int32, (POOL_FACTOR * pooled, tokens), 0)
    column = lax.broadcasted_iota(jnp.int32, (POOL_FACTOR * pooled, tokens), 1)
    wanted = POOL_FACTOR * (row % pooled + first) + row // pooled
    return jnp.where(column == wanted, 1.0, 0.0).astype(jnp.bfloat16)


def weighted(picked, weights, pooled):
    total = picked[:pooled] * weights[0:1]
    for i in range(1, POOL_FACTOR):
        total = total + picked[i * pooled : (i + 1) * pooled] * weights[i : i + 1]
    return total


def pool_kv_kernel(k_ref, v_ref, kw_ref, vw_ref, out_ref):
    tokens = k_ref.shape[0]
    pooled = tokens // POOL_FACTOR
    pick = selection(pooled, tokens, 0)
    both = jnp.concatenate([k_ref[...], v_ref[...]], axis=1)
    weights = jnp.concatenate([kw_ref[...], vw_ref[...]], axis=1)
    result = weighted(dot(pick, both, NN), weights, pooled).astype(jnp.bfloat16)
    for z in range(out_ref.shape[1]):
        out_ref[0, z] = result


def pool_kv(keys, values, kw, vw, copies):
    tokens, columns = keys.shape
    heads = columns // HEAD_SIZE
    pooled = tokens // POOL_FACTOR
    kv_spec = pl.BlockSpec((tokens, HEAD_SIZE), lambda h: (0, h))
    w_spec = pl.BlockSpec((POOL_FACTOR, HEAD_SIZE), lambda h: (0, h))
    return pl.pallas_call(
        pool_kv_kernel,
        grid=(heads,),
        in_specs=[kv_spec, kv_spec, w_spec, w_spec],
        out_specs=pl.BlockSpec((1, copies, pooled, 2 * HEAD_SIZE), lambda h: (h, 0, 0, 0)),
        out_shape=jax.ShapeDtypeStruct((heads, copies, pooled, 2 * HEAD_SIZE), jnp.bfloat16),
        compiler_params=params(),
        cost_estimate=cost(4 * tokens * tokens * columns, 4 * tokens * columns + 2 * copies * tokens * columns),
    )(keys, values, kw, vw)


def pool_q_kernel(q_ref, tail_ref, w_ref, out_ref):
    tokens = q_ref.shape[0]
    pooled = tokens // POOL_FACTOR
    tail_rows = tail_ref.shape[0]
    picked = dot(selection(pooled, tokens, -1), q_ref[...], NN)
    picked = picked + dot(selection(pooled, tail_rows, tail_rows // POOL_FACTOR - 1), tail_ref[...], NN)
    out_ref[0] = weighted(picked, w_ref[...], pooled).astype(jnp.bfloat16)


def pool_q(queries, tail, qw, heads):
    tokens, columns = queries.shape
    pooled = tokens // POOL_FACTOR
    width = columns // heads
    return pl.pallas_call(
        pool_q_kernel,
        grid=(heads,),
        in_specs=[
            pl.BlockSpec((tokens, width), lambda h: (0, h)),
            pl.BlockSpec((tail.shape[0], width), lambda h: (0, h)),
            pl.BlockSpec((POOL_FACTOR, width), lambda h: (0, h)),
        ],
        out_specs=pl.BlockSpec((1, pooled, width), lambda h: (h, 0, 0)),
        out_shape=jax.ShapeDtypeStruct((heads, pooled, width), jnp.bfloat16),
        compiler_params=params(),
        cost_estimate=cost(2 * tokens * tokens * columns, 3 * tokens * columns),
    )(queries, tail, qw)


def with_ones(values):
    return jnp.concatenate([values, jnp.ones_like(values)], axis=1)


def coarse_kernel(seq_count, z_ref, q_ref, kv_ref, out_ref):
    sections, pooled, width = q_ref.shape
    group = width // HEAD_SIZE
    rows = group * pooled
    z = z_ref[0]
    for s in range(sections):
        q = q_ref[s]
        stacked = jnp.concatenate([q[:, g * HEAD_SIZE : (g + 1) * HEAD_SIZE] for g in range(group)], axis=0)
        reach = (s + 1) * seq_count * pooled
        row = lax.broadcasted_iota(jnp.int32, (rows, 1), 0) % pooled
        query_pos = (s * seq_count + z) * pooled + row - 1
        highest = total = None
        for start in range(0, reach, KEY_CHUNK):
            size = min(KEY_CHUNK, reach - start)
            blocks = slice(start // pooled, (start + size) // pooled)
            keys = kv_ref[blocks, :, :HEAD_SIZE].reshape(size, HEAD_SIZE)
            values = kv_ref[blocks, :, HEAD_SIZE:].reshape(size, HEAD_SIZE)
            scores = dot(stacked, keys, NT)
            key_pos = start + lax.broadcasted_iota(jnp.int32, (rows, size), 1)
            scores = jnp.where(key_pos <= query_pos, scores, MASKED)
            newest = jnp.max(scores, axis=1, keepdims=True)
            if highest is not None:
                newest = jnp.maximum(newest, highest)
            weights = jnp.exp2((scores - newest) * EXP2_SCALE).astype(jnp.bfloat16)
            part = dot(weights, with_ones(values), NN)
            total = part if total is None else total * jnp.exp2((highest - newest) * EXP2_SCALE) + part
            highest = newest
        result = total[:, :HEAD_SIZE] / total[:, HEAD_SIZE:]
        result = jnp.where(query_pos >= 0, result, 0.0).astype(jnp.bfloat16)
        for g in range(group):
            out_ref[s, :, g * HEAD_SIZE : (g + 1) * HEAD_SIZE] = result[g * pooled : (g + 1) * pooled]


def coarse_attention(z, queries, kv, seq_count):
    sections, pooled, width = queries.shape
    pairs = queries.size // HEAD_SIZE * kv.shape[0] * pooled
    return pl.pallas_call(
        functools.partial(coarse_kernel, seq_count),
        in_specs=[
            pl.BlockSpec(memory_space=pltpu.SMEM),
            pl.BlockSpec(memory_space=pltpu.VMEM),
            pl.BlockSpec(memory_space=pltpu.VMEM),
        ],
        out_specs=pl.BlockSpec(memory_space=pltpu.VMEM),
        out_shape=jax.ShapeDtypeStruct(queries.shape, jnp.bfloat16),
        compiler_params=params(),
        cost_estimate=cost(4 * pairs * HEAD_SIZE, 2 * (2 * queries.size + kv.size), pairs),
    )(z, queries, kv)


def fine_kernel(pos_ref, q_ref, k0_ref, k1_ref, k2_ref, v0_ref, v1_ref, v2_ref, coarse_ref, up_ref, comb_ref, sq_ref):
    tokens, width = q_ref.shape
    pooled = tokens // POOL_FACTOR
    head = pl.program_id(0)
    position = pos_ref[0]
    bias1 = jnp.where(position >= 1, 0.0, MASKED).astype(jnp.float32)
    bias2 = jnp.where(position >= 2, 0.0, MASKED).astype(jnp.float32)
    row = lax.broadcasted_iota(jnp.int32, (tokens, tokens), 0)
    column = lax.broadcasted_iota(jnp.int32, (tokens, tokens), 1)
    own = column <= row
    keys = [ref[...] for ref in (k0_ref, k1_ref, k2_ref)]
    values = [with_ones(ref[...]) for ref in (v0_ref, v1_ref, v2_ref)]
    token = lax.broadcasted_iota(jnp.int32, (tokens, pooled), 0)
    spread = jnp.where(token // POOL_FACTOR == lax.broadcasted_iota(jnp.int32, (tokens, pooled), 1), 1.0, 0.0)
    upsampled = dot(spread.astype(jnp.bfloat16), coarse_ref[0], NN)
    up = up_ref[...]
    up = jnp.concatenate([up, up], axis=0)
    upsampled = (upsampled.reshape(tokens // 8, 8, width) * up[None]).reshape(tokens, width)
    squares = jnp.zeros((tokens, HEAD_SIZE), jnp.float32)
    for g in range(width // HEAD_SIZE):
        columns = slice(g * HEAD_SIZE, (g + 1) * HEAD_SIZE)
        q = q_ref[:, columns]
        outer = jnp.where(own, dot(q, keys[0], NT), dot(q, keys[2], NT) + bias2)
        inner = dot(q, keys[1], NT) + bias1
        highest = jnp.max(jnp.maximum(outer, inner), axis=1, keepdims=True)
        outer = jnp.exp2((outer - highest) * EXP2_SCALE)
        inner = jnp.exp2((inner - highest) * EXP2_SCALE).astype(jnp.bfloat16)
        first = jnp.where(own, outer, 0.0).astype(jnp.bfloat16)
        last = jnp.where(own, 0.0, outer).astype(jnp.bfloat16)
        total = dot(first, values[0], NN) + dot(inner, values[1], NN) + dot(last, values[2], NN)
        combined = total[:, :HEAD_SIZE] / total[:, HEAD_SIZE:] + upsampled[:, columns]
        comb_ref[:, columns] = combined
        squares = squares + combined * combined

    @pl.when(head == 0)
    def _():
        sq_ref[...] = squares

    @pl.when(head > 0)
    def _():
        sq_ref[...] += squares

    @pl.when(head == pl.num_programs(0) - 1)
    def _():
        sq_ref[...] = jnp.broadcast_to(jnp.sum(sq_ref[...], axis=1, keepdims=True), sq_ref.shape)


def fine_attention(position, queries, keys, values, coarse, up_weight):
    tokens, columns = queries.shape
    heads = keys[0].shape[1] // HEAD_SIZE
    width = columns // heads
    pooled = tokens // POOL_FACTOR
    kv_spec = pl.BlockSpec((tokens, HEAD_SIZE), lambda h: (0, h))
    wide = pl.BlockSpec((tokens, width), lambda h: (0, h))
    pairs = tokens * tokens * 3 * columns // HEAD_SIZE
    return pl.pallas_call(
        fine_kernel,
        grid=(heads,),
        in_specs=[pl.BlockSpec(memory_space=pltpu.SMEM), wide]
        + [kv_spec] * 6
        + [pl.BlockSpec((1, pooled, width), lambda h: (h, 0, 0)), pl.BlockSpec((POOL_FACTOR, width), lambda h: (0, h))],
        out_specs=[wide, pl.BlockSpec((tokens, HEAD_SIZE), lambda h: (0, 0))],
        out_shape=[
            jax.ShapeDtypeStruct((tokens, columns), jnp.float32),
            jax.ShapeDtypeStruct((tokens, HEAD_SIZE), jnp.float32),
        ],
        compiler_params=params(),
        cost_estimate=cost(4 * pairs * HEAD_SIZE, 12 * tokens * columns, pairs),
    )(position, queries, *keys, *values, coarse, up_weight)


def norm_kernel(full, comb_ref, mine_ref, other_ref, gain_ref, out_ref):
    mean = (mine_ref[:, :1] + other_ref[:, :1]) / full
    out_ref[...] = (comb_ref[...] * lax.rsqrt(mean + 1e-05) * gain_ref[...]).astype(jnp.bfloat16)


def normalized(combined, mine, other, gain, full):
    tokens, columns = combined.shape
    parts = 4
    wide = pl.BlockSpec((tokens, columns // parts), lambda h: (0, h))
    narrow = pl.BlockSpec((tokens, HEAD_SIZE), lambda h: (0, 0))
    return pl.pallas_call(
        functools.partial(norm_kernel, full),
        grid=(parts,),
        in_specs=[wide, narrow, narrow, pl.BlockSpec((1, columns // parts), lambda h: (0, h))],
        out_specs=wide,
        out_shape=jax.ShapeDtypeStruct((tokens, columns), jnp.bfloat16),
        compiler_params=params(),
        cost_estimate=cost(3 * tokens * columns, 6 * tokens * columns),
    )(combined, mine, other, gain)


def per_device(queries, keys, values, qw, kw, vw, up_weight, out_gain):
    tokens, columns = queries.shape
    heads = keys.shape[1] // HEAD_SIZE
    seq_count = lax.axis_size("seq")
    section_count = lax.axis_size("section")
    head_count = lax.axis_size("head")
    if WINDOW_LENGTH != 2 * tokens or heads != section_count or head_count != 2:
        raise ValueError("unsupported sizes")
    line = ("section", "seq")
    z = lax.axis_index("seq")
    position = lax.axis_index("section") * seq_count + z

    tail = passed_along(queries[-16:], line, 1)
    k1 = passed_along(keys, line, 1)
    v1 = passed_along(values, line, 1)
    pooled_kv = pool_kv(keys, values, kw, vw, seq_count)
    pooled_kv = pooled_kv.reshape((-1,) + pooled_kv.shape[2:])
    moved_kv = lax.all_to_all(pooled_kv, line, split_axis=0, concat_axis=0, tiled=True)
    pooled_q = pool_q(queries, tail, qw, heads)
    moved_q = lax.all_to_all(pooled_q, "section", split_axis=0, concat_axis=0, tiled=True)
    k2 = passed_along(k1, line, 1)
    v2 = passed_along(v1, line, 1)
    coarse = coarse_attention(z[None], moved_q, moved_kv, seq_count)
    coarse = lax.all_to_all(coarse, "section", split_axis=0, concat_axis=0, tiled=True)
    combined, mine = fine_attention(position[None], queries, (keys, k1, k2), (values, v1, v2), coarse, up_weight)
    other = lax.ppermute(mine, "head", [(0, 1), (1, 0)])
    return normalized(combined, mine, other, out_gain[None], head_count * columns)


def solution(mesh):
    rows = P(("section", "seq"), "head")
    return jax.shard_map(
        per_device,
        mesh=mesh,
        in_specs=(rows, rows, rows, P(None, "head"), P(None, "head"), P(None, "head"), P(None, "head"), P("head")),
        out_specs=rows,
        check_vma=False,
    )
```

time: 131 us -> 85 us (0.65)
  blocking collectives: 30.2 us -> 0 us
  local copies, waits for them, and re-layouts: 22.5 us -> 4.23 us
  Pallas kernels: 0 us -> 15 us
  other arithmetic: 14.4 us -> 0 us
  matrix products: 13.6 us -> 0 us
  starting transfers between devices: 35.9 us -> 46.4 us
  waiting for transfers between devices: 11.9 us -> 18.5 us
  between operations: 1.65 us -> 0.11 us
    all_gather x2 -> x0, blocking collectives: 27.8 us -> none  [the longest x1 14 us: per_device(): lax.all_gather(moved[1], 'seq', axis=0, tiled=True)]
    pallas_call x0 -> x5, Pallas kernels: none -> 15 us  [the longest x1 6.32 us: fine_attention(): pl.pallas_call(fine_kernel, grid=(heads,), in_specs=[pl.BlockSpec(memory_...]
    dot_general x4 -> x0, matrix products: 13.6 us -> none  [the longest x1 9.22 us: window_attention(): jnp.einsum('hgqk,khd->qhgd', weights.astype(jnp.bfloat16), shaped_v, pref...]
    ppermute x5 -> x6, waiting for transfers between devices: 0.01 us -> 11.2 us  [the longest x5 9.82 us: passed_along(): lax.ppermute(value, axis, [(source, source + steps) for source in range(c...]
    all_to_all x4 -> x3, starting transfers between devices: 14.6 us -> 24.2 us  [the longest x1 13.4 us: per_device(): lax.all_to_all(coarse, 'section', split_axis=0, concat_axis=0, tiled=True)]
    mul x4 -> x0, local copies, waits for them, and re-layouts: 6.48 us -> none  [per_device(): coarse_part[:, None, :] * up_weight[None]]
    reduce_sum x5 -> x0, other arithmetic: 6.46 us -> none  [the longest x3 2.95 us: pool_rows(): return jnp.sum(grouped * weights[None], axis=1).astype(jnp.bfloat16)]
    all_to_all x4 -> x3, waiting for transfers between devices: 11.9 us -> 7.32 us  [the longest x1 5.36 us: per_device(): lax.all_to_all(coarse, 'section', split_axis=0, concat_axis=0, tiled=True)]
  transfers between devices with their start and end apart: 9 -> 9, of which waited for: 2 -> 5; matrix products, arithmetic and copies ran while one was open for 17% -> 0% of each run, Pallas kernels for 0% -> 5%
where the time goes in v1:
time: 85 us; the launch traced here: 84.3 us
  starting transfers between devices  46.4 us (55%)
  waiting for transfers between devices  18.5 us (22%)
  Pallas kernels  15 us (18%)
  local copies, waits for them, and re-layouts  4.23 us (5%)
    ppermute x5, starting transfers between devices, passed_along(): lax.ppermute(value, axis, [(source, source + steps) for source in range(c...  22.2 us
    all_to_all x1, starting transfers between devices, per_device(): lax.all_to_all(coarse, 'section', split_axis=0, concat_axis=0, tiled=True)  13.4 us
    ppermute x5, waiting for transfers between devices, passed_along(): lax.ppermute(value, axis, [(source, source + steps) for source in range(c...  9.82 us
    all_to_all x1, starting transfers between devices, per_device(): lax.all_to_all(pooled_q, 'section', split_axis=0, concat_axis=0, tiled=True)  7.2 us
    pallas_call x1, Pallas kernels, fine_attention(): pl.pallas_call(fine_kernel, grid=(heads,), in_specs=[pl.BlockSpec(memory_...  6.32 us
    all_to_all x1, waiting for transfers between devices, per_device(): lax.all_to_all(coarse, 'section', split_axis=0, concat_axis=0, tiled=True)  5.36 us
    all_to_all x1, starting transfers between devices, per_device(): lax.all_to_all(pooled_kv, line, split_axis=0, concat_axis=0, tiled=True)  3.57 us
    unnamed x18, local copies, waits for them, and re-layouts  3.39 us
  transfers between devices with their start and end apart: 9, of which 5 were waited for; matrix products, arithmetic and copies ran while one was open for 0% of the time, Pallas kernels for 5%

profile of v1, /device:TPU:0, one launch (start us, length us, event | category | flops | bytes accessed | tf_op | source)
XLA Modules:
  0.0 84.3 jit_solution(15869908033882243961)
XLA Ops:
  0.0 0.8 %slice.3 = bf16[16,2048]{1,0:T(8,128)(2,1)S(1)} slice(bf16[256,2048]{1,0:T(8,128)(2,1)} %q_ref.3), slice={[240:256], [0:2048]} | slice | bytes 131072 | tf_op jit(solution)/shard_map/slice | solution.py:266
  0.8 4.9 %collective-permute-start.4 = (bf16[16,2048]{1,0:T(8,128)(2,1)S(1)}, bf16[16,2048]{1,0:T(8,128)(2,1)S(1)}, u32[]{:S(2)}, u32[]{:S(2)}) collective-permute-start(bf16[16,2048]{1,0:T(8,128)(2,1)S(1)} %slice.3), channel_id=1, source_target_pairs={{0,2},{2,4},{4,6},{6,8},{8,10},{10,12},{12,14},{14,16},{16,18},{18... | collective-permute-start | bytes 196616 | tf_op jit(solution)/shard_map/ppermute | solution.py:35
  5.8 1.9 %collective-permute-done.4.tail_ref = bf16[16,2048]{1,0:T(8,128)(2,1)S(1)} collective-permute-done((bf16[16,2048]{1,0:T(8,128)(2,1)S(1)}, bf16[16,2048]{1,0:T(8,128)(2,1)S(1)}, u32[]{:S(2)}, u32[]{:S(2)}) %collective-permute-start.4) | collective-permute-done | bytes 65568 | tf_op jit(solution)/shard_map/ppermute | solution.py:35
  7.7 1.2 %copy-done = bf16[256,2048]{1,0:T(8,128)(2,1)S(1)} copy-done((bf16[256,2048]{1,0:T(8,128)(2,1)S(1)}, bf16[256,2048]{1,0:T(8,128)(2,1)}, u32[]{:S(2)}) %copy-start) | copy-done | bytes 1048600
  8.9 0.8 copy-done.4
  9.6 2.2 %shard_map.82 = bf16[4,64,512]{2,1,0:T(8,128)(2,1)} custom-call(bf16[256,2048]{1,0:T(8,128)(2,1)S(1)} %copy-done, bf16[16,2048]{1,0:T(8,128)(2,1)S(1)} %collective-permute-done.4.tail_ref, f32[4,2048]{1,0:T(4,128)S(1)} %copy-done.4), custom_call_target="tpu_custom_call" | custom-call | flops 268435456 | bytes 1572864 | tf_op jit(solution)/shard_map/pallas_call | solution.py:93
  11.9 7.2 %all-to-all-start = ((bf16[4,64,512]{2,1,0:T(8,128)(2,1)}), bf16[4,64,512]{2,1,0:T(8,128)(2,1)S(1)}, u32[]{:S(2)}, u32[]{:S(2)}) async-start(bf16[4,64,512]{2,1,0:T(8,128)(2,1)} %shard_map.82), calls=%async_computation | async-start | bytes 524288 | tf_op jit(solution)/shard_map/all_to_all | solution.py:273
  19.1 0.0 copy-done.2
  19.1 0.0 copy-done.3
  19.1 0.7 copy-done.5
  19.8 0.7 copy-done.6
  20.5 2.0 %shard_map.83 = bf16[4,4,64,256]{3,2,1,0:T(8,128)(2,1)} custom-call(bf16[256,512]{1,0:T(8,128)(2,1)S(1)} %copy-done.2, bf16[256,512]{1,0:T(8,128)(2,1)S(1)} %copy-done.3, f32[4,512]{1,0:T(4,128)S(1)} %copy-done.5, f32[4,512]{1,0:T(4,128)S(1)} %copy-done.6), custom_call_target="tpu_custom_call" | custom-call | flops 134217728 | bytes 1572864 | tf_op jit(solution)/shard_map/pallas_call | solution.py:69
  22.5 2.0 %all-to-all-done.q_ref = bf16[4,64,512]{2,1,0:T(8,128)(2,1)S(1)} async-done(((bf16[4,64,512]{2,1,0:T(8,128)(2,1)}), bf16[4,64,512]{2,1,0:T(8,128)(2,1)S(1)}, u32[]{:S(2)}, u32[]{:S(2)}) %all-to-all-start) | async-done | bytes 262176 | tf_op jit(solution)/shard_map/all_to_all | solution.py:273
  24.4 3.6 %all-to-all-start.1 = ((bf16[16,64,256]{2,1,0:T(8,128)(2,1)}), bf16[16,64,256]{2,1,0:T(8,128)(2,1)S(1)}, u32[]{:S(2)}, u32[]{:S(2)}) async-start(bf16[16,64,256]{2,1,0:T(8,128)(2,1)} %bitcast.2), calls=%async_computation.1 | async-start | bytes 1048576 | tf_op jit(solution)/shard_map/all_to_all | solution.py:271
  28.0 3.7 %collective-permute-start = (bf16[256,512]{1,0:T(8,128)(2,1)S(1)}, bf16[256,512]{1,0:T(8,128)(2,1)S(1)}, u32[]{:S(2)}, u32[]{:S(2)}) collective-permute-start(bf16[256,512]{1,0:T(8,128)(2,1)S(1)} %copy-done.2), channel_id=1, source_target_pairs={{0,2},{2,4},{4,6},{6,8},{8,10},{10,12},{12,14},{14,16},{16,18},{18... | collective-permute-start | bytes 786440 | tf_op jit(solution)/shard_map/ppermute | solution.py:35
  31.7 3.4 %collective-permute-start.2 = (bf16[256,512]{1,0:T(8,128)(2,1)S(1)}, bf16[256,512]{1,0:T(8,128)(2,1)S(1)}, u32[]{:S(2)}, u32[]{:S(2)}) collective-permute-start(bf16[256,512]{1,0:T(8,128)(2,1)S(1)} %copy-done.3), channel_id=1, source_target_pairs={{0,2},{2,4},{4,6},{6,8},{8,10},{10,12},{12,14},{14,16},{16,18},{18... | collective-permute-start | bytes 786440 | tf_op jit(solution)/shard_map/ppermute | solution.py:35
  35.1 7.9 %collective-permute-done.k1_ref = bf16[256,512]{1,0:T(8,128)(2,1)S(1)} collective-permute-done((bf16[256,512]{1,0:T(8,128)(2,1)S(1)}, bf16[256,512]{1,0:T(8,128)(2,1)S(1)}, u32[]{:S(2)}, u32[]{:S(2)}) %collective-permute-start) | collective-permute-done | bytes 262176 | tf_op jit(solution)/shard_map/ppermute | solution.py:35
  43.0 4.6 %collective-permute-start.1 = (bf16[256,512]{1,0:T(8,128)(2,1)S(1)}, bf16[256,512]{1,0:T(8,128)(2,1)S(1)}, u32[]{:S(2)}, u32[]{:S(2)}) collective-permute-start(bf16[256,512]{1,0:T(8,128)(2,1)S(1)} %collective-permute-done.k1_ref), channel_id=1, source_target_pairs={{0,2},{2,4},{4,6},{6,8},{8,10},{10,12},{12,14},{14,16},{16,18},{18... | collective-permute-start | bytes 786440 | tf_op jit(solution)/shard_map/ppermute | solution.py:35
  47.6 0.0 collective-permute-done.2.v1_ref
  47.6 5.6 %collective-permute-start.3 = (bf16[256,512]{1,0:T(8,128)(2,1)S(1)}, bf16[256,512]{1,0:T(8,128)(2,1)S(1)}, u32[]{:S(2)}, u32[]{:S(2)}) collective-permute-start(bf16[256,512]{1,0:T(8,128)(2,1)S(1)} %collective-permute-done.2.v1_ref), channel_id=1, source_target_pairs={{0,2},{2,4},{4,6},{6,8},{8,10},{10,12},{12,14},{14,16},{16,18},{18... | collective-permute-start | bytes 786440 | tf_op jit(solution)/shard_map/ppermute | solution.py:35
  53.3 0.0 all-to-all-done.1.kv_ref
  53.3 2.6 %shard_map.84 = bf16[4,64,512]{2,1,0:T(8,128)(2,1)} custom-call(s32[1]{0:T(128)} %bitcast.1.z_ref, bf16[4,64,512]{2,1,0:T(8,128)(2,1)S(1)} %all-to-all-done.q_ref, bf16[16,64,256]{2,1,0:T(8,128)(2,1)S(1)} %all-to-all-done.1.kv_ref), custom_call_target="tpu_custom_call" | custom-call | flops 536870912 | bytes 1048576 | tf_op jit(solution)/shard_map/pallas_call | solution.py:148
  55.9 13.4 %all-to-all-start.2 = ((bf16[4,64,512]{2,1,0:T(8,128)(2,1)}), bf16[4,64,512]{2,1,0:T(8,128)(2,1)S(1)}, u32[]{:S(2)}, u32[]{:S(2)}) async-start(bf16[4,64,512]{2,1,0:T(8,128)(2,1)} %shard_map.84), calls=%async_computation.2 | async-start | bytes 524288 | tf_op jit(solution)/shard_map/all_to_all | solution.py:277
  69.3 0.0 collective-permute-done.1.k2_ref
  69.3 0.0 collective-permute-done.3.v2_ref
  69.3 5.4 %all-to-all-done.2.coarse_ref = bf16[4,64,512]{2,1,0:T(8,128)(2,1)S(1)} async-done(((bf16[4,64,512]{2,1,0:T(8,128)(2,1)}), bf16[4,64,512]{2,1,0:T(8,128)(2,1)S(1)}, u32[]{:S(2)}, u32[]{:S(2)}) %all-to-all-start.2) | async-done | bytes 262176 | tf_op jit(solution)/shard_map/all_to_all | solution.py:277
  74.7 0.0 copy-done.8
  74.7 6.3 %shard_map.85 = (f32[256,2048]{1,0:T(8,128)S(1)}, f32[256,128]{1,0:T(8,128)S(1)}) custom-call(s32[1]{0:T(128)} %bitcast.pos_ref, bf16[256,2048]{1,0:T(8,128)(2,1)S(1)} %copy-done.1, bf16[256,512]{1,0:T(8,128)(2,1)S(1)} %copy-done.2, bf16[256,512]{1,0:T(8,128)(2,1)S(1)} %collective-permute-done.k1_ref, bf16[256,512]{1,0:T(8,128)(2,1)S(1)} %collective-permute-done.1.k2_ref, ...), custom_call_target="tpu_custom_call" | custom-call | flops 1610612736 | bytes 6291456 | tf_op jit(solution)/shard_map/pallas_call | solution.py:217
  81.0 0.1 collective-permute-start.5
  81.1 1.3 %collective-permute-done.5.other_ref = f32[256,128]{1,0:T(8,128)S(1)} collective-permute-done((f32[256,128]{1,0:T(8,128)S(1)}, f32[256,128]{1,0:T(8,128)S(1)}, u32[]{:S(2)}, u32[]{:S(2)}) %collective-permute-start.5) | collective-permute-done | bytes 131104 | tf_op jit(solution)/shard_map/ppermute | solution.py:279
  82.4 0.0 copy-done.7
  82.4 1.9 %shard_map.86 = bf16[256,2048]{1,0:T(8,128)(2,1)} custom-call(f32[256,2048]{1,0:T(8,128)S(1)} %get-tuple-element.7.comb_ref, f32[256,128]{1,0:T(8,128)S(1)} %get-tuple-element.8.mine_ref, f32[256,128]{1,0:T(8,128)S(1)} %collective-permute-done.5.other_ref, f32[1,2048]{1,0:T(1,128)S(1)} %bitcast.4), custom_call_target="tpu_custom_call" | custom-call | flops 1572864 | bytes 3145728 | tf_op jit(solution)/shard_map/pallas_call | solution.py:243
  (10 shorter events, 0.0 us)
Async XLA Ops:
  0.8 6.8 %collective-permute-start.4 = (bf16[16,2048]{1,0:T(8,128)(2,1)S(1)}, bf16[16,2048]{1,0:T(8,128)(2,1)S(1)}, u32[]{:S(2)}, u32[]{:S(2)}) collective-permute-start(bf16[16,2048]{1,0:T(8,128)(2,1)S(1)} %slice.3), channel_id=1, source_target_pairs={{0,2},{2,4},{4,6},{6,8},{8,10},{10,12},{12,14},{14,16},{16,18},{18... | collective-permute-start | bytes 196616 | tf_op jit(solution)/shard_map/ppermute | solution.py:35
  7.7 1.2 %copy-start = (bf16[256,2048]{1,0:T(8,128)(2,1)S(1)}, bf16[256,2048]{1,0:T(8,128)(2,1)}, u32[]{:S(2)}) copy-start(bf16[256,2048]{1,0:T(8,128)(2,1)} %q_ref.3) | copy-start | bytes 3145732
  8.9 0.8 copy-start.4
  9.6 9.4 %copy-start.2 = (bf16[256,512]{1,0:T(8,128)(2,1)S(1)}, bf16[256,512]{1,0:T(8,128)(2,1)}, u32[]{:S(2)}) copy-start(bf16[256,512]{1,0:T(8,128)(2,1)} %k0_ref.1) | copy-start | bytes 786436
  9.6 9.4 %copy-start.3 = (bf16[256,512]{1,0:T(8,128)(2,1)S(1)}, bf16[256,512]{1,0:T(8,128)(2,1)}, u32[]{:S(2)}) copy-start(bf16[256,512]{1,0:T(8,128)(2,1)} %v0_ref.1) | copy-start | bytes 786436
  11.9 12.6 %all-to-all-start = ((bf16[4,64,512]{2,1,0:T(8,128)(2,1)}), bf16[4,64,512]{2,1,0:T(8,128)(2,1)S(1)}, u32[]{:S(2)}, u32[]{:S(2)}) async-start(bf16[4,64,512]{2,1,0:T(8,128)(2,1)} %shard_map.82), calls=%async_computation | async-start | bytes 524288 | tf_op jit(solution)/shard_map/all_to_all | solution.py:273
  19.1 0.7 copy-start.5
  19.8 0.7 copy-start.6
  20.5 54.2 %copy-start.1 = (bf16[256,2048]{1,0:T(8,128)(2,1)S(1)}, bf16[256,2048]{1,0:T(8,128)(2,1)}, u32[]{:S(2)}) copy-start(bf16[256,2048]{1,0:T(8,128)(2,1)} %q_ref.3) | copy-start | bytes 3145732
  20.5 54.2 %copy-start.8 = (f32[4,2048]{1,0:T(4,128)S(1)}, f32[4,2048]{1,0:T(4,128)}, u32[]{:S(2)}) copy-start(f32[4,2048]{1,0:T(4,128)} %up_ref.1) | copy-start | bytes 98308
  24.4 28.8 %all-to-all-start.1 = ((bf16[16,64,256]{2,1,0:T(8,128)(2,1)}), bf16[16,64,256]{2,1,0:T(8,128)(2,1)S(1)}, u32[]{:S(2)}, u32[]{:S(2)}) async-start(bf16[16,64,256]{2,1,0:T(8,128)(2,1)} %bitcast.2), calls=%async_computation.1 | async-start | bytes 1048576 | tf_op jit(solution)/shard_map/all_to_all | solution.py:271
  28.0 15.0 %collective-permute-start = (bf16[256,512]{1,0:T(8,128)(2,1)S(1)}, bf16[256,512]{1,0:T(8,128)(2,1)S(1)}, u32[]{:S(2)}, u32[]{:S(2)}) collective-permute-start(bf16[256,512]{1,0:T(8,128)(2,1)S(1)} %copy-done.2), channel_id=1, source_target_pairs={{0,2},{2,4},{4,6},{6,8},{8,10},{10,12},{12,14},{14,16},{16,18},{18... | collective-permute-start | bytes 786440 | tf_op jit(solution)/shard_map/ppermute | solution.py:35
  31.7 15.9 %collective-permute-start.2 = (bf16[256,512]{1,0:T(8,128)(2,1)S(1)}, bf16[256,512]{1,0:T(8,128)(2,1)S(1)}, u32[]{:S(2)}, u32[]{:S(2)}) collective-permute-start(bf16[256,512]{1,0:T(8,128)(2,1)S(1)} %copy-done.3), channel_id=1, source_target_pairs={{0,2},{2,4},{4,6},{6,8},{8,10},{10,12},{12,14},{14,16},{16,18},{18... | collective-permute-start | bytes 786440 | tf_op jit(solution)/shard_map/ppermute | solution.py:35
  43.0 26.2 %collective-permute-start.1 = (bf16[256,512]{1,0:T(8,128)(2,1)S(1)}, bf16[256,512]{1,0:T(8,128)(2,1)S(1)}, u32[]{:S(2)}, u32[]{:S(2)}) collective-permute-start(bf16[256,512]{1,0:T(8,128)(2,1)S(1)} %collective-permute-done.k1_ref), channel_id=1, source_target_pairs={{0,2},{2,4},{4,6},{6,8},{8,10},{10,12},{12,14},{14,16},{16,18},{18... | collective-permute-start | bytes 786440 | tf_op jit(solution)/shard_map/ppermute | solution.py:35
  47.6 21.6 %collective-permute-start.3 = (bf16[256,512]{1,0:T(8,128)(2,1)S(1)}, bf16[256,512]{1,0:T(8,128)(2,1)S(1)}, u32[]{:S(2)}, u32[]{:S(2)}) collective-permute-start(bf16[256,512]{1,0:T(8,128)(2,1)S(1)} %collective-permute-done.2.v1_ref), channel_id=1, source_target_pairs={{0,2},{2,4},{4,6},{6,8},{8,10},{10,12},{12,14},{14,16},{16,18},{18... | collective-permute-start | bytes 786440 | tf_op jit(solution)/shard_map/ppermute | solution.py:35
  55.9 18.8 %all-to-all-start.2 = ((bf16[4,64,512]{2,1,0:T(8,128)(2,1)}), bf16[4,64,512]{2,1,0:T(8,128)(2,1)S(1)}, u32[]{:S(2)}, u32[]{:S(2)}) async-start(bf16[4,64,512]{2,1,0:T(8,128)(2,1)} %shard_map.84), calls=%async_computation.2 | async-start | bytes 524288 | tf_op jit(solution)/shard_map/all_to_all | solution.py:277
  74.7 7.7 %copy-start.7 = (f32[2048]{0:T(1024)S(1)}, f32[2048]{0:T(1024)}, u32[]{:S(2)}) copy-start(f32[2048]{0:T(1024)} %param.15) | copy-start | bytes 24580
  81.0 1.4 %collective-permute-start.5 = (f32[256,128]{1,0:T(8,128)S(1)}, f32[256,128]{1,0:T(8,128)S(1)}, u32[]{:S(2)}, u32[]{:S(2)}) collective-permute-start(f32[256,128]{1,0:T(8,128)S(1)} %get-tuple-element.8.mine_ref), channel_id=1, source_target_pairs={{0,1},{1,0},{2,3},{3,2},{4,5},{5,4},{6,7},{7,6},{8,9},{9,8},{10,11... | collective-permute-start | bytes 393224 | tf_op jit(solution)/shard_map/ppermute | solution.py:279

commit v2 on v1

v2 whole, which is shorter than its diff:
```python
import functools
import math

import jax
import jax.numpy as jnp
from jax import lax
from jax.experimental import pallas as pl
from jax.experimental.pallas import tpu as pltpu
from jax.sharding import PartitionSpec as P

HEAD_SIZE = 128
POOL_FACTOR = 4
WINDOW_LENGTH = 512
CARRY_ROWS = 16
MASKED = -1e30
EXP2_SCALE = HEAD_SIZE ** (-0.5) * math.log2(math.e)
NT = (((1,), (1,)), ((), ()))
NN = (((1,), (0,)), ((), ()))
ANY = pl.BlockSpec(memory_space=pl.ANY)
VMEM = pl.BlockSpec(memory_space=pltpu.VMEM)
SMEM = pl.BlockSpec(memory_space=pltpu.SMEM)


def params(mib=40):
    return pltpu.CompilerParams(vmem_limit_bytes=mib * 1024 * 1024)


def cost(flops, nbytes, exps=0):
    return pl.CostEstimate(flops=int(flops), bytes_accessed=int(nbytes), transcendentals=int(exps))


def dot(a, b, dims):
    return lax.dot_general(a, b, dims, preferred_element_type=jnp.float32)


def head_columns(h, width=HEAD_SIZE):
    return pl.ds(pl.multiple_of(h * width, width), width)


def in_ring(value, axis):
    count = lax.axis_size(axis)
    return lax.ppermute(value, axis, [(source, (source + 1) % count) for source in range(count)])


def exchanged(value, axis, offset):
    count = lax.axis_size(axis)
    return lax.ppermute(value, axis, [(source, source ^ offset) for source in range(count)])


def gathered(value, axis):
    held = {0: value}
    bit = lax.axis_size(axis) // 2
    while bit:
        held.update({offset ^ bit: exchanged(array, axis, bit) for offset, array in list(held.items())})
        bit //= 2
    return [held[offset] for offset in range(len(held))]


def pool_kernel(my_ref, q_hbm, k_hbm, v_hbm, qw_hbm, kw_hbm, vw_hbm, *rest):
    heads = len(rest) - 5
    outs, (q_buf, kv_buf, qw_buf, kvw_buf, sems) = rest[:heads], rest[heads:]
    tokens = q_hbm.shape[0]
    width = q_hbm.shape[1] // heads
    pooled = tokens // POOL_FACTOR
    my = my_ref[0]
    left, right = pl.ds(0, HEAD_SIZE), pl.ds(HEAD_SIZE, HEAD_SIZE)
    copies = []
    for m in range(heads):
        h = my ^ m
        wide, narrow = head_columns(h, width), head_columns(h)
        pairs = [
            (k_hbm.at[:, narrow], kv_buf.at[m, :, left]),
            (v_hbm.at[:, narrow], kv_buf.at[m, :, right]),
            (kw_hbm.at[:, narrow], kvw_buf.at[m, :, left]),
            (vw_hbm.at[:, narrow], kvw_buf.at[m, :, right]),
            (q_hbm.at[:, wide], q_buf.at[m]),
            (qw_hbm.at[:, wide], qw_buf.at[m]),
        ]
        copies.append([pltpu.make_async_copy(a, b, sems.at[m, i]) for i, (a, b) in enumerate(pairs)])
    for group in copies:
        for copy in group:
            copy.start()
    row = lax.broadcasted_iota(jnp.int32, (tokens, tokens), 0)
    column = lax.broadcasted_iota(jnp.int32, (tokens, tokens), 1)
    wanted = POOL_FACTOR * (row % pooled) + row // pooled
    pick = jnp.where(column == wanted, 1.0, 0.0).astype(jnp.bfloat16)

    def weighted(rows, weights):
        picked = dot(pick, rows, NN)
        total = picked[:pooled] * weights[0:1]
        for i in range(1, POOL_FACTOR):
            total = total + picked[i * pooled : (i + 1) * pooled] * weights[i : i + 1]
        return total.astype(jnp.bfloat16)

    for m in range(heads):
        for copy in copies[m]:
            copy.wait()
        outs[m][:, :width] = weighted(q_buf[m], qw_buf[m])
        outs[m][:, width:] = weighted(kv_buf[m], kvw_buf[m])


def pool(my, queries, keys, values, qw, kw, vw):
    tokens, columns = queries.shape
    heads = keys.shape[1] // HEAD_SIZE
    width = columns // heads
    span = 2 * HEAD_SIZE
    payload = jax.ShapeDtypeStruct((tokens // POOL_FACTOR, width + span), jnp.bfloat16)
    return pl.pallas_call(
        pool_kernel,
        in_specs=[SMEM] + [ANY] * 6,
        out_specs=[VMEM] * heads,
        out_shape=[payload] * heads,
        scratch_shapes=[
            pltpu.VMEM((heads, tokens, width), jnp.bfloat16),
            pltpu.VMEM((heads, tokens, span), jnp.bfloat16),
            pltpu.VMEM((heads, POOL_FACTOR, width), jnp.float32),
            pltpu.VMEM((heads, POOL_FACTOR, span), jnp.float32),
            pltpu.SemaphoreType.DMA((heads, 6)),
        ],
        compiler_params=params(),
        cost_estimate=cost(3 * tokens * tokens * columns, 4 * tokens * columns),
    )(my, queries, keys, values, qw, kw, vw)


def stack_kernel(my_ref, *refs):
    payloads, out_ref = refs[:-1], refs[-1]
    sections = len(payloads)
    pooled, span = payloads[0].shape[0], out_ref.shape[1]
    width = payloads[0].shape[1] - span
    my = my_ref[0]
    parts = width // span
    row = lax.broadcasted_iota(jnp.int32, (CARRY_ROWS, span), 0)
    carry = jnp.zeros((CARRY_ROWS, span), jnp.float32)
    for m in range(sections):
        s = my ^ m
        out_ref[pl.ds(pl.multiple_of(s * pooled, pooled), pooled), :] = payloads[m][:, width:]
        last = payloads[m][pooled - 16 :, :width].astype(jnp.float32)[15:]
        for i in range(parts):
            carry = jnp.where(row == parts * s + i, last[:, i * span : (i + 1) * span], carry)
    out_ref[sections * pooled :, :] = carry.astype(jnp.bfloat16)


def stack(my, payloads):
    sections = len(payloads)
    pooled, columns = payloads[0].shape
    span = 2 * HEAD_SIZE
    return pl.pallas_call(
        stack_kernel,
        in_specs=[SMEM] + [VMEM] * sections,
        out_specs=VMEM,
        out_shape=jax.ShapeDtypeStruct((sections * pooled + CARRY_ROWS, span), jnp.bfloat16),
        compiler_params=params(),
        cost_estimate=cost(sections * pooled * span, 4 * sections * pooled * span),
    )(my, *payloads)


def with_ones(values):
    return jnp.concatenate([values, jnp.ones_like(values)], axis=1)


def coarse_kernel(sections, seq_count, place_ref, *refs):
    payloads, blocks = refs[:sections], refs[sections : sections + seq_count]
    outs = refs[sections + seq_count : -4]
    q_buf, kv_buf, carry_buf, out_buf = refs[-4:]
    pooled = payloads[0].shape[0]
    span = kv_buf.shape[2]
    width = payloads[0].shape[1] - span
    group = width // HEAD_SIZE
    rows = group * pooled
    parts = width // span
    my, z = place_ref[0], place_ref[1]
    for m in range(sections):
        q_buf[my ^ m] = payloads[m][:, :width]
    for m in range(seq_count):
        carry_buf[z ^ m] = blocks[m][sections * pooled :, :]
        for s in range(sections):
            at = pl.ds(pl.multiple_of((z ^ m) * pooled, pooled), pooled)
            kv_buf[s, at, :] = blocks[m][s * pooled : (s + 1) * pooled, :]
    before = carry_buf[jnp.where(z == 0, seq_count - 1, z - 1)].astype(jnp.float32)
    chunk = seq_count * pooled
    row = lax.broadcasted_iota(jnp.int32, (rows, chunk), 0) % pooled
    column = lax.broadcasted_iota(jnp.int32, (rows, chunk), 1)
    allowed = column < z * pooled + row
    first = lax.broadcasted_iota(jnp.int32, (rows, HEAD_SIZE), 0) % pooled == 0
    for s in range(sections):
        q = q_buf[s].astype(jnp.float32)
        shifted = jnp.concatenate([q[-1:], q[:-1]], axis=0)
        here = before[parts * s : parts * (s + 1)]
        if s > 0:
            here = jnp.where(z == 0, before[parts * (s - 1) : parts * s], here)
        pieces = []
        for g in range(group):
            at = g * HEAD_SIZE
            piece = here[at // span : at // span + 1, at % span : at % span + HEAD_SIZE]
            pieces.append(jnp.where(first[:pooled], piece, shifted[:, at : at + HEAD_SIZE]))
        stacked = jnp.concatenate(pieces, axis=0).astype(jnp.bfloat16)
        scores = [dot(stacked, kv_buf[c, :, :HEAD_SIZE], NT) for c in range(s + 1)]
        scores[s] = jnp.where(allowed, scores[s], MASKED)
        highest = functools.reduce(jnp.maximum, scores)
        highest = jnp.max(highest, axis=1, keepdims=True)
        total = None
        for c in range(s + 1):
            weights = jnp.exp2((scores[c] - highest) * EXP2_SCALE).astype(jnp.bfloat16)
            part = dot(weights, with_ones(kv_buf[c, :, HEAD_SIZE:]), NN)
            total = part if total is None else total + part
        result = total[:, :HEAD_SIZE] / total[:, HEAD_SIZE:]
        if s == 0:
            result = jnp.where(first & (z == 0), 0.0, result)
        result = result.astype(jnp.bfloat16)
        for g in range(group):
            out_buf[s, :, g * HEAD_SIZE : (g + 1) * HEAD_SIZE] = result[g * pooled : (g + 1) * pooled]
    for m in range(sections):
        outs[m][...] = out_buf[my ^ m]


def coarse_attention(place, payloads, blocks):
    sections, seq_count = len(payloads), len(blocks)
    pooled, columns = payloads[0].shape
    span = 2 * HEAD_SIZE
    width = columns - span
    pairs = sections * pooled * width // HEAD_SIZE * sections * seq_count * pooled
    return pl.pallas_call(
        functools.partial(coarse_kernel, sections, seq_count),
        in_specs=[SMEM] + [VMEM] * (sections + seq_count),
        out_specs=[VMEM] * sections,
        out_shape=[jax.ShapeDtypeStruct((pooled, width), jnp.bfloat16)] * sections,
        scratch_shapes=[
            pltpu.VMEM((sections, pooled, width), jnp.bfloat16),
            pltpu.VMEM((sections, seq_count * pooled, span), jnp.bfloat16),
            pltpu.VMEM((seq_count, CARRY_ROWS, span), jnp.bfloat16),
            pltpu.VMEM((sections, pooled, width), jnp.bfloat16),
        ],
        compiler_params=params(),
        cost_estimate=cost(4 * pairs * HEAD_SIZE, 4 * sections * seq_count * pooled * span, pairs),
    )(place, *payloads, *blocks)


def fine_kernel(pos_ref, q_hbm, k0_hbm, k1_hbm, k2_hbm, v0_hbm, v1_hbm, acc_ref, last_ref, q_buf, kv_buf, sems):
    heads, tokens, width = q_buf.shape
    group = width // HEAD_SIZE
    sources = (k0_hbm, k1_hbm, v0_hbm, v1_hbm, k2_hbm)

    def copies(h):
        narrow = head_columns(h)
        found = [
            pltpu.make_async_copy(ref.at[:, narrow], kv_buf.at[i, h], sems.at[i, h]) for i, ref in enumerate(sources)
        ]
        found.append(pltpu.make_async_copy(q_hbm.at[:, head_columns(h, width)], q_buf.at[h], sems.at[len(sources), h]))
        return found

    for h in range(heads):
        for copy in copies(h):
            copy.start()
    position = pos_ref[0]
    bias1 = jnp.where(position >= 1, 0.0, MASKED).astype(jnp.float32)
    bias2 = jnp.where(position >= 2, 0.0, MASKED).astype(jnp.float32)
    row = lax.broadcasted_iota(jnp.int32, (tokens, tokens), 0)
    column = lax.broadcasted_iota(jnp.int32, (tokens, tokens), 1)
    own = column <= row
    ones = jnp.ones((tokens, HEAD_SIZE), jnp.bfloat16)

    def one_head(h, carried):
        for copy in copies(h):
            copy.wait()
        k0, k1, v0, v1, k2 = [kv_buf[i, h] for i in range(len(sources))]
        v0, v1 = with_ones(v0), with_ones(v1)
        for g in range(group):
            q = q_buf[h, :, g * HEAD_SIZE : (g + 1) * HEAD_SIZE]
            outer = jnp.where(own, dot(q, k0, NT), dot(q, k2, NT) + bias2)
            inner = dot(q, k1, NT) + bias1
            highest = jnp.max(jnp.maximum(outer, inner), axis=1, keepdims=True)
            outer = jnp.exp2((outer - highest) * EXP2_SCALE)
            inner = jnp.exp2((inner - highest) * EXP2_SCALE).astype(jnp.bfloat16)
            first = jnp.where(own, outer, 0.0).astype(jnp.bfloat16)
            last = jnp.where(own, 0.0, outer)
            total = dot(first, v0, NN) + dot(inner, v1, NN)
            scale = 1.0 / (total[:, HEAD_SIZE:] + dot(last.astype(jnp.bfloat16), ones, NN))
            acc_ref[:, head_columns(h * group + g)] = total[:, :HEAD_SIZE] * scale
            scaled = last * jnp.concatenate([scale] * (tokens // HEAD_SIZE), axis=1)
            last_ref[:, head_columns(h * group + g, tokens)] = scaled.astype(jnp.bfloat16)
        return carried

    lax.fori_loop(0, heads, one_head, 0)


def fine_attention(position, queries, keys, values):
    tokens, columns = queries.shape
    heads = keys[0].shape[1] // HEAD_SIZE
    width = columns // heads
    pairs = tokens * tokens * 3 * columns // HEAD_SIZE
    return pl.pallas_call(
        fine_kernel,
        in_specs=[SMEM] + [ANY] * 6,
        out_specs=[VMEM, VMEM],
        out_shape=[
            jax.ShapeDtypeStruct((tokens, columns), jnp.float32),
            jax.ShapeDtypeStruct((tokens, columns // HEAD_SIZE * tokens), jnp.bfloat16),
        ],
        scratch_shapes=[
            pltpu.VMEM((heads, tokens, width), jnp.bfloat16),
            pltpu.VMEM((5, heads, tokens, HEAD_SIZE), jnp.bfloat16),
            pltpu.SemaphoreType.DMA((6, heads)),
        ],
        compiler_params=params(),
        cost_estimate=cost(4 * pairs * HEAD_SIZE, 12 * tokens * columns, pairs),
    )(position, queries, *keys, *values)


def join_kernel(my_ref, acc_ref, last_ref, v2_hbm, up_ref, *refs):
    sections = len(refs) - 5
    coarse, (comb_ref, sq_ref, v2_buf, coarse_buf, sem) = refs[:sections], refs[sections:]
    copy = pltpu.make_async_copy(v2_hbm, v2_buf, sem)
    copy.start()
    tokens, columns = acc_ref.shape
    heads = v2_buf.shape[1] // HEAD_SIZE
    width = columns // heads
    pooled = tokens // POOL_FACTOR
    my = my_ref[0]
    for m in range(sections):
        coarse_buf[my ^ m] = coarse[m][...]
    token = lax.broadcasted_iota(jnp.int32, (tokens, pooled), 0)
    spread = jnp.where(token // POOL_FACTOR == lax.broadcasted_iota(jnp.int32, (tokens, pooled), 1), 1.0, 0.0)
    spread = spread.astype(jnp.bfloat16)
    copy.wait()

    def one_head(h, squares):
        wide = head_columns(h, width)
        upsampled = dot(spread, coarse_buf[h], NN)
        up = up_ref[:, wide]
        up = jnp.concatenate([up, up], axis=0)
        upsampled = (upsampled.reshape(tokens // 8, 8, width) * up[None]).reshape(tokens, width)
        values = v2_buf[:, head_columns(h)]
        for g in range(width // HEAD_SIZE):
            at = h * (width // HEAD_SIZE) + g
            part = dot(last_ref[:, head_columns(at, tokens)], values, NN)
            here = slice(g * HEAD_SIZE, (g + 1) * HEAD_SIZE)
            combined = acc_ref[:, head_columns(at)] + part + upsampled[:, here]
            comb_ref[:, head_columns(at)] = combined
            squares = squares + combined * combined
        return squares

    squares = lax.fori_loop(0, heads, one_head, jnp.zeros((tokens, HEAD_SIZE), jnp.float32))
    sq_ref[...] = jnp.broadcast_to(jnp.sum(squares, axis=1, keepdims=True), sq_ref.shape)


def join(my, acc, last, values, up_weight, coarse):
    tokens, columns = acc.shape
    pooled, width = coarse[0].shape
    return pl.pallas_call(
        join_kernel,
        in_specs=[SMEM, VMEM, VMEM, ANY, VMEM] + [VMEM] * len(coarse),
        out_specs=[VMEM, VMEM],
        out_shape=[
            jax.ShapeDtypeStruct((tokens, columns), jnp.float32),
            jax.ShapeDtypeStruct((tokens, HEAD_SIZE), jnp.float32),
        ],
        scratch_shapes=[
            pltpu.VMEM(values.shape, jnp.bfloat16),
            pltpu.VMEM((len(coarse), pooled, width), jnp.bfloat16),
            pltpu.SemaphoreType.DMA,
        ],
        compiler_params=params(),
        cost_estimate=cost(2 * tokens * tokens * columns, 12 * tokens * columns),
    )(my, acc, last, values, up_weight, *coarse)


def norm_kernel(full, comb_ref, mine_ref, other_ref, gain_ref, out_hbm, buf, sems):
    parts, rows, columns = buf.shape
    copies = []
    for i in range(parts):
        here = pl.ds(i * rows, rows)
        mean = (mine_ref[here, :1] + other_ref[here, :1]) / full
        buf[i] = (comb_ref[here, :] * lax.rsqrt(mean + 1e-05) * gain_ref[...]).astype(jnp.bfloat16)
        copies.append(pltpu.make_async_copy(buf.at[i], out_hbm.at[here, :], sems.at[i]))
        copies[-1].start()
    for copy in copies:
        copy.wait()


def normalized(combined, mine, other, gain, full):
    tokens, columns = combined.shape
    parts = 4
    return pl.pallas_call(
        functools.partial(norm_kernel, full),
        in_specs=[VMEM] * 4,
        out_specs=ANY,
        out_shape=jax.ShapeDtypeStruct((tokens, columns), jnp.bfloat16),
        scratch_shapes=[
            pltpu.VMEM((parts, tokens // parts, columns), jnp.bfloat16),
            pltpu.SemaphoreType.DMA((parts,)),
        ],
        compiler_params=params(),
        cost_estimate=cost(3 * tokens * columns, 6 * tokens * columns),
    )(combined, mine, other, gain)


def per_device(queries, keys, values, qw, kw, vw, up_weight, out_gain):
    tokens, columns = queries.shape
    heads = keys.shape[1] // HEAD_SIZE
    seq_count = lax.axis_size("seq")
    section_count = lax.axis_size("section")
    head_count = lax.axis_size("head")
    if WINDOW_LENGTH != 2 * tokens or heads != section_count or head_count != 2:
        raise ValueError("unsupported sizes")
    line = ("section", "seq")
    section = lax.axis_index("section")
    z = lax.axis_index("seq")
    position = section * seq_count + z
    my = section[None]
    others = range(1, section_count)

    k1 = in_ring(keys, line)
    v1 = in_ring(values, line)
    payloads = pool(my, queries, keys, values, qw, kw, vw)
    payloads = [payloads[0]] + [exchanged(payloads[m], "section", m) for m in others]
    blocks = gathered(stack(my, payloads), "seq")
    k2 = in_ring(k1, line)
    v2 = in_ring(v1, line)
    coarse = coarse_attention(jnp.stack([section, z]), payloads, blocks)
    coarse = [coarse[0]] + [exchanged(coarse[m], "section", m) for m in others]
    acc, last = fine_attention(position[None], queries, (keys, k1, k2), (values, v1))
    combined, mine = join(my, acc, last, v2, up_weight, coarse)
    other = exchanged(mine, "head", 1)
    return normalized(combined, mine, other, out_gain[None], head_count * columns)


def solution(mesh):
    rows = P(("section", "seq"), "head")
    return jax.shard_map(
        per_device,
        mesh=mesh,
        in_specs=(rows, rows, rows, P(None, "head"), P(None, "head"), P(None, "head"), P(None, "head"), P("head")),
        out_specs=rows,
        check_vma=False,
    )
```

time: 85 us -> 64.7 us (0.76)
  starting transfers between devices: 46.4 us -> 17.4 us
  waiting for transfers between devices: 18.5 us -> 26.8 us
    all_to_all x3 -> x0, starting transfers between devices: 24.2 us -> none  [the longest x1 13.4 us: per_device(): lax.all_to_all(coarse, 'section', split_axis=0, concat_axis=0, tiled=True)]
    ppermute x6 -> x14, waiting for transfers between devices: 11.2 us -> 26.8 us  [the longest x10 26.8 us: exchanged(): lax.ppermute(value, axis, [(source, source ^ offset) for source in range(...]
    all_to_all x3 -> x0, waiting for transfers between devices: 7.32 us -> none  [the longest x1 5.36 us: per_device(): lax.all_to_all(coarse, 'section', split_axis=0, concat_axis=0, tiled=True)]
    ppermute x6 -> x14, starting transfers between devices: 22.3 us -> 17.4 us  [the longest x10 10.1 us: exchanged(): lax.ppermute(value, axis, [(source, source ^ offset) for source in range(...]
    unnamed x18, local copies, waits for them, and re-layouts: 3.39 us -> 4.34 us
    pallas_call x5 -> x6, Pallas kernels: 15 us -> 15.6 us  [the longest x1 8 us: fine_attention(): pl.pallas_call(fine_kernel, in_specs=[SMEM] + [ANY] * 6, out_specs=[VMEM,...]
  transfers between devices with their start and end apart: 9 -> 14, of which waited for: 5 -> 6; matrix products, arithmetic and copies ran while one was open for 0% -> 0% of each run, Pallas kernels for 5% -> 20%
where the time goes in v2:
time: 64.7 us; the launch traced here: 64.3 us
  waiting for transfers between devices  26.8 us (41%)
  starting transfers between devices  17.4 us (27%)
  Pallas kernels  15.6 us (24%)
  local copies, waits for them, and re-layouts  4.34 us (7%)
    ppermute x10, waiting for transfers between devices, exchanged(): lax.ppermute(value, axis, [(source, source ^ offset) for source in range(...  26.8 us
    ppermute x10, starting transfers between devices, exchanged(): lax.ppermute(value, axis, [(source, source ^ offset) for source in range(...  10.1 us
    pallas_call x1, Pallas kernels, fine_attention(): pl.pallas_call(fine_kernel, in_specs=[SMEM] + [ANY] * 6, out_specs=[VMEM,...  8 us
    ppermute x4, starting transfers between devices, in_ring(): lax.ppermute(value, axis, [(source, (source + 1) % count) for source in r...  7.26 us
    unnamed x18, local copies, waits for them, and re-layouts  4.34 us
    pallas_call x1, Pallas kernels, pool(): pl.pallas_call(pool_kernel, in_specs=[SMEM] + [ANY] * 6, out_specs=[VMEM]...  2.41 us
    pallas_call x1, Pallas kernels, coarse_attention(): pl.pallas_call(functools.partial(coarse_kernel, sections, seq_count), in_...  2.39 us
    pallas_call x1, Pallas kernels, join(): pl.pallas_call(join_kernel, in_specs=[SMEM, VMEM, VMEM, ANY, VMEM] + [VME...  1.68 us
  transfers between devices with their start and end apart: 14, of which 6 were waited for; matrix products, arithmetic and copies ran while one was open for 0% of the time, Pallas kernels for 20%

profile of v2, /device:TPU:0, one launch (start us, length us, event | category | flops | bytes accessed | tf_op | source)
XLA Modules:
  0.0 64.3 jit_solution(13449394024345688505)
XLA Ops:
  0.0 3.0 %collective-permute-start = (bf16[256,512]{1,0:T(8,128)(2,1)}, bf16[256,512]{1,0:T(8,128)(2,1)S(1)}, u32[]{:S(2)}, u32[]{:S(2)}) collective-permute-start(bf16[256,512]{1,0:T(8,128)(2,1)} %k_hbm.1), channel_id=1, source_target_pairs={{0,2},{2,4},{4,6},{6,8},{8,10},{10,12},{12,14},{14,16},{16,18},{18... | collective-permute-start | bytes 786440 | tf_op jit(solution)/shard_map/ppermute | solution.py:42
  3.0 1.2 %copy-done = bf16[256,2048]{1,0:T(8,128)(2,1)S(1)} copy-done((bf16[256,2048]{1,0:T(8,128)(2,1)S(1)}, bf16[256,2048]{1,0:T(8,128)(2,1)}, u32[]{:S(2)}) %copy-start) | copy-done | bytes 1048600
  4.3 0.9 %copy-done.2 = bf16[256,512]{1,0:T(8,128)(2,1)S(1)} copy-done((bf16[256,512]{1,0:T(8,128)(2,1)S(1)}, bf16[256,512]{1,0:T(8,128)(2,1)}, u32[]{:S(2)}) %copy-start.2) | copy-done | bytes 262168
  5.2 0.8 %copy-done.5 = f32[4,2048]{1,0:T(4,128)S(1)} copy-done((f32[4,2048]{1,0:T(4,128)S(1)}, f32[4,2048]{1,0:T(4,128)}, u32[]{:S(2)}) %copy-start.5) | copy-done | bytes 32792
  6.0 0.7 %copy-done.6 = f32[4,512]{1,0:T(4,128)S(1)} copy-done((f32[4,512]{1,0:T(4,128)S(1)}, f32[4,512]{1,0:T(4,128)}, u32[]{:S(2)}) %copy-start.6) | copy-done | bytes 8216
  6.7 0.7 %copy-done.7 = f32[4,512]{1,0:T(4,128)S(1)} copy-done((f32[4,512]{1,0:T(4,128)S(1)}, f32[4,512]{1,0:T(4,128)}, u32[]{:S(2)}) %copy-start.7) | copy-done | bytes 8216
  7.4 2.4 %shard_map.83 = (bf16[64,768]{1,0:T(8,128)(2,1)S(1)}, bf16[64,768]{1,0:T(8,128)(2,1)S(1)}, bf16[64,768]{1,0:T(8,128)(2,1)S(1)}, bf16[64,768]{1,0:T(8,128)(2,1)S(1)}) custom-call(s32[1]{0:T(128)} %bitcast.my_ref, bf16[256,2048]{1,0:T(8,128)(2,1)S(1)} %copy-done, bf16[256,512]{1,0:T(8,128)(2,1)S(1)} %copy-done.2, bf16[256,512]{1,0:T(8,128)(2,1)} %v_hbm.1, ...), custom_call_target="tpu_custom_call" | custom-call | flops 402653184 | bytes 2097152 | tf_op jit(solution)/shard_map/pallas_call | solution.py:108
  9.8 1.6 %collective-permute-start.4 = (bf16[64,768]{1,0:T(8,128)(2,1)S(1)}, bf16[64,768]{1,0:T(8,128)(2,1)S(1)}, u32[]{:S(2)}, u32[]{:S(2)}) collective-permute-start(bf16[64,768]{1,0:T(8,128)(2,1)S(1)} %get-tuple-element.20), channel_id=1, source_target_pairs={{0,8},{8,0},{16,24},{24,16},{1,9},{9,1},{17,25},{25,17},{2,10},{10... | collective-permute-start | bytes 294920 | tf_op jit(solution)/shard_map/ppermute | solution.py:47
  11.3 1.5 %collective-permute-start.5 = (bf16[64,768]{1,0:T(8,128)(2,1)S(1)}, bf16[64,768]{1,0:T(8,128)(2,1)S(1)}, u32[]{:S(2)}, u32[]{:S(2)}) collective-permute-start(bf16[64,768]{1,0:T(8,128)(2,1)S(1)} %get-tuple-element.21), channel_id=1, source_target_pairs={{0,16},{8,24},{16,0},{24,8},{1,17},{9,25},{17,1},{25,9},{2,18},{10... | collective-permute-start | bytes 294920 | tf_op jit(solution)/shard_map/ppermute | solution.py:47
  12.9 0.5 collective-permute-start.6
  13.3 1.6 %collective-permute-start.2 = (bf16[256,512]{1,0:T(8,128)(2,1)}, bf16[256,512]{1,0:T(8,128)(2,1)S(1)}, u32[]{:S(2)}, u32[]{:S(2)}) collective-permute-start(bf16[256,512]{1,0:T(8,128)(2,1)} %v_hbm.1), channel_id=1, source_target_pairs={{0,2},{2,4},{4,6},{6,8},{8,10},{10,12},{12,14},{14,16},{16,18},{18... | collective-permute-start | bytes 786440 | tf_op jit(solution)/shard_map/ppermute | solution.py:42
  14.9 0.6 %collective-permute-done.4.refs_1_ = bf16[64,768]{1,0:T(8,128)(2,1)S(1)} collective-permute-done((bf16[64,768]{1,0:T(8,128)(2,1)S(1)}, bf16[64,768]{1,0:T(8,128)(2,1)S(1)}, u32[]{:S(2)}, u32[]{:S(2)}) %collective-permute-start.4) | collective-permute-done | bytes 98336 | tf_op jit(solution)/shard_map/ppermute | solution.py:47
  15.6 1.6 %collective-permute-done.5.refs_2_ = bf16[64,768]{1,0:T(8,128)(2,1)S(1)} collective-permute-done((bf16[64,768]{1,0:T(8,128)(2,1)S(1)}, bf16[64,768]{1,0:T(8,128)(2,1)S(1)}, u32[]{:S(2)}, u32[]{:S(2)}) %collective-permute-start.5) | collective-permute-done | bytes 98336 | tf_op jit(solution)/shard_map/ppermute | solution.py:47
  17.1 1.2 %collective-permute-done.6.refs_3_ = bf16[64,768]{1,0:T(8,128)(2,1)S(1)} collective-permute-done((bf16[64,768]{1,0:T(8,128)(2,1)S(1)}, bf16[64,768]{1,0:T(8,128)(2,1)S(1)}, u32[]{:S(2)}, u32[]{:S(2)}) %collective-permute-start.6) | collective-permute-done | bytes 98336 | tf_op jit(solution)/shard_map/ppermute | solution.py:47
  18.4 2.6 %collective-permute-start.8 = (bf16[272,256]{1,0:T(8,128)(2,1)S(1)}, bf16[272,256]{1,0:T(8,128)(2,1)S(1)}, u32[]{:S(2)}, u32[]{:S(2)}) collective-permute-start(bf16[272,256]{1,0:T(8,128)(2,1)S(1)} %shard_map.84.refs_4_), channel_id=1, source_target_pairs={{0,4},{2,6},{4,0},{6,2},{1,5},{3,7},{5,1},{7,3},{8,12},{10,14},{12... | collective-permute-start | bytes 417800 | tf_op jit(solution)/shard_map/ppermute | solution.py:47
  21.0 0.6 collective-permute-start.1
  21.7 0.3 collective-permute-start.7
  21.9 12.9 %collective-permute-done.8.refs_6_ = bf16[272,256]{1,0:T(8,128)(2,1)S(1)} collective-permute-done((bf16[272,256]{1,0:T(8,128)(2,1)S(1)}, bf16[272,256]{1,0:T(8,128)(2,1)S(1)}, u32[]{:S(2)}, u32[]{:S(2)}) %collective-permute-start.8) | collective-permute-done | bytes 139296 | tf_op jit(solution)/shard_map/ppermute | solution.py:47
  34.9 2.0 %collective-permute-start.3 = (bf16[256,512]{1,0:T(8,128)(2,1)S(1)}, bf16[256,512]{1,0:T(8,128)(2,1)S(1)}, u32[]{:S(2)}, u32[]{:S(2)}) collective-permute-start(bf16[256,512]{1,0:T(8,128)(2,1)S(1)} %collective-permute-done.2.v1_hbm), channel_id=1, source_target_pairs={{0,2},{2,4},{4,6},{6,8},{8,10},{10,12},{12,14},{14,16},{16,18},{18... | collective-permute-start | bytes 786440 | tf_op jit(solution)/shard_map/ppermute | solution.py:42
  36.9 0.1 pad_add_fusion.place_ref
  37.0 9.0 %collective-permute-done.9.refs_7_ = bf16[272,256]{1,0:T(8,128)(2,1)S(1)} collective-permute-done((bf16[272,256]{1,0:T(8,128)(2,1)S(1)}, bf16[272,256]{1,0:T(8,128)(2,1)S(1)}, u32[]{:S(2)}, u32[]{:S(2)}) %collective-permute-start.9) | collective-permute-done | bytes 139296 | tf_op jit(solution)/shard_map/ppermute | solution.py:47
  46.0 2.4 %shard_map.85 = (bf16[64,512]{1,0:T(8,128)(2,1)S(1)}, bf16[64,512]{1,0:T(8,128)(2,1)S(1)}, bf16[64,512]{1,0:T(8,128)(2,1)S(1)}, bf16[64,512]{1,0:T(8,128)(2,1)S(1)}) custom-call(s32[2]{0:T(128)S(1)} %pad_add_fusion.place_ref, bf16[64,768]{1,0:T(8,128)(2,1)S(1)} %get-tuple-element.19.refs_0_, bf16[64,768]{1,0:T(8,128)(2,1)S(1)} %collective-permute-done.4.refs_1_, ...), custom_call_target="tpu_custom_call" | custom-call | flops 536870912 | bytes 1048576 | tf_op jit(solution)/shard_map/pallas_call | solution.py:222
  48.4 1.5 %collective-permute-start.10 = (bf16[64,512]{1,0:T(8,128)(2,1)S(1)}, bf16[64,512]{1,0:T(8,128)(2,1)S(1)}, u32[]{:S(2)}, u32[]{:S(2)}) collective-permute-start(bf16[64,512]{1,0:T(8,128)(2,1)S(1)} %get-tuple-element.24), channel_id=1, source_target_pairs={{0,8},{8,0},{16,24},{24,16},{1,9},{9,1},{17,25},{25,17},{2,10},{10... | collective-permute-start | bytes 196616 | tf_op jit(solution)/shard_map/ppermute | solution.py:47
  50.0 0.5 collective-permute-start.11
  50.5 1.5 %collective-permute-start.12 = (bf16[64,512]{1,0:T(8,128)(2,1)S(1)}, bf16[64,512]{1,0:T(8,128)(2,1)S(1)}, u32[]{:S(2)}, u32[]{:S(2)}) collective-permute-start(bf16[64,512]{1,0:T(8,128)(2,1)S(1)} %get-tuple-element.26), channel_id=1, source_target_pairs={{0,24},{8,16},{16,8},{24,0},{1,25},{9,17},{17,9},{25,1},{2,26},{10... | collective-permute-start | bytes 196616 | tf_op jit(solution)/shard_map/ppermute | solution.py:47
  52.0 0.0 copy-start.4
  52.0 8.0 %shard_map.82 = (f32[256,2048]{1,0:T(8,128)S(1)}, bf16[256,4096]{1,0:T(8,128)(2,1)S(1)}) custom-call(s32[1]{0:T(128)} %bitcast.1.pos_ref, bf16[256,2048]{1,0:T(8,128)(2,1)S(1)} %copy-done.1, bf16[256,512]{1,0:T(8,128)(2,1)S(1)} %copy-done.3, bf16[256,512]{1,0:T(8,128)(2,1)S(1)} %collective-permute-done.k1_hbm, ...), custom_call_target="tpu_custom_call" | custom-call | flops 1610612736 | bytes 6291456 | tf_op jit(solution)/shard_map/pallas_call | solution.py:291
  60.1 0.0 copy-start.8
  60.1 1.7 %shard_map.86 = (f32[256,2048]{1,0:T(8,128)S(1)}, f32[256,128]{1,0:T(8,128)S(1)}) custom-call(s32[1]{0:T(128)} %bitcast.my_ref, f32[256,2048]{1,0:T(8,128)S(1)} %get-tuple-element.17.acc_ref, bf16[256,4096]{1,0:T(8,128)(2,1)S(1)} %get-tuple-element.18.last_ref, bf16[256,512]{1,0:T(8,128)(2,1)S(1)} %collective-permute-done.3.v2_hbm, f32[4,2048]{1,0:T(4,128)S(1)} %copy-done.4, ...), custom_call_target="tpu_custom_call" | custom-call | flops 268435456 | bytes 6291456 | tf_op jit(solution)/shard_map/pallas_call | solution.py:349
  61.8 0.1 collective-permute-start.13
  61.9 1.3 %collective-permute-done.13.other_ref = f32[256,128]{1,0:T(8,128)S(1)} collective-permute-done((f32[256,128]{1,0:T(8,128)S(1)}, f32[256,128]{1,0:T(8,128)S(1)}, u32[]{:S(2)}, u32[]{:S(2)}) %collective-permute-start.13) | collective-permute-done | bytes 131104 | tf_op jit(solution)/shard_map/ppermute | solution.py:47
  63.2 1.1 %shard_map.87 = bf16[256,2048]{1,0:T(8,128)(2,1)} custom-call(f32[256,2048]{1,0:T(8,128)S(1)} %get-tuple-element.27.comb_ref, f32[256,128]{1,0:T(8,128)S(1)} %get-tuple-element.28.mine_ref, f32[256,128]{1,0:T(8,128)S(1)} %collective-permute-done.13.other_ref, f32[1,2048]{1,0:T(1,128)S(1)} %bitcast.4), custom_call_target="tpu_custom_call" | custom-call | flops 1572864 | bytes 3145728 | tf_op jit(solution)/shard_map/pallas_call | solution.py:383
  (21 shorter events, 0.1 us)
Async XLA Ops:
  0.0 21.0 %collective-permute-start = (bf16[256,512]{1,0:T(8,128)(2,1)}, bf16[256,512]{1,0:T(8,128)(2,1)S(1)}, u32[]{:S(2)}, u32[]{:S(2)}) collective-permute-start(bf16[256,512]{1,0:T(8,128)(2,1)} %k_hbm.1), channel_id=1, source_target_pairs={{0,2},{2,4},{4,6},{6,8},{8,10},{10,12},{12,14},{14,16},{16,18},{18... | collective-permute-start | bytes 786440 | tf_op jit(solution)/shard_map/ppermute | solution.py:42
  3.0 1.2 %copy-start = (bf16[256,2048]{1,0:T(8,128)(2,1)S(1)}, bf16[256,2048]{1,0:T(8,128)(2,1)}, u32[]{:S(2)}) copy-start(bf16[256,2048]{1,0:T(8,128)(2,1)} %q_hbm.3) | copy-start | bytes 3145732
  4.2 0.9 %copy-start.2 = (bf16[256,512]{1,0:T(8,128)(2,1)S(1)}, bf16[256,512]{1,0:T(8,128)(2,1)}, u32[]{:S(2)}) copy-start(bf16[256,512]{1,0:T(8,128)(2,1)} %k_hbm.1) | copy-start | bytes 786436
  5.2 0.8 %copy-start.5 = (f32[4,2048]{1,0:T(4,128)S(1)}, f32[4,2048]{1,0:T(4,128)}, u32[]{:S(2)}) copy-start(f32[4,2048]{1,0:T(4,128)} %qw_hbm.1) | copy-start | bytes 98308
  6.0 0.7 %copy-start.6 = (f32[4,512]{1,0:T(4,128)S(1)}, f32[4,512]{1,0:T(4,128)}, u32[]{:S(2)}) copy-start(f32[4,512]{1,0:T(4,128)} %kw_hbm.1) | copy-start | bytes 24580
  6.7 0.7 %copy-start.7 = (f32[4,512]{1,0:T(4,128)S(1)}, f32[4,512]{1,0:T(4,128)}, u32[]{:S(2)}) copy-start(f32[4,512]{1,0:T(4,128)} %vw_hbm.1) | copy-start | bytes 24580
  7.4 44.6 %copy-start.1 = (bf16[256,2048]{1,0:T(8,128)(2,1)S(1)}, bf16[256,2048]{1,0:T(8,128)(2,1)}, u32[]{:S(2)}) copy-start(bf16[256,2048]{1,0:T(8,128)(2,1)} %q_hbm.3) | copy-start | bytes 3145732
  7.4 44.6 %copy-start.3 = (bf16[256,512]{1,0:T(8,128)(2,1)S(1)}, bf16[256,512]{1,0:T(8,128)(2,1)}, u32[]{:S(2)}) copy-start(bf16[256,512]{1,0:T(8,128)(2,1)} %k_hbm.1) | copy-start | bytes 786436
  9.8 5.8 %collective-permute-start.4 = (bf16[64,768]{1,0:T(8,128)(2,1)S(1)}, bf16[64,768]{1,0:T(8,128)(2,1)S(1)}, u32[]{:S(2)}, u32[]{:S(2)}) collective-permute-start(bf16[64,768]{1,0:T(8,128)(2,1)S(1)} %get-tuple-element.20), channel_id=1, source_target_pairs={{0,8},{8,0},{16,24},{24,16},{1,9},{9,1},{17,25},{25,17},{2,10},{10... | collective-permute-start | bytes 294920 | tf_op jit(solution)/shard_map/ppermute | solution.py:47
  11.3 5.8 %collective-permute-start.5 = (bf16[64,768]{1,0:T(8,128)(2,1)S(1)}, bf16[64,768]{1,0:T(8,128)(2,1)S(1)}, u32[]{:S(2)}, u32[]{:S(2)}) collective-permute-start(bf16[64,768]{1,0:T(8,128)(2,1)S(1)} %get-tuple-element.21), channel_id=1, source_target_pairs={{0,16},{8,24},{16,0},{24,8},{1,17},{9,25},{17,1},{25,9},{2,18},{10... | collective-permute-start | bytes 294920 | tf_op jit(solution)/shard_map/ppermute | solution.py:47
  12.9 5.5 %collective-permute-start.6 = (bf16[64,768]{1,0:T(8,128)(2,1)S(1)}, bf16[64,768]{1,0:T(8,128)(2,1)S(1)}, u32[]{:S(2)}, u32[]{:S(2)}) collective-permute-start(bf16[64,768]{1,0:T(8,128)(2,1)S(1)} %get-tuple-element.22), channel_id=1, source_target_pairs={{0,24},{8,16},{16,8},{24,0},{1,25},{9,17},{17,9},{25,1},{2,26},{10... | collective-permute-start | bytes 294920 | tf_op jit(solution)/shard_map/ppermute | solution.py:47
  13.3 21.6 %collective-permute-start.2 = (bf16[256,512]{1,0:T(8,128)(2,1)}, bf16[256,512]{1,0:T(8,128)(2,1)S(1)}, u32[]{:S(2)}, u32[]{:S(2)}) collective-permute-start(bf16[256,512]{1,0:T(8,128)(2,1)} %v_hbm.1), channel_id=1, source_target_pairs={{0,2},{2,4},{4,6},{6,8},{8,10},{10,12},{12,14},{14,16},{16,18},{18... | collective-permute-start | bytes 786440 | tf_op jit(solution)/shard_map/ppermute | solution.py:42
  18.4 16.5 %collective-permute-start.8 = (bf16[272,256]{1,0:T(8,128)(2,1)S(1)}, bf16[272,256]{1,0:T(8,128)(2,1)S(1)}, u32[]{:S(2)}, u32[]{:S(2)}) collective-permute-start(bf16[272,256]{1,0:T(8,128)(2,1)S(1)} %shard_map.84.refs_4_), channel_id=1, source_target_pairs={{0,4},{2,6},{4,0},{6,2},{1,5},{3,7},{5,1},{7,3},{8,12},{10,14},{12... | collective-permute-start | bytes 417800 | tf_op jit(solution)/shard_map/ppermute | solution.py:47
  21.0 31.0 %collective-permute-start.1 = (bf16[256,512]{1,0:T(8,128)(2,1)S(1)}, bf16[256,512]{1,0:T(8,128)(2,1)S(1)}, u32[]{:S(2)}, u32[]{:S(2)}) collective-permute-start(bf16[256,512]{1,0:T(8,128)(2,1)S(1)} %collective-permute-done.k1_hbm), channel_id=1, source_target_pairs={{0,2},{2,4},{4,6},{6,8},{8,10},{10,12},{12,14},{14,16},{16,18},{18... | collective-permute-start | bytes 786440 | tf_op jit(solution)/shard_map/ppermute | solution.py:42
  21.7 15.3 %collective-permute-start.7 = (bf16[272,256]{1,0:T(8,128)(2,1)S(1)}, bf16[272,256]{1,0:T(8,128)(2,1)S(1)}, u32[]{:S(2)}, u32[]{:S(2)}) collective-permute-start(bf16[272,256]{1,0:T(8,128)(2,1)S(1)} %shard_map.84.refs_4_), channel_id=1, source_target_pairs={{0,2},{2,0},{4,6},{6,4},{1,3},{3,1},{5,7},{7,5},{8,10},{10,8},{12,... | collective-permute-start | bytes 417800 | tf_op jit(solution)/shard_map/ppermute | solution.py:47
  34.9 11.2 %collective-permute-start.9 = (bf16[272,256]{1,0:T(8,128)(2,1)S(1)}, bf16[272,256]{1,0:T(8,128)(2,1)S(1)}, u32[]{:S(2)}, u32[]{:S(2)}) collective-permute-start(bf16[272,256]{1,0:T(8,128)(2,1)S(1)} %collective-permute-done.8.refs_6_), channel_id=1, source_target_pairs={{0,2},{2,0},{4,6},{6,4},{1,3},{3,1},{5,7},{7,5},{8,10},{10,8},{12,... | collective-permute-start | bytes 417800 | tf_op jit(solution)/shard_map/ppermute | solution.py:47
  34.9 25.2 %collective-permute-start.3 = (bf16[256,512]{1,0:T(8,128)(2,1)S(1)}, bf16[256,512]{1,0:T(8,128)(2,1)S(1)}, u32[]{:S(2)}, u32[]{:S(2)}) collective-permute-start(bf16[256,512]{1,0:T(8,128)(2,1)S(1)} %collective-permute-done.2.v1_hbm), channel_id=1, source_target_pairs={{0,2},{2,4},{4,6},{6,8},{8,10},{10,12},{12,14},{14,16},{16,18},{18... | collective-permute-start | bytes 786440 | tf_op jit(solution)/shard_map/ppermute | solution.py:42
  48.4 11.6 %collective-permute-start.10 = (bf16[64,512]{1,0:T(8,128)(2,1)S(1)}, bf16[64,512]{1,0:T(8,128)(2,1)S(1)}, u32[]{:S(2)}, u32[]{:S(2)}) collective-permute-start(bf16[64,512]{1,0:T(8,128)(2,1)S(1)} %get-tuple-element.24), channel_id=1, source_target_pairs={{0,8},{8,0},{16,24},{24,16},{1,9},{9,1},{17,25},{25,17},{2,10},{10... | collective-permute-start | bytes 196616 | tf_op jit(solution)/shard_map/ppermute | solution.py:47
  50.0 10.1 %collective-permute-start.11 = (bf16[64,512]{1,0:T(8,128)(2,1)S(1)}, bf16[64,512]{1,0:T(8,128)(2,1)S(1)}, u32[]{:S(2)}, u32[]{:S(2)}) collective-permute-start(bf16[64,512]{1,0:T(8,128)(2,1)S(1)} %get-tuple-element.25), channel_id=1, source_target_pairs={{0,16},{8,24},{16,0},{24,8},{1,17},{9,25},{17,1},{25,9},{2,18},{10... | collective-permute-start | bytes 196616 | tf_op jit(solution)/shard_map/ppermute | solution.py:47
  50.5 9.6 %collective-permute-start.12 = (bf16[64,512]{1,0:T(8,128)(2,1)S(1)}, bf16[64,512]{1,0:T(8,128)(2,1)S(1)}, u32[]{:S(2)}, u32[]{:S(2)}) collective-permute-start(bf16[64,512]{1,0:T(8,128)(2,1)S(1)} %get-tuple-element.26), channel_id=1, source_target_pairs={{0,24},{8,16},{16,8},{24,0},{1,25},{9,17},{17,9},{25,1},{2,26},{10... | collective-permute-start | bytes 196616 | tf_op jit(solution)/shard_map/ppermute | solution.py:47
  52.0 8.1 %copy-start.4 = (f32[4,2048]{1,0:T(4,128)S(1)}, f32[4,2048]{1,0:T(4,128)}, u32[]{:S(2)}) copy-start(f32[4,2048]{1,0:T(4,128)} %up_ref.1) | copy-start | bytes 98308
  60.1 3.1 %copy-start.8 = (f32[2048]{0:T(1024)S(1)}, f32[2048]{0:T(1024)}, u32[]{:S(2)}) copy-start(f32[2048]{0:T(1024)} %param.15) | copy-start | bytes 24580
  61.8 1.4 %collective-permute-start.13 = (f32[256,128]{1,0:T(8,128)S(1)}, f32[256,128]{1,0:T(8,128)S(1)}, u32[]{:S(2)}, u32[]{:S(2)}) collective-permute-start(f32[256,128]{1,0:T(8,128)S(1)} %get-tuple-element.28.mine_ref), channel_id=1, source_target_pairs={{0,1},{1,0},{2,3},{3,2},{4,5},{5,4},{6,7},{7,6},{8,9},{9,8},{10,11... | collective-permute-start | bytes 393224 | tf_op jit(solution)/shard_map/ppermute | solution.py:47

commit v3 on v2

--- a/solution.py
+++ b/solution.py
@@ -33,27 +33,24 @@
     return lax.dot_general(a, b, dims, preferred_element_type=jnp.float32)
 
 
+def in_hbm(*arrays):
+    return [pltpu.with_memory_space_constraint(array, pltpu.HBM) for array in arrays]
+
+
 def head_columns(h, width=HEAD_SIZE):
     return pl.ds(pl.multiple_of(h * width, width), width)
 
 
-def in_ring(value, axis):
+def in_ring(value, axis, name):
     count = lax.axis_size(axis)
-    return lax.ppermute(value, axis, [(source, (source + 1) % count) for source in range(count)])
-
-
-def exchanged(value, axis, offset):
+    with jax.named_scope(name):
+        return lax.ppermute(value, axis, [(source, (source + 1) % count) for source in range(count)])
+
+
+def exchanged(value, axis, offset, name):
     count = lax.axis_size(axis)
-    return lax.ppermute(value, axis, [(source, source ^ offset) for source in range(count)])
-
-
-def gathered(value, axis):
-    held = {0: value}
-    bit = lax.axis_size(axis) // 2
-    while bit:
-        held.update({offset ^ bit: exchanged(array, axis, bit) for offset, array in list(held.items())})
-        bit //= 2
-    return [held[offset] for offset in range(len(held))]
+    with jax.named_scope(f"{name}{offset}"):
+        return lax.ppermute(value, axis, [(source, source ^ offset) for source in range(count)])
 
 
 def pool_kernel(my_ref, q_hbm, k_hbm, v_hbm, qw_hbm, kw_hbm, vw_hbm, *rest):
@@ -118,8 +115,8 @@
             pltpu.SemaphoreType.DMA((heads, 6)),
         ],
         compiler_params=params(),
-        cost_estimate=cost(3 * tokens * tokens * columns, 4 * tokens * columns),
-    )(my, queries, keys, values, qw, kw, vw)
+        cost_estimate=cost(1000, 1000),
+    )(my, *in_hbm(queries, keys, values, qw, kw, vw))
 
 
 def stack_kernel(my_ref, *refs):
@@ -150,7 +147,7 @@
         out_specs=VMEM,
         out_shape=jax.ShapeDtypeStruct((sections * pooled + CARRY_ROWS, span), jnp.bfloat16),
         compiler_params=params(),
-        cost_estimate=cost(sections * pooled * span, 4 * sections * pooled * span),
+        cost_estimate=cost(1000, 1000),
     )(my, *payloads)
 
 
@@ -235,10 +232,10 @@
     )(place, *payloads, *blocks)
 
 
-def fine_kernel(pos_ref, q_hbm, k0_hbm, k1_hbm, k2_hbm, v0_hbm, v1_hbm, acc_ref, last_ref, q_buf, kv_buf, sems):
+def near_kernel(pos_ref, q_hbm, k0_hbm, k1_hbm, v0_hbm, v1_hbm, acc_ref, sum_ref, max_ref, q_buf, kv_buf, sems):
     heads, tokens, width = q_buf.shape
     group = width // HEAD_SIZE
-    sources = (k0_hbm, k1_hbm, v0_hbm, v1_hbm, k2_hbm)
+    sources = (k0_hbm, k1_hbm, v0_hbm, v1_hbm)
 
     def copies(h):
         narrow = head_columns(h)
@@ -251,66 +248,128 @@
     for h in range(heads):
         for copy in copies(h):
             copy.start()
-    position = pos_ref[0]
-    bias1 = jnp.where(position >= 1, 0.0, MASKED).astype(jnp.float32)
-    bias2 = jnp.where(position >= 2, 0.0, MASKED).astype(jnp.float32)
+    bias = jnp.where(pos_ref[0] >= 1, 0.0, MASKED).astype(jnp.float32)
     row = lax.broadcasted_iota(jnp.int32, (tokens, tokens), 0)
     column = lax.broadcasted_iota(jnp.int32, (tokens, tokens), 1)
-    own = column <= row
-    ones = jnp.ones((tokens, HEAD_SIZE), jnp.bfloat16)
+    own = jnp.concatenate([column <= row] * group, axis=0)
 
     def one_head(h, carried):
         for copy in copies(h):
             copy.wait()
-        k0, k1, v0, v1, k2 = [kv_buf[i, h] for i in range(len(sources))]
-        v0, v1 = with_ones(v0), with_ones(v1)
+        k0, k1, v0, v1 = [kv_buf[i, h] for i in range(len(sources))]
+        q = jnp.concatenate([q_buf[h, :, g * HEAD_SIZE : (g + 1) * HEAD_SIZE] for g in range(group)], axis=0)
+        outer = jnp.where(own, dot(q, k0, NT), MASKED)
+        inner = dot(q, k1, NT) + bias
+        highest = jnp.max(jnp.maximum(outer, inner), axis=1, keepdims=True)
+        outer = jnp.exp2((outer - highest) * EXP2_SCALE).astype(jnp.bfloat16)
+        inner = jnp.exp2((inner - highest) * EXP2_SCALE).astype(jnp.bfloat16)
+        total = dot(outer, with_ones(v0), NN) + dot(inner, with_ones(v1), NN)
+        highest = jnp.broadcast_to(highest, (group * tokens, HEAD_SIZE))
         for g in range(group):
-            q = q_buf[h, :, g * HEAD_SIZE : (g + 1) * HEAD_SIZE]
-            outer = jnp.where(own, dot(q, k0, NT), dot(q, k2, NT) + bias2)
-            inner = dot(q, k1, NT) + bias1
-            highest = jnp.max(jnp.maximum(outer, inner), axis=1, keepdims=True)
-            outer = jnp.exp2((outer - highest) * EXP2_SCALE)
-            inner = jnp.exp2((inner - highest) * EXP2_SCALE).astype(jnp.bfloat16)
-            first = jnp.where(own, outer, 0.0).astype(jnp.bfloat16)
-            last = jnp.where(own, 0.0, outer)
-            total = dot(first, v0, NN) + dot(inner, v1, NN)
-            scale = 1.0 / (total[:, HEAD_SIZE:] + dot(last.astype(jnp.bfloat16), ones, NN))
-            acc_ref[:, head_columns(h * group + g)] = total[:, :HEAD_SIZE] * scale
-            scaled = last * jnp.concatenate([scale] * (tokens // HEAD_SIZE), axis=1)
-            last_ref[:, head_columns(h * group + g, tokens)] = scaled.astype(jnp.bfloat16)
+            here = slice(g * tokens, (g + 1) * tokens)
+            at = head_columns(h * group + g)
+            acc_ref[:, at] = total[here, :HEAD_SIZE]
+            sum_ref[:, at] = total[here, HEAD_SIZE:]
+            max_ref[:, at] = highest[here]
         return carried
 
     lax.fori_loop(0, heads, one_head, 0)
 
 
-def fine_attention(position, queries, keys, values):
+def near_attention(position, queries, keys, values):
     tokens, columns = queries.shape
     heads = keys[0].shape[1] // HEAD_SIZE
     width = columns // heads
-    pairs = tokens * tokens * 3 * columns // HEAD_SIZE
-    return pl.pallas_call(
-        fine_kernel,
-        in_specs=[SMEM] + [ANY] * 6,
-        out_specs=[VMEM, VMEM],
+    pairs = tokens * tokens * 2 * columns // HEAD_SIZE
+    return pl.pallas_call(
+        near_kernel,
+        in_specs=[SMEM] + [ANY] * 5,
+        out_specs=[VMEM] * 3,
+        out_shape=[jax.ShapeDtypeStruct((tokens, columns), jnp.float32)] * 3,
+        scratch_shapes=[
+            pltpu.VMEM((heads, tokens, width), jnp.bfloat16),
+            pltpu.VMEM((4, heads, tokens, HEAD_SIZE), jnp.bfloat16),
+            pltpu.SemaphoreType.DMA((5, heads)),
+        ],
+        compiler_params=params(),
+        cost_estimate=cost(4 * pairs * HEAD_SIZE, 8 * tokens * columns, pairs),
+    )(position, *in_hbm(queries, keys[0]), keys[1], *in_hbm(values[0]), values[1])
+
+
+def far_kernel(pos_ref, q_hbm, k2_hbm, acc_in, sum_in, max_in, acc_ref, last_ref, q_buf, k_buf, sems):
+    heads, tokens, width = q_buf.shape
+    group = width // HEAD_SIZE
+
+    def copies(h):
+        return [
+            pltpu.make_async_copy(k2_hbm.at[:, head_columns(h)], k_buf.at[h], sems.at[0, h]),
+            pltpu.make_async_copy(q_hbm.at[:, head_columns(h, width)], q_buf.at[h], sems.at[1, h]),
+        ]
+
+    for h in range(heads):
+        for copy in copies(h):
+            copy.start()
+    row = lax.broadcasted_iota(jnp.int32, (tokens, tokens), 0)
+    column = lax.broadcasted_iota(jnp.int32, (tokens, tokens), 1)
+    seen = jnp.concatenate([(column > row) & (pos_ref[0] >= 2)] * group, axis=0)
+    ones = jnp.ones((tokens, HEAD_SIZE), jnp.bfloat16)
+
+    def one_head(h, carried):
+        for copy in copies(h):
+            copy.wait()
+        ats = [head_columns(h * group + g) for g in range(group)]
+        q = jnp.concatenate([q_buf[h, :, g * HEAD_SIZE : (g + 1) * HEAD_SIZE] for g in range(group)], axis=0)
+        scores = jnp.where(seen, dot(q, k_buf[h], NT), MASKED)
+        before = jnp.concatenate([max_in[:, at] for at in ats], axis=0)
+        highest = jnp.maximum(before, jnp.max(scores, axis=1, keepdims=True))
+        spread = jnp.concatenate([highest] * (tokens // HEAD_SIZE), axis=1)
+        weights = jnp.exp2((scores - spread) * EXP2_SCALE).astype(jnp.bfloat16)
+        decay = jnp.exp2((before - highest) * EXP2_SCALE)
+        total = jnp.concatenate([sum_in[:, at] for at in ats], axis=0) * decay + dot(weights, ones, NN)
+        scale = 1.0 / total
+        decay = decay * scale
+        weights = (weights * jnp.concatenate([scale] * (tokens // HEAD_SIZE), axis=1)).astype(jnp.bfloat16)
+        for g in range(group):
+            here = slice(g * tokens, (g + 1) * tokens)
+            acc_ref[:, ats[g]] = acc_in[:, ats[g]] * decay[here]
+            last_ref[:, head_columns(h * group + g, tokens)] = weights[here]
+        return carried
+
+    lax.fori_loop(0, heads, one_head, 0)
+
+
+def far_attention(position, queries, keys, acc, total, highest):
+    tokens, columns = queries.shape
+    heads = keys.shape[1] // HEAD_SIZE
+    width = columns // heads
+    pairs = tokens * tokens * columns // HEAD_SIZE
+    return pl.pallas_call(
+        far_kernel,
+        in_specs=[SMEM, ANY, ANY] + [VMEM] * 3,
+        out_specs=[VMEM] * 2,
         out_shape=[
             jax.ShapeDtypeStruct((tokens, columns), jnp.float32),
             jax.ShapeDtypeStruct((tokens, columns // HEAD_SIZE * tokens), jnp.bfloat16),
         ],
         scratch_shapes=[
             pltpu.VMEM((heads, tokens, width), jnp.bfloat16),
-            pltpu.VMEM((5, heads, tokens, HEAD_SIZE), jnp.bfloat16),
-            pltpu.SemaphoreType.DMA((6, heads)),
+            pltpu.VMEM((heads, tokens, HEAD_SIZE), jnp.bfloat16),
+            pltpu.SemaphoreType.DMA((2, heads)),
         ],
         compiler_params=params(),
         cost_estimate=cost(4 * pairs * HEAD_SIZE, 12 * tokens * columns, pairs),
-    )(position, queries, *keys, *values)
-
-
-def join_kernel(my_ref, acc_ref, last_ref, v2_hbm, up_ref, *refs):
-    sections = len(refs) - 5
-    coarse, (comb_ref, sq_ref, v2_buf, coarse_buf, sem) = refs[:sections], refs[sections:]
-    copy = pltpu.make_async_copy(v2_hbm, v2_buf, sem)
-    copy.start()
+    )(position, *in_hbm(queries), keys, acc, total, highest)
+
+
+def join_kernel(my_ref, acc_ref, last_ref, v2_hbm, up_hbm, *refs):
+    sections = len(refs) - 6
+    coarse, (comb_ref, sq_ref, v2_buf, up_ref, coarse_buf, sems) = refs[:sections], refs[sections:]
+    copies = [
+        pltpu.make_async_copy(v2_hbm, v2_buf, sems.at[0]),
+        pltpu.make_async_copy(up_hbm, up_ref, sems.at[1]),
+    ]
+    for copy in copies:
+        copy.start()
     tokens, columns = acc_ref.shape
     heads = v2_buf.shape[1] // HEAD_SIZE
     width = columns // heads
@@ -321,7 +380,8 @@
     token = lax.broadcasted_iota(jnp.int32, (tokens, pooled), 0)
     spread = jnp.where(token // POOL_FACTOR == lax.broadcasted_iota(jnp.int32, (tokens, pooled), 1), 1.0, 0.0)
     spread = spread.astype(jnp.bfloat16)
-    copy.wait()
+    for copy in copies:
+        copy.wait()
 
     def one_head(h, squares):
         wide = head_columns(h, width)
@@ -348,7 +408,7 @@
     pooled, width = coarse[0].shape
     return pl.pallas_call(
         join_kernel,
-        in_specs=[SMEM, VMEM, VMEM, ANY, VMEM] + [VMEM] * len(coarse),
+        in_specs=[SMEM, VMEM, VMEM, ANY, ANY] + [VMEM] * len(coarse),
         out_specs=[VMEM, VMEM],
         out_shape=[
             jax.ShapeDtypeStruct((tokens, columns), jnp.float32),
@@ -356,12 +416,13 @@
         ],
         scratch_shapes=[
             pltpu.VMEM(values.shape, jnp.bfloat16),
+            pltpu.VMEM(up_weight.shape, jnp.float32),
             pltpu.VMEM((len(coarse), pooled, width), jnp.bfloat16),
-            pltpu.SemaphoreType.DMA,
+            pltpu.SemaphoreType.DMA((2,)),
         ],
         compiler_params=params(),
         cost_estimate=cost(2 * tokens * tokens * columns, 12 * tokens * columns),
-    )(my, acc, last, values, up_weight, *coarse)
+    )(my, acc, last, values, *in_hbm(up_weight), *coarse)
 
 
 def norm_kernel(full, comb_ref, mine_ref, other_ref, gain_ref, out_hbm, buf, sems):
@@ -409,18 +470,29 @@
     my = section[None]
     others = range(1, section_count)
 
-    k1 = in_ring(keys, line)
-    v1 = in_ring(values, line)
-    payloads = pool(my, queries, keys, values, qw, kw, vw)
-    payloads = [payloads[0]] + [exchanged(payloads[m], "section", m) for m in others]
-    blocks = gathered(stack(my, payloads), "seq")
-    k2 = in_ring(k1, line)
-    v2 = in_ring(v1, line)
-    coarse = coarse_attention(jnp.stack([section, z]), payloads, blocks)
-    coarse = [coarse[0]] + [exchanged(coarse[m], "section", m) for m in others]
-    acc, last = fine_attention(position[None], queries, (keys, k1, k2), (values, v1))
+    k1 = in_ring(keys, line, "first_keys")
+    payloads = list(pool(my, queries, keys, values, qw, kw, vw))
+    for m in others:
+        payloads[m] = exchanged(payloads[m], "section", m, "pooled_to_heads")
+    *payloads, late_values = lax.optimization_barrier((*payloads, values))
+    v1 = in_ring(late_values, line, "first_values")
+    stacked = stack(my, payloads)
+    far = exchanged(stacked, "seq", 2, "pooled_far")
+    near = exchanged(stacked, "seq", 1, "pooled_near")
+    acc, total, highest = near_attention(position[None], queries, (keys, k1), (values, v1))
+    far, near, acc = lax.optimization_barrier((far, near, acc))
+    farther = exchanged(far, "seq", 1, "pooled_farther")
+    far, k1 = lax.optimization_barrier((far, k1))
+    k2 = in_ring(k1, line, "second_keys")
+    farther, v1 = lax.optimization_barrier((farther, v1))
+    v2 = in_ring(v1, line, "second_values")
+    blocks = [stacked, near, far, farther]
+    coarse = list(coarse_attention(jnp.stack([section, z]), payloads, blocks))
+    for m in others:
+        coarse[m] = exchanged(coarse[m], "section", m, "coarse_back")
+    acc, last = far_attention(position[None], queries, k2, acc, total, highest)
     combined, mine = join(my, acc, last, v2, up_weight, coarse)
-    other = exchanged(mine, "head", 1)
+    other = exchanged(mine, "head", 1, "squares")
     return normalized(combined, mine, other, out_gain[None], head_count * columns)
 
 

time: 64.7 us -> 55.9 us (0.86)
  waiting for transfers between devices: 26.8 us -> 20.3 us
  local copies, waits for them, and re-layouts: 4.34 us -> 0.01 us
  Pallas kernels: 15.6 us -> 18.5 us
    ppermute x10, waiting for transfers between devices: 26.8 us -> 11.2 us  [exchanged(): lax.ppermute(value, axis, [(source, source ^ offset) for source in range(...]
    ppermute x4, waiting for transfers between devices: 0.01 us -> 9.08 us  [in_ring(): lax.ppermute(value, axis, [(source, (source + 1) % count) for source in r...]
    unnamed x18 -> x2, local copies, waits for them, and re-layouts: 4.34 us -> 0.01 us
    pallas_call x2 -> x3, Pallas kernels: 9.68 us -> 12.4 us  [the longest x1 5.98 us: near_attention(): pl.pallas_call(near_kernel, in_specs=[SMEM] + [ANY] * 5, out_specs=[VMEM]...]
    ppermute x4, starting transfers between devices: 7.26 us -> 5.62 us  [in_ring(): lax.ppermute(value, axis, [(source, (source + 1) % count) for source in r...]
    ppermute x10, starting transfers between devices: 10.1 us -> 11.2 us  [exchanged(): lax.ppermute(value, axis, [(source, source ^ offset) for source in range(...]
  transfers between devices with their start and end apart: 14 -> 14, of which waited for: 6 -> 9; matrix products, arithmetic and copies ran while one was open for 0% -> 0% of each run, Pallas kernels for 20% -> 22%
where the time goes in v3:
time: 55.9 us; the launch traced here: 55.7 us
  waiting for transfers between devices  20.3 us (36%)
  Pallas kernels  18.5 us (33%)
  starting transfers between devices  16.8 us (30%)
    ppermute x10, starting transfers between devices, exchanged(): lax.ppermute(value, axis, [(source, source ^ offset) for source in range(...  11.2 us
    ppermute x10, waiting for transfers between devices, exchanged(): lax.ppermute(value, axis, [(source, source ^ offset) for source in range(...  11.2 us
    ppermute x4, waiting for transfers between devices, in_ring(): lax.ppermute(value, axis, [(source, (source + 1) % count) for source in r...  9.08 us
    pallas_call x1, Pallas kernels, near_attention(): pl.pallas_call(near_kernel, in_specs=[SMEM] + [ANY] * 5, out_specs=[VMEM]...  5.98 us
    ppermute x4, starting transfers between devices, in_ring(): lax.ppermute(value, axis, [(source, (source + 1) % count) for source in r...  5.62 us
    pallas_call x1, Pallas kernels, far_attention(): pl.pallas_call(far_kernel, in_specs=[SMEM, ANY, ANY] + [VMEM] * 3, out_sp...  3.99 us
    pallas_call x1, Pallas kernels, pool(): pl.pallas_call(pool_kernel, in_specs=[SMEM] + [ANY] * 6, out_specs=[VMEM]...  2.51 us
    pallas_call x1, Pallas kernels, join(): pl.pallas_call(join_kernel, in_specs=[SMEM, VMEM, VMEM, ANY, ANY] + [VMEM...  2.44 us
  transfers between devices with their start and end apart: 14, of which 9 were waited for; matrix products, arithmetic and copies ran while one was open for 0% of the time, Pallas kernels for 22%

profile of v3, /device:TPU:0, one launch (start us, length us, event | category | flops | bytes accessed | tf_op | source)
XLA Modules:
  0.0 55.7 jit_solution(15796178137131116179)
XLA Ops:
  0.0 2.5 %shard_map.82 = (bf16[64,768]{1,0:T(8,128)(2,1)S(1)}, bf16[64,768]{1,0:T(8,128)(2,1)S(1)}, bf16[64,768]{1,0:T(8,128)(2,1)S(1)}, bf16[64,768]{1,0:T(8,128)(2,1)S(1)}) custom-call(s32[1]{0:T(128)} %bitcast.my_ref, bf16[256,2048]{1,0:T(8,128)(2,1)} %q_hbm.5, bf16[256,512]{1,0:T(8,128)(2,1)} %k0_hbm.1, bf16[256,512]{1,0:T(8,128)(2,1)} %v0_hbm.1, ...), custom_call_target="tpu_custom_call" | custom-call | flops 1000 | bytes 1000 | tf_op jit(solution)/shard_map/pallas_call | solution.py:105
  2.5 3.0 %collective-permute-start = (bf16[64,768]{1,0:T(8,128)(2,1)S(1)}, bf16[64,768]{1,0:T(8,128)(2,1)S(1)}, u32[]{:S(2)}, u32[]{:S(2)}) collective-permute-start(bf16[64,768]{1,0:T(8,128)(2,1)S(1)} %get-tuple-element.33), channel_id=1, source_target_pairs={{0,8},{8,0},{16,24},{24,16},{1,9},{9,1},{17,25},{25,17},{2,10},{10... | collective-permute-start | bytes 294920 | tf_op jit(solution)/shard_map/pooled_to_heads1/ppermute | solution.py:53
  5.5 1.5 %collective-permute-start.1 = (bf16[64,768]{1,0:T(8,128)(2,1)S(1)}, bf16[64,768]{1,0:T(8,128)(2,1)S(1)}, u32[]{:S(2)}, u32[]{:S(2)}) collective-permute-start(bf16[64,768]{1,0:T(8,128)(2,1)S(1)} %get-tuple-element.34), channel_id=1, source_target_pairs={{0,16},{8,24},{16,0},{24,8},{1,17},{9,25},{17,1},{25,9},{2,18},{10... | collective-permute-start | bytes 294920 | tf_op jit(solution)/shard_map/pooled_to_heads2/ppermute | solution.py:53
  7.1 0.0 collective-permute-start.2
  7.1 2.0 %collective-permute-start.5 = (bf16[256,512]{1,0:T(8,128)(2,1)}, bf16[256,512]{1,0:T(8,128)(2,1)S(1)}, u32[]{:S(2)}, u32[]{:S(2)}) collective-permute-start(bf16[256,512]{1,0:T(8,128)(2,1)} %k0_hbm.1), channel_id=1, source_target_pairs={{0,2},{2,4},{4,6},{6,8},{8,10},{10,12},{12,14},{14,16},{16,18},{18... | collective-permute-start | bytes 786440 | tf_op jit(solution)/shard_map/first_keys/ppermute | solution.py:47
  9.1 0.0 collective-permute-done.refs_1_
  9.1 2.1 %collective-permute-done.1.refs_2_ = bf16[64,768]{1,0:T(8,128)(2,1)S(1)} collective-permute-done((bf16[64,768]{1,0:T(8,128)(2,1)S(1)}, bf16[64,768]{1,0:T(8,128)(2,1)S(1)}, u32[]{:S(2)}, u32[]{:S(2)}) %collective-permute-start.1) | collective-permute-done | bytes 98336 | tf_op jit(solution)/shard_map/pooled_to_heads2/ppermute | solution.py:53
  11.2 1.4 %collective-permute-done.2.refs_3_ = bf16[64,768]{1,0:T(8,128)(2,1)S(1)} collective-permute-done((bf16[64,768]{1,0:T(8,128)(2,1)S(1)}, bf16[64,768]{1,0:T(8,128)(2,1)S(1)}, u32[]{:S(2)}, u32[]{:S(2)}) %collective-permute-start.2) | collective-permute-done | bytes 98336 | tf_op jit(solution)/shard_map/pooled_to_heads3/ppermute | solution.py:53
  12.6 1.6 %collective-permute-start.6 = (bf16[256,512]{1,0:T(8,128)(2,1)}, bf16[256,512]{1,0:T(8,128)(2,1)S(1)}, u32[]{:S(2)}, u32[]{:S(2)}) collective-permute-start(bf16[256,512]{1,0:T(8,128)(2,1)} %v0_hbm.1), channel_id=1, source_target_pairs={{0,2},{2,4},{4,6},{6,8},{8,10},{10,12},{12,14},{14,16},{16,18},{18... | collective-permute-start | bytes 786440 | tf_op jit(solution)/shard_map/first_values/ppermute | solution.py:47
  14.2 1.6 %collective-permute-start.4 = (bf16[272,256]{1,0:T(8,128)(2,1)S(1)}, bf16[272,256]{1,0:T(8,128)(2,1)S(1)}, u32[]{:S(2)}, u32[]{:S(2)}) collective-permute-start(bf16[272,256]{1,0:T(8,128)(2,1)S(1)} %shard_map.83.refs_4_), channel_id=1, source_target_pairs={{0,2},{2,0},{4,6},{6,4},{1,3},{3,1},{5,7},{7,5},{8,10},{10,8},{12,... | collective-permute-start | bytes 417800 | tf_op jit(solution)/shard_map/pooled_near1/ppermute | solution.py:53
  15.8 1.3 %collective-permute-start.3 = (bf16[272,256]{1,0:T(8,128)(2,1)S(1)}, bf16[272,256]{1,0:T(8,128)(2,1)S(1)}, u32[]{:S(2)}, u32[]{:S(2)}) collective-permute-start(bf16[272,256]{1,0:T(8,128)(2,1)S(1)} %shard_map.83.refs_4_), channel_id=1, source_target_pairs={{0,4},{2,6},{4,0},{6,2},{1,5},{3,7},{5,1},{7,3},{8,12},{10,14},{12... | collective-permute-start | bytes 417800 | tf_op jit(solution)/shard_map/pooled_far2/ppermute | solution.py:53
  17.1 3.2 %collective-permute-done.5.k1_hbm = bf16[256,512]{1,0:T(8,128)(2,1)S(1)} collective-permute-done((bf16[256,512]{1,0:T(8,128)(2,1)}, bf16[256,512]{1,0:T(8,128)(2,1)S(1)}, u32[]{:S(2)}, u32[]{:S(2)}) %collective-permute-start.5) | collective-permute-done | bytes 262176 | tf_op jit(solution)/shard_map/first_keys/ppermute | solution.py:47
  20.3 5.6 %collective-permute-done.6.v1_hbm = bf16[256,512]{1,0:T(8,128)(2,1)S(1)} collective-permute-done((bf16[256,512]{1,0:T(8,128)(2,1)}, bf16[256,512]{1,0:T(8,128)(2,1)S(1)}, u32[]{:S(2)}, u32[]{:S(2)}) %collective-permute-start.6) | collective-permute-done | bytes 262176 | tf_op jit(solution)/shard_map/first_values/ppermute | solution.py:47
  25.9 6.0 %shard_map.84 = (f32[256,2048]{1,0:T(8,128)S(1)}, f32[256,2048]{1,0:T(8,128)S(1)}, f32[256,2048]{1,0:T(8,128)S(1)}) custom-call(s32[1]{0:T(128)} %bitcast.1.pos_ref, bf16[256,2048]{1,0:T(8,128)(2,1)} %q_hbm.5, bf16[256,512]{1,0:T(8,128)(2,1)} %k0_hbm.1, bf16[256,512]{1,0:T(8,128)(2,1)S(1)} %collective-permute-done.5.k1_hbm, bf16[256,512]{1,0:T(8,128)(2,1)} %v0_hbm.1, ...), custom_call_target="tpu_custom_call" | custom-call | flops 1073741824 | bytes 4194304 | tf_op jit(solution)/shard_map/pallas_call | solution.py:284
  31.9 0.0 collective-permute-done.4.refs_5_
  31.9 0.0 collective-permute-done.3.refs_6_
  31.9 0.1 collective-permute-start.8
  32.0 2.0 %collective-permute-start.7 = (bf16[256,512]{1,0:T(8,128)(2,1)S(1)}, bf16[256,512]{1,0:T(8,128)(2,1)S(1)}, u32[]{:S(2)}, u32[]{:S(2)}) collective-permute-start(bf16[256,512]{1,0:T(8,128)(2,1)S(1)} %collective-permute-done.5.k1_hbm), channel_id=1, source_target_pairs={{0,2},{2,4},{4,6},{6,8},{8,10},{10,12},{12,14},{14,16},{16,18},{18... | collective-permute-start | bytes 786440 | tf_op jit(solution)/shard_map/second_keys/ppermute | solution.py:47
  34.0 5.2 %collective-permute-done.8.refs_7_ = bf16[272,256]{1,0:T(8,128)(2,1)S(1)} collective-permute-done((bf16[272,256]{1,0:T(8,128)(2,1)S(1)}, bf16[272,256]{1,0:T(8,128)(2,1)S(1)}, u32[]{:S(2)}, u32[]{:S(2)}) %collective-permute-start.8) | collective-permute-done | bytes 139296 | tf_op jit(solution)/shard_map/pooled_farther1/ppermute | solution.py:53
  39.2 0.1 pad_add_fusion.place_ref
  39.2 2.4 %shard_map.86 = (bf16[64,512]{1,0:T(8,128)(2,1)S(1)}, bf16[64,512]{1,0:T(8,128)(2,1)S(1)}, bf16[64,512]{1,0:T(8,128)(2,1)S(1)}, bf16[64,512]{1,0:T(8,128)(2,1)S(1)}) custom-call(s32[2]{0:T(128)S(1)} %pad_add_fusion.place_ref, bf16[64,768]{1,0:T(8,128)(2,1)S(1)} %get-tuple-element.36.refs_0_, bf16[64,768]{1,0:T(8,128)(2,1)S(1)} %collective-permute-done.refs_1_, ...), custom_call_target="tpu_custom_call" | custom-call | flops 536870912 | bytes 1048576 | tf_op jit(solution)/shard_map/pallas_call | solution.py:219
  41.7 0.8 %collective-permute-start.10 = (bf16[64,512]{1,0:T(8,128)(2,1)S(1)}, bf16[64,512]{1,0:T(8,128)(2,1)S(1)}, u32[]{:S(2)}, u32[]{:S(2)}) collective-permute-start(bf16[64,512]{1,0:T(8,128)(2,1)S(1)} %get-tuple-element.54), channel_id=1, source_target_pairs={{0,8},{8,0},{16,24},{24,16},{1,9},{9,1},{17,25},{25,17},{2,10},{10... | collective-permute-start | bytes 196616 | tf_op jit(solution)/shard_map/coarse_back1/ppermute | solution.py:53
  42.5 1.3 %collective-permute-start.11 = (bf16[64,512]{1,0:T(8,128)(2,1)S(1)}, bf16[64,512]{1,0:T(8,128)(2,1)S(1)}, u32[]{:S(2)}, u32[]{:S(2)}) collective-permute-start(bf16[64,512]{1,0:T(8,128)(2,1)S(1)} %get-tuple-element.55), channel_id=1, source_target_pairs={{0,16},{8,24},{16,0},{24,8},{1,17},{9,25},{17,1},{25,9},{2,18},{10... | collective-permute-start | bytes 196616 | tf_op jit(solution)/shard_map/coarse_back2/ppermute | solution.py:53
  43.8 1.4 %collective-permute-start.12 = (bf16[64,512]{1,0:T(8,128)(2,1)S(1)}, bf16[64,512]{1,0:T(8,128)(2,1)S(1)}, u32[]{:S(2)}, u32[]{:S(2)}) collective-permute-start(bf16[64,512]{1,0:T(8,128)(2,1)S(1)} %get-tuple-element.56), channel_id=1, source_target_pairs={{0,24},{8,16},{16,8},{24,0},{1,25},{9,17},{17,9},{25,1},{2,26},{10... | collective-permute-start | bytes 196616 | tf_op jit(solution)/shard_map/coarse_back3/ppermute | solution.py:53
  45.2 0.3 collective-permute-done.7.k2_hbm
  45.5 4.0 %shard_map.85 = (f32[256,2048]{1,0:T(8,128)S(1)}, bf16[256,4096]{1,0:T(8,128)(2,1)S(1)}) custom-call(s32[1]{0:T(128)} %bitcast.1.pos_ref, bf16[256,2048]{1,0:T(8,128)(2,1)} %q_hbm.5, bf16[256,512]{1,0:T(8,128)(2,1)S(1)} %collective-permute-done.7.k2_hbm, f32[256,2048]{1,0:T(8,128)S(1)} %get-tuple-element.44.acc_in, ...), custom_call_target="tpu_custom_call" | custom-call | flops 536870912 | bytes 6291456 | tf_op jit(solution)/shard_map/pallas_call | solution.py:346
  49.5 0.1 collective-permute-done.10.refs_1_
  49.7 1.0 %collective-permute-done.11.refs_2_ = bf16[64,512]{1,0:T(8,128)(2,1)S(1)} collective-permute-done((bf16[64,512]{1,0:T(8,128)(2,1)S(1)}, bf16[64,512]{1,0:T(8,128)(2,1)S(1)}, u32[]{:S(2)}, u32[]{:S(2)}) %collective-permute-start.11) | collective-permute-done | bytes 65568 | tf_op jit(solution)/shard_map/coarse_back2/ppermute | solution.py:53
  50.7 2.4 %shard_map.87 = (f32[256,2048]{1,0:T(8,128)S(1)}, f32[256,128]{1,0:T(8,128)S(1)}) custom-call(s32[1]{0:T(128)} %bitcast.my_ref, f32[256,2048]{1,0:T(8,128)S(1)} %get-tuple-element.47.acc_ref, bf16[256,4096]{1,0:T(8,128)(2,1)S(1)} %get-tuple-element.48.last_ref, bf16[256,512]{1,0:T(8,128)(2,1)S(1)} %collective-permute-done.9.v2_hbm, f32[4,2048]{1,0:T(4,128)} %up_hbm.1, ...), custom_call_target="tpu_custom_call" | custom-call | flops 268435456 | bytes 6291456 | tf_op jit(solution)/shard_map/pallas_call | solution.py:409
  53.2 0.1 collective-permute-start.13
  53.2 1.3 %collective-permute-done.13.other_ref = f32[256,128]{1,0:T(8,128)S(1)} collective-permute-done((f32[256,128]{1,0:T(8,128)S(1)}, f32[256,128]{1,0:T(8,128)S(1)}, u32[]{:S(2)}, u32[]{:S(2)}) %collective-permute-start.13) | collective-permute-done | bytes 131104 | tf_op jit(solution)/shard_map/squares1/ppermute | solution.py:53
  54.6 1.1 %shard_map.88 = bf16[256,2048]{1,0:T(8,128)(2,1)} custom-call(f32[256,2048]{1,0:T(8,128)S(1)} %get-tuple-element.57.comb_ref, f32[256,128]{1,0:T(8,128)S(1)} %get-tuple-element.58.mine_ref, f32[256,128]{1,0:T(8,128)S(1)} %collective-permute-done.13.other_ref, f32[1,2048]{1,0:T(1,128)S(1)} %bitcast.4), custom_call_target="tpu_custom_call" | custom-call | flops 1572864 | bytes 3145728 | tf_op jit(solution)/shard_map/pallas_call | solution.py:444
  (6 shorter events, 0.0 us)
Async XLA Ops:
  2.5 6.6 %collective-permute-start = (bf16[64,768]{1,0:T(8,128)(2,1)S(1)}, bf16[64,768]{1,0:T(8,128)(2,1)S(1)}, u32[]{:S(2)}, u32[]{:S(2)}) collective-permute-start(bf16[64,768]{1,0:T(8,128)(2,1)S(1)} %get-tuple-element.33), channel_id=1, source_target_pairs={{0,8},{8,0},{16,24},{24,16},{1,9},{9,1},{17,25},{25,17},{2,10},{10... | collective-permute-start | bytes 294920 | tf_op jit(solution)/shard_map/pooled_to_heads1/ppermute | solution.py:53
  5.5 5.7 %collective-permute-start.1 = (bf16[64,768]{1,0:T(8,128)(2,1)S(1)}, bf16[64,768]{1,0:T(8,128)(2,1)S(1)}, u32[]{:S(2)}, u32[]{:S(2)}) collective-permute-start(bf16[64,768]{1,0:T(8,128)(2,1)S(1)} %get-tuple-element.34), channel_id=1, source_target_pairs={{0,16},{8,24},{16,0},{24,8},{1,17},{9,25},{17,1},{25,9},{2,18},{10... | collective-permute-start | bytes 294920 | tf_op jit(solution)/shard_map/pooled_to_heads2/ppermute | solution.py:53
  7.1 5.5 %collective-permute-start.2 = (bf16[64,768]{1,0:T(8,128)(2,1)S(1)}, bf16[64,768]{1,0:T(8,128)(2,1)S(1)}, u32[]{:S(2)}, u32[]{:S(2)}) collective-permute-start(bf16[64,768]{1,0:T(8,128)(2,1)S(1)} %get-tuple-element.35), channel_id=1, source_target_pairs={{0,24},{8,16},{16,8},{24,0},{1,25},{9,17},{17,9},{25,1},{2,26},{10... | collective-permute-start | bytes 294920 | tf_op jit(solution)/shard_map/pooled_to_heads3/ppermute | solution.py:53
  7.1 13.2 %collective-permute-start.5 = (bf16[256,512]{1,0:T(8,128)(2,1)}, bf16[256,512]{1,0:T(8,128)(2,1)S(1)}, u32[]{:S(2)}, u32[]{:S(2)}) collective-permute-start(bf16[256,512]{1,0:T(8,128)(2,1)} %k0_hbm.1), channel_id=1, source_target_pairs={{0,2},{2,4},{4,6},{6,8},{8,10},{10,12},{12,14},{14,16},{16,18},{18... | collective-permute-start | bytes 786440 | tf_op jit(solution)/shard_map/first_keys/ppermute | solution.py:47
  12.6 13.3 %collective-permute-start.6 = (bf16[256,512]{1,0:T(8,128)(2,1)}, bf16[256,512]{1,0:T(8,128)(2,1)S(1)}, u32[]{:S(2)}, u32[]{:S(2)}) collective-permute-start(bf16[256,512]{1,0:T(8,128)(2,1)} %v0_hbm.1), channel_id=1, source_target_pairs={{0,2},{2,4},{4,6},{6,8},{8,10},{10,12},{12,14},{14,16},{16,18},{18... | collective-permute-start | bytes 786440 | tf_op jit(solution)/shard_map/first_values/ppermute | solution.py:47
  14.2 17.7 %collective-permute-start.4 = (bf16[272,256]{1,0:T(8,128)(2,1)S(1)}, bf16[272,256]{1,0:T(8,128)(2,1)S(1)}, u32[]{:S(2)}, u32[]{:S(2)}) collective-permute-start(bf16[272,256]{1,0:T(8,128)(2,1)S(1)} %shard_map.83.refs_4_), channel_id=1, source_target_pairs={{0,2},{2,0},{4,6},{6,4},{1,3},{3,1},{5,7},{7,5},{8,10},{10,8},{12,... | collective-permute-start | bytes 417800 | tf_op jit(solution)/shard_map/pooled_near1/ppermute | solution.py:53
  15.8 16.1 %collective-permute-start.3 = (bf16[272,256]{1,0:T(8,128)(2,1)S(1)}, bf16[272,256]{1,0:T(8,128)(2,1)S(1)}, u32[]{:S(2)}, u32[]{:S(2)}) collective-permute-start(bf16[272,256]{1,0:T(8,128)(2,1)S(1)} %shard_map.83.refs_4_), channel_id=1, source_target_pairs={{0,4},{2,6},{4,0},{6,2},{1,5},{3,7},{5,1},{7,3},{8,12},{10,14},{12... | collective-permute-start | bytes 417800 | tf_op jit(solution)/shard_map/pooled_far2/ppermute | solution.py:53
  31.9 7.3 %collective-permute-start.8 = (bf16[272,256]{1,0:T(8,128)(2,1)S(1)}, bf16[272,256]{1,0:T(8,128)(2,1)S(1)}, u32[]{:S(2)}, u32[]{:S(2)}) collective-permute-start(bf16[272,256]{1,0:T(8,128)(2,1)S(1)} %collective-permute-done.3.refs_6_), channel_id=1, source_target_pairs={{0,2},{2,0},{4,6},{6,4},{1,3},{3,1},{5,7},{7,5},{8,10},{10,8},{12,... | collective-permute-start | bytes 417800 | tf_op jit(solution)/shard_map/pooled_farther1/ppermute | solution.py:53
  32.0 13.6 %collective-permute-start.7 = (bf16[256,512]{1,0:T(8,128)(2,1)S(1)}, bf16[256,512]{1,0:T(8,128)(2,1)S(1)}, u32[]{:S(2)}, u32[]{:S(2)}) collective-permute-start(bf16[256,512]{1,0:T(8,128)(2,1)S(1)} %collective-permute-done.5.k1_hbm), channel_id=1, source_target_pairs={{0,2},{2,4},{4,6},{6,8},{8,10},{10,12},{12,14},{14,16},{16,18},{18... | collective-permute-start | bytes 786440 | tf_op jit(solution)/shard_map/second_keys/ppermute | solution.py:47
  39.2 11.5 %collective-permute-start.9 = (bf16[256,512]{1,0:T(8,128)(2,1)S(1)}, bf16[256,512]{1,0:T(8,128)(2,1)S(1)}, u32[]{:S(2)}, u32[]{:S(2)}) collective-permute-start(bf16[256,512]{1,0:T(8,128)(2,1)S(1)} %collective-permute-done.6.v1_hbm), channel_id=1, source_target_pairs={{0,2},{2,4},{4,6},{6,8},{8,10},{10,12},{12,14},{14,16},{16,18},{18... | collective-permute-start | bytes 786440 | tf_op jit(solution)/shard_map/second_values/ppermute | solution.py:47
  41.7 8.0 %collective-permute-start.10 = (bf16[64,512]{1,0:T(8,128)(2,1)S(1)}, bf16[64,512]{1,0:T(8,128)(2,1)S(1)}, u32[]{:S(2)}, u32[]{:S(2)}) collective-permute-start(bf16[64,512]{1,0:T(8,128)(2,1)S(1)} %get-tuple-element.54), channel_id=1, source_target_pairs={{0,8},{8,0},{16,24},{24,16},{1,9},{9,1},{17,25},{25,17},{2,10},{10... | collective-permute-start | bytes 196616 | tf_op jit(solution)/shard_map/coarse_back1/ppermute | solution.py:53
  42.5 8.2 %collective-permute-start.11 = (bf16[64,512]{1,0:T(8,128)(2,1)S(1)}, bf16[64,512]{1,0:T(8,128)(2,1)S(1)}, u32[]{:S(2)}, u32[]{:S(2)}) collective-permute-start(bf16[64,512]{1,0:T(8,128)(2,1)S(1)} %get-tuple-element.55), channel_id=1, source_target_pairs={{0,16},{8,24},{16,0},{24,8},{1,17},{9,25},{17,1},{25,9},{2,18},{10... | collective-permute-start | bytes 196616 | tf_op jit(solution)/shard_map/coarse_back2/ppermute | solution.py:53
  43.8 6.9 %collective-permute-start.12 = (bf16[64,512]{1,0:T(8,128)(2,1)S(1)}, bf16[64,512]{1,0:T(8,128)(2,1)S(1)}, u32[]{:S(2)}, u32[]{:S(2)}) collective-permute-start(bf16[64,512]{1,0:T(8,128)(2,1)S(1)} %get-tuple-element.56), channel_id=1, source_target_pairs={{0,24},{8,16},{16,8},{24,0},{1,25},{9,17},{17,9},{25,1},{2,26},{10... | collective-permute-start | bytes 196616 | tf_op jit(solution)/shard_map/coarse_back3/ppermute | solution.py:53
  50.7 3.9 %copy-start = (f32[2048]{0:T(1024)S(1)}, f32[2048]{0:T(1024)}, u32[]{:S(2)}) copy-start(f32[2048]{0:T(1024)} %param.15) | copy-start | bytes 24580
  53.2 1.4 %collective-permute-start.13 = (f32[256,128]{1,0:T(8,128)S(1)}, f32[256,128]{1,0:T(8,128)S(1)}, u32[]{:S(2)}, u32[]{:S(2)}) collective-permute-start(f32[256,128]{1,0:T(8,128)S(1)} %get-tuple-element.58.mine_ref), channel_id=1, source_target_pairs={{0,1},{1,0},{2,3},{3,2},{4,5},{5,4},{6,7},{7,6},{8,9},{9,8},{10,11... | collective-permute-start | bytes 393224 | tf_op jit(solution)/shard_map/squares1/ppermute | solution.py:53

commit v4 on v3

--- a/solution.py
+++ b/solution.py
@@ -54,29 +54,23 @@
 
 
 def pool_kernel(my_ref, q_hbm, k_hbm, v_hbm, qw_hbm, kw_hbm, vw_hbm, *rest):
-    heads = len(rest) - 5
-    outs, (q_buf, kv_buf, qw_buf, kvw_buf, sems) = rest[:heads], rest[heads:]
+    heads = len(rest) - 7
+    outs, (q_buf, k_buf, v_buf, qw_buf, kw_buf, vw_buf, sems) = rest[:heads], rest[heads:]
     tokens = q_hbm.shape[0]
     width = q_hbm.shape[1] // heads
     pooled = tokens // POOL_FACTOR
     my = my_ref[0]
-    left, right = pl.ds(0, HEAD_SIZE), pl.ds(HEAD_SIZE, HEAD_SIZE)
-    copies = []
-    for m in range(heads):
-        h = my ^ m
-        wide, narrow = head_columns(h, width), head_columns(h)
-        pairs = [
-            (k_hbm.at[:, narrow], kv_buf.at[m, :, left]),
-            (v_hbm.at[:, narrow], kv_buf.at[m, :, right]),
-            (kw_hbm.at[:, narrow], kvw_buf.at[m, :, left]),
-            (vw_hbm.at[:, narrow], kvw_buf.at[m, :, right]),
-            (q_hbm.at[:, wide], q_buf.at[m]),
-            (qw_hbm.at[:, wide], qw_buf.at[m]),
-        ]
-        copies.append([pltpu.make_async_copy(a, b, sems.at[m, i]) for i, (a, b) in enumerate(pairs)])
-    for group in copies:
-        for copy in group:
-            copy.start()
+    pairs = (
+        (k_hbm, k_buf),
+        (v_hbm, v_buf),
+        (kw_hbm, kw_buf),
+        (vw_hbm, vw_buf),
+        (qw_hbm, qw_buf),
+        (q_hbm, q_buf),
+    )
+    copies = [pltpu.make_async_copy(a, b, sems.at[i]) for i, (a, b) in enumerate(pairs)]
+    for copy in copies:
+        copy.start()
     row = lax.broadcasted_iota(jnp.int32, (tokens, tokens), 0)
     column = lax.broadcasted_iota(jnp.int32, (tokens, tokens), 1)
     wanted = POOL_FACTOR * (row % pooled) + row // pooled
@@ -89,11 +83,18 @@
             total = total + picked[i * pooled : (i + 1) * pooled] * weights[i : i + 1]
         return total.astype(jnp.bfloat16)
 
+    for copy in copies[:4]:
+        copy.wait()
     for m in range(heads):
-        for copy in copies[m]:
-            copy.wait()
-        outs[m][:, :width] = weighted(q_buf[m], qw_buf[m])
-        outs[m][:, width:] = weighted(kv_buf[m], kvw_buf[m])
+        narrow = head_columns(my ^ m)
+        rows = jnp.concatenate([k_buf[:, narrow], v_buf[:, narrow]], axis=1)
+        weights = jnp.concatenate([kw_buf[:, narrow], vw_buf[:, narrow]], axis=1)
+        outs[m][:, width:] = weighted(rows, weights)
+    for copy in copies[4:]:
+        copy.wait()
+    for m in range(heads):
+        wide = head_columns(my ^ m, width)
+        outs[m][:, :width] = weighted(q_buf[:, wide], qw_buf[:, wide])
 
 
 def pool(my, queries, keys, values, qw, kw, vw):
@@ -108,11 +109,13 @@
         out_specs=[VMEM] * heads,
         out_shape=[payload] * heads,
         scratch_shapes=[
-            pltpu.VMEM((heads, tokens, width), jnp.bfloat16),
-            pltpu.VMEM((heads, tokens, span), jnp.bfloat16),
-            pltpu.VMEM((heads, POOL_FACTOR, width), jnp.float32),
-            pltpu.VMEM((heads, POOL_FACTOR, span), jnp.float32),
-            pltpu.SemaphoreType.DMA((heads, 6)),
+            pltpu.VMEM(queries.shape, jnp.bfloat16),
+            pltpu.VMEM(keys.shape, jnp.bfloat16),
+            pltpu.VMEM(values.shape, jnp.bfloat16),
+            pltpu.VMEM(qw.shape, jnp.float32),
+            pltpu.VMEM(kw.shape, jnp.float32),
+            pltpu.VMEM(vw.shape, jnp.float32),
+            pltpu.SemaphoreType.DMA((6,)),
         ],
         compiler_params=params(),
         cost_estimate=cost(1000, 1000),
@@ -236,27 +239,29 @@
     heads, tokens, width = q_buf.shape
     group = width // HEAD_SIZE
     sources = (k0_hbm, k1_hbm, v0_hbm, v1_hbm)
-
-    def copies(h):
-        narrow = head_columns(h)
-        found = [
-            pltpu.make_async_copy(ref.at[:, narrow], kv_buf.at[i, h], sems.at[i, h]) for i, ref in enumerate(sources)
-        ]
-        found.append(pltpu.make_async_copy(q_hbm.at[:, head_columns(h, width)], q_buf.at[h], sems.at[len(sources), h]))
-        return found
-
-    for h in range(heads):
-        for copy in copies(h):
-            copy.start()
+    whole = [pltpu.make_async_copy(ref, kv_buf.at[i], sems.at[i]) for i, ref in enumerate(sources)]
+
+    def q_copy(h):
+        return pltpu.make_async_copy(q_hbm.at[:, head_columns(h, width)], q_buf.at[h], sems.at[len(sources) + h])
+
+    whole[0].start()
+    whole[1].start()
+    q_copy(0).start()
+    whole[2].start()
+    whole[3].start()
+    for h in range(1, heads):
+        q_copy(h).start()
     bias = jnp.where(pos_ref[0] >= 1, 0.0, MASKED).astype(jnp.float32)
     row = lax.broadcasted_iota(jnp.int32, (tokens, tokens), 0)
     column = lax.broadcasted_iota(jnp.int32, (tokens, tokens), 1)
     own = jnp.concatenate([column <= row] * group, axis=0)
 
+    for copy in whole:
+        copy.wait()
+
     def one_head(h, carried):
-        for copy in copies(h):
-            copy.wait()
-        k0, k1, v0, v1 = [kv_buf[i, h] for i in range(len(sources))]
+        q_copy(h).wait()
+        k0, k1, v0, v1 = [kv_buf[i, :, head_columns(h)] for i in range(len(sources))]
         q = jnp.concatenate([q_buf[h, :, g * HEAD_SIZE : (g + 1) * HEAD_SIZE] for g in range(group)], axis=0)
         outer = jnp.where(own, dot(q, k0, NT), MASKED)
         inner = dot(q, k1, NT) + bias
@@ -288,8 +293,8 @@
         out_shape=[jax.ShapeDtypeStruct((tokens, columns), jnp.float32)] * 3,
         scratch_shapes=[
             pltpu.VMEM((heads, tokens, width), jnp.bfloat16),
-            pltpu.VMEM((4, heads, tokens, HEAD_SIZE), jnp.bfloat16),
-            pltpu.SemaphoreType.DMA((5, heads)),
+            pltpu.VMEM((4,) + values[0].shape, jnp.bfloat16),
+            pltpu.SemaphoreType.DMA((4 + heads,)),
         ],
         compiler_params=params(),
         cost_estimate=cost(4 * pairs * HEAD_SIZE, 8 * tokens * columns, pairs),
@@ -300,26 +305,26 @@
     heads, tokens, width = q_buf.shape
     group = width // HEAD_SIZE
 
-    def copies(h):
-        return [
-            pltpu.make_async_copy(k2_hbm.at[:, head_columns(h)], k_buf.at[h], sems.at[0, h]),
-            pltpu.make_async_copy(q_hbm.at[:, head_columns(h, width)], q_buf.at[h], sems.at[1, h]),
-        ]
-
+    k_copy = pltpu.make_async_copy(k2_hbm, k_buf, sems.at[heads])
+
+    def q_copy(h):
+        return pltpu.make_async_copy(q_hbm.at[:, head_columns(h, width)], q_buf.at[h], sems.at[h])
+
+    k_copy.start()
     for h in range(heads):
-        for copy in copies(h):
-            copy.start()
+        q_copy(h).start()
     row = lax.broadcasted_iota(jnp.int32, (tokens, tokens), 0)
     column = lax.broadcasted_iota(jnp.int32, (tokens, tokens), 1)
     seen = jnp.concatenate([(column > row) & (pos_ref[0] >= 2)] * group, axis=0)
     ones = jnp.ones((tokens, HEAD_SIZE), jnp.bfloat16)
 
+    k_copy.wait()
+
     def one_head(h, carried):
-        for copy in copies(h):
-            copy.wait()
+        q_copy(h).wait()
         ats = [head_columns(h * group + g) for g in range(group)]
         q = jnp.concatenate([q_buf[h, :, g * HEAD_SIZE : (g + 1) * HEAD_SIZE] for g in range(group)], axis=0)
-        scores = jnp.where(seen, dot(q, k_buf[h], NT), MASKED)
+        scores = jnp.where(seen, dot(q, k_buf[:, head_columns(h)], NT), MASKED)
         before = jnp.concatenate([max_in[:, at] for at in ats], axis=0)
         highest = jnp.maximum(before, jnp.max(scores, axis=1, keepdims=True))
         spread = jnp.concatenate([highest] * (tokens // HEAD_SIZE), axis=1)
@@ -353,8 +358,8 @@
         ],
         scratch_shapes=[
             pltpu.VMEM((heads, tokens, width), jnp.bfloat16),
-            pltpu.VMEM((heads, tokens, HEAD_SIZE), jnp.bfloat16),
-            pltpu.SemaphoreType.DMA((2, heads)),
+            pltpu.VMEM(keys.shape, jnp.bfloat16),
+            pltpu.SemaphoreType.DMA((heads + 1,)),
         ],
         compiler_params=params(),
         cost_estimate=cost(4 * pairs * HEAD_SIZE, 12 * tokens * columns, pairs),

time: 55.9 us -> 55.4 us (level)
  Pallas kernels: 18.5 us -> 17.8 us
    pallas_call x1, Pallas kernels: 2.51 us -> 1.94 us  [pool(): pl.pallas_call(pool_kernel, in_specs=[SMEM] + [ANY] * 6, out_specs=[VMEM]...]
where the time goes in v4:
time: 55.4 us; the launch traced here: 55.1 us
  waiting for transfers between devices  20.3 us (37%)
  Pallas kernels  17.8 us (32%)
  starting transfers between devices  16.8 us (30%)
    ppermute x10, starting transfers between devices, exchanged(): lax.ppermute(value, axis, [(source, source ^ offset) for source in range(...  11.2 us
    ppermute x10, waiting for transfers between devices, exchanged(): lax.ppermute(value, axis, [(source, source ^ offset) for source in range(...  11.2 us
    ppermute x4, waiting for transfers between devices, in_ring(): lax.ppermute(value, axis, [(source, (source + 1) % count) for source in r...  9.11 us
    pallas_call x1, Pallas kernels, near_attention(): pl.pallas_call(near_kernel, in_specs=[SMEM] + [ANY] * 5, out_specs=[VMEM]...  5.96 us
    ppermute x4, starting transfers between devices, in_ring(): lax.ppermute(value, axis, [(source, (source + 1) % count) for source in r...  5.63 us
    pallas_call x1, Pallas kernels, far_attention(): pl.pallas_call(far_kernel, in_specs=[SMEM, ANY, ANY] + [VMEM] * 3, out_sp...  3.97 us
    pallas_call x1, Pallas kernels, join(): pl.pallas_call(join_kernel, in_specs=[SMEM, VMEM, VMEM, ANY, ANY] + [VMEM...  2.43 us
    pallas_call x1, Pallas kernels, coarse_attention(): pl.pallas_call(functools.partial(coarse_kernel, sections, seq_count), in_...  2.39 us
  transfers between devices with their start and end apart: 14, of which 9 were waited for; matrix products, arithmetic and copies ran while one was open for 0% of the time, Pallas kernels for 22%

profile of v4, /device:TPU:0, one launch (start us, length us, event | category | flops | bytes accessed | tf_op | source)
XLA Modules:
  0.0 55.1 jit_solution(9881660136065119897)
XLA Ops:
  0.0 1.9 %shard_map.82 = (bf16[64,768]{1,0:T(8,128)(2,1)S(1)}, bf16[64,768]{1,0:T(8,128)(2,1)S(1)}, bf16[64,768]{1,0:T(8,128)(2,1)S(1)}, bf16[64,768]{1,0:T(8,128)(2,1)S(1)}) custom-call(s32[1]{0:T(128)} %bitcast.my_ref, bf16[256,2048]{1,0:T(8,128)(2,1)} %q_hbm.5, bf16[256,512]{1,0:T(8,128)(2,1)} %k0_hbm.1, bf16[256,512]{1,0:T(8,128)(2,1)} %v0_hbm.1, ...), custom_call_target="tpu_custom_call" | custom-call | flops 1000 | bytes 1000 | tf_op jit(solution)/shard_map/pallas_call | solution.py:106
  1.9 3.0 %collective-permute-start = (bf16[64,768]{1,0:T(8,128)(2,1)S(1)}, bf16[64,768]{1,0:T(8,128)(2,1)S(1)}, u32[]{:S(2)}, u32[]{:S(2)}) collective-permute-start(bf16[64,768]{1,0:T(8,128)(2,1)S(1)} %get-tuple-element.33), channel_id=1, source_target_pairs={{0,8},{8,0},{16,24},{24,16},{1,9},{9,1},{17,25},{25,17},{2,10},{10... | collective-permute-start | bytes 294920 | tf_op jit(solution)/shard_map/pooled_to_heads1/ppermute | solution.py:53
  5.0 1.5 %collective-permute-start.1 = (bf16[64,768]{1,0:T(8,128)(2,1)S(1)}, bf16[64,768]{1,0:T(8,128)(2,1)S(1)}, u32[]{:S(2)}, u32[]{:S(2)}) collective-permute-start(bf16[64,768]{1,0:T(8,128)(2,1)S(1)} %get-tuple-element.34), channel_id=1, source_target_pairs={{0,16},{8,24},{16,0},{24,8},{1,17},{9,25},{17,1},{25,9},{2,18},{10... | collective-permute-start | bytes 294920 | tf_op jit(solution)/shard_map/pooled_to_heads2/ppermute | solution.py:53
  6.5 0.0 collective-permute-start.2
  6.5 2.0 %collective-permute-start.5 = (bf16[256,512]{1,0:T(8,128)(2,1)}, bf16[256,512]{1,0:T(8,128)(2,1)S(1)}, u32[]{:S(2)}, u32[]{:S(2)}) collective-permute-start(bf16[256,512]{1,0:T(8,128)(2,1)} %k0_hbm.1), channel_id=1, source_target_pairs={{0,2},{2,4},{4,6},{6,8},{8,10},{10,12},{12,14},{14,16},{16,18},{18... | collective-permute-start | bytes 786440 | tf_op jit(solution)/shard_map/first_keys/ppermute | solution.py:47
  8.5 2.1 %collective-permute-done.1.refs_2_ = bf16[64,768]{1,0:T(8,128)(2,1)S(1)} collective-permute-done((bf16[64,768]{1,0:T(8,128)(2,1)S(1)}, bf16[64,768]{1,0:T(8,128)(2,1)S(1)}, u32[]{:S(2)}, u32[]{:S(2)}) %collective-permute-start.1) | collective-permute-done | bytes 98336 | tf_op jit(solution)/shard_map/pooled_to_heads2/ppermute | solution.py:53
  10.6 1.4 %collective-permute-done.2.refs_3_ = bf16[64,768]{1,0:T(8,128)(2,1)S(1)} collective-permute-done((bf16[64,768]{1,0:T(8,128)(2,1)S(1)}, bf16[64,768]{1,0:T(8,128)(2,1)S(1)}, u32[]{:S(2)}, u32[]{:S(2)}) %collective-permute-start.2) | collective-permute-done | bytes 98336 | tf_op jit(solution)/shard_map/pooled_to_heads3/ppermute | solution.py:53
  12.0 1.6 %collective-permute-start.6 = (bf16[256,512]{1,0:T(8,128)(2,1)}, bf16[256,512]{1,0:T(8,128)(2,1)S(1)}, u32[]{:S(2)}, u32[]{:S(2)}) collective-permute-start(bf16[256,512]{1,0:T(8,128)(2,1)} %v0_hbm.1), channel_id=1, source_target_pairs={{0,2},{2,4},{4,6},{6,8},{8,10},{10,12},{12,14},{14,16},{16,18},{18... | collective-permute-start | bytes 786440 | tf_op jit(solution)/shard_map/first_values/ppermute | solution.py:47
  13.6 1.6 %collective-permute-start.4 = (bf16[272,256]{1,0:T(8,128)(2,1)S(1)}, bf16[272,256]{1,0:T(8,128)(2,1)S(1)}, u32[]{:S(2)}, u32[]{:S(2)}) collective-permute-start(bf16[272,256]{1,0:T(8,128)(2,1)S(1)} %shard_map.83.refs_4_), channel_id=1, source_target_pairs={{0,2},{2,0},{4,6},{6,4},{1,3},{3,1},{5,7},{7,5},{8,10},{10,8},{12,... | collective-permute-start | bytes 417800 | tf_op jit(solution)/shard_map/pooled_near1/ppermute | solution.py:53
  15.2 1.3 %collective-permute-start.3 = (bf16[272,256]{1,0:T(8,128)(2,1)S(1)}, bf16[272,256]{1,0:T(8,128)(2,1)S(1)}, u32[]{:S(2)}, u32[]{:S(2)}) collective-permute-start(bf16[272,256]{1,0:T(8,128)(2,1)S(1)} %shard_map.83.refs_4_), channel_id=1, source_target_pairs={{0,4},{2,6},{4,0},{6,2},{1,5},{3,7},{5,1},{7,3},{8,12},{10,14},{12... | collective-permute-start | bytes 417800 | tf_op jit(solution)/shard_map/pooled_far2/ppermute | solution.py:53
  16.5 3.2 %collective-permute-done.5.k1_hbm = bf16[256,512]{1,0:T(8,128)(2,1)S(1)} collective-permute-done((bf16[256,512]{1,0:T(8,128)(2,1)}, bf16[256,512]{1,0:T(8,128)(2,1)S(1)}, u32[]{:S(2)}, u32[]{:S(2)}) %collective-permute-start.5) | collective-permute-done | bytes 262176 | tf_op jit(solution)/shard_map/first_keys/ppermute | solution.py:47
  19.7 5.6 %collective-permute-done.6.v1_hbm = bf16[256,512]{1,0:T(8,128)(2,1)S(1)} collective-permute-done((bf16[256,512]{1,0:T(8,128)(2,1)}, bf16[256,512]{1,0:T(8,128)(2,1)S(1)}, u32[]{:S(2)}, u32[]{:S(2)}) %collective-permute-start.6) | collective-permute-done | bytes 262176 | tf_op jit(solution)/shard_map/first_values/ppermute | solution.py:47
  25.3 6.0 %shard_map.84 = (f32[256,2048]{1,0:T(8,128)S(1)}, f32[256,2048]{1,0:T(8,128)S(1)}, f32[256,2048]{1,0:T(8,128)S(1)}) custom-call(s32[1]{0:T(128)} %bitcast.1.pos_ref, bf16[256,2048]{1,0:T(8,128)(2,1)} %q_hbm.5, bf16[256,512]{1,0:T(8,128)(2,1)} %k0_hbm.1, bf16[256,512]{1,0:T(8,128)(2,1)S(1)} %collective-permute-done.5.k1_hbm, bf16[256,512]{1,0:T(8,128)(2,1)} %v0_hbm.1, ...), custom_call_target="tpu_custom_call" | custom-call | flops 1073741824 | bytes 4194304 | tf_op jit(solution)/shard_map/pallas_call | solution.py:289
  31.3 0.0 collective-permute-done.4.refs_5_
  31.3 0.1 collective-permute-start.8
  31.4 2.0 %collective-permute-start.7 = (bf16[256,512]{1,0:T(8,128)(2,1)S(1)}, bf16[256,512]{1,0:T(8,128)(2,1)S(1)}, u32[]{:S(2)}, u32[]{:S(2)}) collective-permute-start(bf16[256,512]{1,0:T(8,128)(2,1)S(1)} %collective-permute-done.5.k1_hbm), channel_id=1, source_target_pairs={{0,2},{2,4},{4,6},{6,8},{8,10},{10,12},{12,14},{14,16},{16,18},{18... | collective-permute-start | bytes 786440 | tf_op jit(solution)/shard_map/second_keys/ppermute | solution.py:47
  33.4 5.2 %collective-permute-done.8.refs_7_ = bf16[272,256]{1,0:T(8,128)(2,1)S(1)} collective-permute-done((bf16[272,256]{1,0:T(8,128)(2,1)S(1)}, bf16[272,256]{1,0:T(8,128)(2,1)S(1)}, u32[]{:S(2)}, u32[]{:S(2)}) %collective-permute-start.8) | collective-permute-done | bytes 139296 | tf_op jit(solution)/shard_map/pooled_farther1/ppermute | solution.py:53
  38.6 0.0 collective-permute-start.9
  38.6 0.1 pad_add_fusion.place_ref
  38.7 2.4 %shard_map.86 = (bf16[64,512]{1,0:T(8,128)(2,1)S(1)}, bf16[64,512]{1,0:T(8,128)(2,1)S(1)}, bf16[64,512]{1,0:T(8,128)(2,1)S(1)}, bf16[64,512]{1,0:T(8,128)(2,1)S(1)}) custom-call(s32[2]{0:T(128)S(1)} %pad_add_fusion.place_ref, bf16[64,768]{1,0:T(8,128)(2,1)S(1)} %get-tuple-element.36.refs_0_, bf16[64,768]{1,0:T(8,128)(2,1)S(1)} %collective-permute-done.refs_1_, ...), custom_call_target="tpu_custom_call" | custom-call | flops 536870912 | bytes 1048576 | tf_op jit(solution)/shard_map/pallas_call | solution.py:222
  41.1 0.8 %collective-permute-start.10 = (bf16[64,512]{1,0:T(8,128)(2,1)S(1)}, bf16[64,512]{1,0:T(8,128)(2,1)S(1)}, u32[]{:S(2)}, u32[]{:S(2)}) collective-permute-start(bf16[64,512]{1,0:T(8,128)(2,1)S(1)} %get-tuple-element.54), channel_id=1, source_target_pairs={{0,8},{8,0},{16,24},{24,16},{1,9},{9,1},{17,25},{25,17},{2,10},{10... | collective-permute-start | bytes 196616 | tf_op jit(solution)/shard_map/coarse_back1/ppermute | solution.py:53
  41.8 1.4 %collective-permute-start.11 = (bf16[64,512]{1,0:T(8,128)(2,1)S(1)}, bf16[64,512]{1,0:T(8,128)(2,1)S(1)}, u32[]{:S(2)}, u32[]{:S(2)}) collective-permute-start(bf16[64,512]{1,0:T(8,128)(2,1)S(1)} %get-tuple-element.55), channel_id=1, source_target_pairs={{0,16},{8,24},{16,0},{24,8},{1,17},{9,25},{17,1},{25,9},{2,18},{10... | collective-permute-start | bytes 196616 | tf_op jit(solution)/shard_map/coarse_back2/ppermute | solution.py:53
  43.2 1.4 %collective-permute-start.12 = (bf16[64,512]{1,0:T(8,128)(2,1)S(1)}, bf16[64,512]{1,0:T(8,128)(2,1)S(1)}, u32[]{:S(2)}, u32[]{:S(2)}) collective-permute-start(bf16[64,512]{1,0:T(8,128)(2,1)S(1)} %get-tuple-element.56), channel_id=1, source_target_pairs={{0,24},{8,16},{16,8},{24,0},{1,25},{9,17},{17,9},{25,1},{2,26},{10... | collective-permute-start | bytes 196616 | tf_op jit(solution)/shard_map/coarse_back3/ppermute | solution.py:53
  44.6 0.4 collective-permute-done.7.k2_hbm
  45.0 4.0 %shard_map.85 = (f32[256,2048]{1,0:T(8,128)S(1)}, bf16[256,4096]{1,0:T(8,128)(2,1)S(1)}) custom-call(s32[1]{0:T(128)} %bitcast.1.pos_ref, bf16[256,2048]{1,0:T(8,128)(2,1)} %q_hbm.5, bf16[256,512]{1,0:T(8,128)(2,1)S(1)} %collective-permute-done.7.k2_hbm, f32[256,2048]{1,0:T(8,128)S(1)} %get-tuple-element.44.acc_in, ...), custom_call_target="tpu_custom_call" | custom-call | flops 536870912 | bytes 6291456 | tf_op jit(solution)/shard_map/pallas_call | solution.py:351
  48.9 0.2 collective-permute-done.10.refs_1_
  49.1 1.0 %collective-permute-done.11.refs_2_ = bf16[64,512]{1,0:T(8,128)(2,1)S(1)} collective-permute-done((bf16[64,512]{1,0:T(8,128)(2,1)S(1)}, bf16[64,512]{1,0:T(8,128)(2,1)S(1)}, u32[]{:S(2)}, u32[]{:S(2)}) %collective-permute-start.11) | collective-permute-done | bytes 65568 | tf_op jit(solution)/shard_map/coarse_back2/ppermute | solution.py:53
  50.1 0.0 collective-permute-done.9.v2_hbm
  50.1 2.4 %shard_map.87 = (f32[256,2048]{1,0:T(8,128)S(1)}, f32[256,128]{1,0:T(8,128)S(1)}) custom-call(s32[1]{0:T(128)} %bitcast.my_ref, f32[256,2048]{1,0:T(8,128)S(1)} %get-tuple-element.47.acc_ref, bf16[256,4096]{1,0:T(8,128)(2,1)S(1)} %get-tuple-element.48.last_ref, bf16[256,512]{1,0:T(8,128)(2,1)S(1)} %collective-permute-done.9.v2_hbm, f32[4,2048]{1,0:T(4,128)} %up_hbm.1, ...), custom_call_target="tpu_custom_call" | custom-call | flops 268435456 | bytes 6291456 | tf_op jit(solution)/shard_map/pallas_call | solution.py:414
  52.6 0.1 collective-permute-start.13
  52.7 1.3 %collective-permute-done.13.other_ref = f32[256,128]{1,0:T(8,128)S(1)} collective-permute-done((f32[256,128]{1,0:T(8,128)S(1)}, f32[256,128]{1,0:T(8,128)S(1)}, u32[]{:S(2)}, u32[]{:S(2)}) %collective-permute-start.13) | collective-permute-done | bytes 131104 | tf_op jit(solution)/shard_map/squares1/ppermute | solution.py:53
  54.0 1.1 %shard_map.88 = bf16[256,2048]{1,0:T(8,128)(2,1)} custom-call(f32[256,2048]{1,0:T(8,128)S(1)} %get-tuple-element.57.comb_ref, f32[256,128]{1,0:T(8,128)S(1)} %get-tuple-element.58.mine_ref, f32[256,128]{1,0:T(8,128)S(1)} %collective-permute-done.13.other_ref, f32[1,2048]{1,0:T(1,128)S(1)} %bitcast.4), custom_call_target="tpu_custom_call" | custom-call | flops 1572864 | bytes 3145728 | tf_op jit(solution)/shard_map/pallas_call | solution.py:449
  (6 shorter events, 0.0 us)
Async XLA Ops:
  1.9 6.6 %collective-permute-start = (bf16[64,768]{1,0:T(8,128)(2,1)S(1)}, bf16[64,768]{1,0:T(8,128)(2,1)S(1)}, u32[]{:S(2)}, u32[]{:S(2)}) collective-permute-start(bf16[64,768]{1,0:T(8,128)(2,1)S(1)} %get-tuple-element.33), channel_id=1, source_target_pairs={{0,8},{8,0},{16,24},{24,16},{1,9},{9,1},{17,25},{25,17},{2,10},{10... | collective-permute-start | bytes 294920 | tf_op jit(solution)/shard_map/pooled_to_heads1/ppermute | solution.py:53
  5.0 5.7 %collective-permute-start.1 = (bf16[64,768]{1,0:T(8,128)(2,1)S(1)}, bf16[64,768]{1,0:T(8,128)(2,1)S(1)}, u32[]{:S(2)}, u32[]{:S(2)}) collective-permute-start(bf16[64,768]{1,0:T(8,128)(2,1)S(1)} %get-tuple-element.34), channel_id=1, source_target_pairs={{0,16},{8,24},{16,0},{24,8},{1,17},{9,25},{17,1},{25,9},{2,18},{10... | collective-permute-start | bytes 294920 | tf_op jit(solution)/shard_map/pooled_to_heads2/ppermute | solution.py:53
  6.5 5.5 %collective-permute-start.2 = (bf16[64,768]{1,0:T(8,128)(2,1)S(1)}, bf16[64,768]{1,0:T(8,128)(2,1)S(1)}, u32[]{:S(2)}, u32[]{:S(2)}) collective-permute-start(bf16[64,768]{1,0:T(8,128)(2,1)S(1)} %get-tuple-element.35), channel_id=1, source_target_pairs={{0,24},{8,16},{16,8},{24,0},{1,25},{9,17},{17,9},{25,1},{2,26},{10... | collective-permute-start | bytes 294920 | tf_op jit(solution)/shard_map/pooled_to_heads3/ppermute | solution.py:53
  6.5 13.2 %collective-permute-start.5 = (bf16[256,512]{1,0:T(8,128)(2,1)}, bf16[256,512]{1,0:T(8,128)(2,1)S(1)}, u32[]{:S(2)}, u32[]{:S(2)}) collective-permute-start(bf16[256,512]{1,0:T(8,128)(2,1)} %k0_hbm.1), channel_id=1, source_target_pairs={{0,2},{2,4},{4,6},{6,8},{8,10},{10,12},{12,14},{14,16},{16,18},{18... | collective-permute-start | bytes 786440 | tf_op jit(solution)/shard_map/first_keys/ppermute | solution.py:47
  12.0 13.3 %collective-permute-start.6 = (bf16[256,512]{1,0:T(8,128)(2,1)}, bf16[256,512]{1,0:T(8,128)(2,1)S(1)}, u32[]{:S(2)}, u32[]{:S(2)}) collective-permute-start(bf16[256,512]{1,0:T(8,128)(2,1)} %v0_hbm.1), channel_id=1, source_target_pairs={{0,2},{2,4},{4,6},{6,8},{8,10},{10,12},{12,14},{14,16},{16,18},{18... | collective-permute-start | bytes 786440 | tf_op jit(solution)/shard_map/first_values/ppermute | solution.py:47
  13.6 17.7 %collective-permute-start.4 = (bf16[272,256]{1,0:T(8,128)(2,1)S(1)}, bf16[272,256]{1,0:T(8,128)(2,1)S(1)}, u32[]{:S(2)}, u32[]{:S(2)}) collective-permute-start(bf16[272,256]{1,0:T(8,128)(2,1)S(1)} %shard_map.83.refs_4_), channel_id=1, source_target_pairs={{0,2},{2,0},{4,6},{6,4},{1,3},{3,1},{5,7},{7,5},{8,10},{10,8},{12,... | collective-permute-start | bytes 417800 | tf_op jit(solution)/shard_map/pooled_near1/ppermute | solution.py:53
  15.2 16.0 %collective-permute-start.3 = (bf16[272,256]{1,0:T(8,128)(2,1)S(1)}, bf16[272,256]{1,0:T(8,128)(2,1)S(1)}, u32[]{:S(2)}, u32[]{:S(2)}) collective-permute-start(bf16[272,256]{1,0:T(8,128)(2,1)S(1)} %shard_map.83.refs_4_), channel_id=1, source_target_pairs={{0,4},{2,6},{4,0},{6,2},{1,5},{3,7},{5,1},{7,3},{8,12},{10,14},{12... | collective-permute-start | bytes 417800 | tf_op jit(solution)/shard_map/pooled_far2/ppermute | solution.py:53
  31.3 7.3 %collective-permute-start.8 = (bf16[272,256]{1,0:T(8,128)(2,1)S(1)}, bf16[272,256]{1,0:T(8,128)(2,1)S(1)}, u32[]{:S(2)}, u32[]{:S(2)}) collective-permute-start(bf16[272,256]{1,0:T(8,128)(2,1)S(1)} %collective-permute-done.3.refs_6_), channel_id=1, source_target_pairs={{0,2},{2,0},{4,6},{6,4},{1,3},{3,1},{5,7},{7,5},{8,10},{10,8},{12,... | collective-permute-start | bytes 417800 | tf_op jit(solution)/shard_map/pooled_farther1/ppermute | solution.py:53
  31.4 13.6 %collective-permute-start.7 = (bf16[256,512]{1,0:T(8,128)(2,1)S(1)}, bf16[256,512]{1,0:T(8,128)(2,1)S(1)}, u32[]{:S(2)}, u32[]{:S(2)}) collective-permute-start(bf16[256,512]{1,0:T(8,128)(2,1)S(1)} %collective-permute-done.5.k1_hbm), channel_id=1, source_target_pairs={{0,2},{2,4},{4,6},{6,8},{8,10},{10,12},{12,14},{14,16},{16,18},{18... | collective-permute-start | bytes 786440 | tf_op jit(solution)/shard_map/second_keys/ppermute | solution.py:47
  38.6 11.6 %collective-permute-start.9 = (bf16[256,512]{1,0:T(8,128)(2,1)S(1)}, bf16[256,512]{1,0:T(8,128)(2,1)S(1)}, u32[]{:S(2)}, u32[]{:S(2)}) collective-permute-start(bf16[256,512]{1,0:T(8,128)(2,1)S(1)} %collective-permute-done.6.v1_hbm), channel_id=1, source_target_pairs={{0,2},{2,4},{4,6},{6,8},{8,10},{10,12},{12,14},{14,16},{16,18},{18... | collective-permute-start | bytes 786440 | tf_op jit(solution)/shard_map/second_values/ppermute | solution.py:47
  41.1 8.1 %collective-permute-start.10 = (bf16[64,512]{1,0:T(8,128)(2,1)S(1)}, bf16[64,512]{1,0:T(8,128)(2,1)S(1)}, u32[]{:S(2)}, u32[]{:S(2)}) collective-permute-start(bf16[64,512]{1,0:T(8,128)(2,1)S(1)} %get-tuple-element.54), channel_id=1, source_target_pairs={{0,8},{8,0},{16,24},{24,16},{1,9},{9,1},{17,25},{25,17},{2,10},{10... | collective-permute-start | bytes 196616 | tf_op jit(solution)/shard_map/coarse_back1/ppermute | solution.py:53
  41.8 8.3 %collective-permute-start.11 = (bf16[64,512]{1,0:T(8,128)(2,1)S(1)}, bf16[64,512]{1,0:T(8,128)(2,1)S(1)}, u32[]{:S(2)}, u32[]{:S(2)}) collective-permute-start(bf16[64,512]{1,0:T(8,128)(2,1)S(1)} %get-tuple-element.55), channel_id=1, source_target_pairs={{0,16},{8,24},{16,0},{24,8},{1,17},{9,25},{17,1},{25,9},{2,18},{10... | collective-permute-start | bytes 196616 | tf_op jit(solution)/shard_map/coarse_back2/ppermute | solution.py:53
  43.2 6.9 %collective-permute-start.12 = (bf16[64,512]{1,0:T(8,128)(2,1)S(1)}, bf16[64,512]{1,0:T(8,128)(2,1)S(1)}, u32[]{:S(2)}, u32[]{:S(2)}) collective-permute-start(bf16[64,512]{1,0:T(8,128)(2,1)S(1)} %get-tuple-element.56), channel_id=1, source_target_pairs={{0,24},{8,16},{16,8},{24,0},{1,25},{9,17},{17,9},{25,1},{2,26},{10... | collective-permute-start | bytes 196616 | tf_op jit(solution)/shard_map/coarse_back3/ppermute | solution.py:53
  50.1 3.9 %copy-start = (f32[2048]{0:T(1024)S(1)}, f32[2048]{0:T(1024)}, u32[]{:S(2)}) copy-start(f32[2048]{0:T(1024)} %param.15) | copy-start | bytes 24580
  52.6 1.4 %collective-permute-start.13 = (f32[256,128]{1,0:T(8,128)S(1)}, f32[256,128]{1,0:T(8,128)S(1)}, u32[]{:S(2)}, u32[]{:S(2)}) collective-permute-start(f32[256,128]{1,0:T(8,128)S(1)} %get-tuple-element.58.mine_ref), channel_id=1, source_target_pairs={{0,1},{1,0},{2,3},{3,2},{4,5},{5,4},{6,7},{7,6},{8,9},{9,8},{10,11... | collective-permute-start | bytes 393224 | tf_op jit(solution)/shard_map/squares1/ppermute | solution.py:53

commit v5 on v4

--- a/solution.py
+++ b/solution.py
@@ -38,6 +38,8 @@
 
 
 def head_columns(h, width=HEAD_SIZE):
+    if isinstance(h, int):
+        return slice(h * width, (h + 1) * width)
     return pl.ds(pl.multiple_of(h * width, width), width)
 
 
@@ -259,26 +261,32 @@
     for copy in whole:
         copy.wait()
 
-    def one_head(h, carried):
+    def scores_of(h):
         q_copy(h).wait()
-        k0, k1, v0, v1 = [kv_buf[i, :, head_columns(h)] for i in range(len(sources))]
         q = jnp.concatenate([q_buf[h, :, g * HEAD_SIZE : (g + 1) * HEAD_SIZE] for g in range(group)], axis=0)
-        outer = jnp.where(own, dot(q, k0, NT), MASKED)
-        inner = dot(q, k1, NT) + bias
+        narrow = slice(h * HEAD_SIZE, (h + 1) * HEAD_SIZE)
+        return dot(q, kv_buf[0, :, narrow], NT), dot(q, kv_buf[1, :, narrow], NT)
+
+    scores = scores_of(0)
+    for h in range(heads):
+        outer, inner = scores
+        if h + 1 < heads:
+            scores = scores_of(h + 1)
+        outer = jnp.where(own, outer, MASKED)
+        inner = inner + bias
         highest = jnp.max(jnp.maximum(outer, inner), axis=1, keepdims=True)
         outer = jnp.exp2((outer - highest) * EXP2_SCALE).astype(jnp.bfloat16)
         inner = jnp.exp2((inner - highest) * EXP2_SCALE).astype(jnp.bfloat16)
+        narrow = slice(h * HEAD_SIZE, (h + 1) * HEAD_SIZE)
+        v0, v1 = kv_buf[2, :, narrow], kv_buf[3, :, narrow]
         total = dot(outer, with_ones(v0), NN) + dot(inner, with_ones(v1), NN)
         highest = jnp.broadcast_to(highest, (group * tokens, HEAD_SIZE))
         for g in range(group):
             here = slice(g * tokens, (g + 1) * tokens)
-            at = head_columns(h * group + g)
+            at = slice((h * group + g) * HEAD_SIZE, (h * group + g + 1) * HEAD_SIZE)
             acc_ref[:, at] = total[here, :HEAD_SIZE]
             sum_ref[:, at] = total[here, HEAD_SIZE:]
             max_ref[:, at] = highest[here]
-        return carried
-
-    lax.fori_loop(0, heads, one_head, 0)
 
 
 def near_attention(position, queries, keys, values):
@@ -404,7 +412,9 @@
             squares = squares + combined * combined
         return squares
 
-    squares = lax.fori_loop(0, heads, one_head, jnp.zeros((tokens, HEAD_SIZE), jnp.float32))
+    squares = jnp.zeros((tokens, HEAD_SIZE), jnp.float32)
+    for h in range(heads):
+        squares = one_head(h, squares)
     sq_ref[...] = jnp.broadcast_to(jnp.sum(squares, axis=1, keepdims=True), sq_ref.shape)
 
 

time: 55.4 us -> 54.9 us (level)
  Pallas kernels: 17.8 us -> 17 us
where the time goes in v5:
time: 54.9 us; the launch traced here: 54.6 us
  waiting for transfers between devices  20.6 us (38%)
  Pallas kernels  17 us (31%)
  starting transfers between devices  16.8 us (31%)
    ppermute x10, starting transfers between devices, exchanged(): lax.ppermute(value, axis, [(source, source ^ offset) for source in range(...  11.2 us
    ppermute x10, waiting for transfers between devices, exchanged(): lax.ppermute(value, axis, [(source, source ^ offset) for source in range(...  11.2 us
    ppermute x4, waiting for transfers between devices, in_ring(): lax.ppermute(value, axis, [(source, (source + 1) % count) for source in r...  9.48 us
    pallas_call x1, Pallas kernels, near_attention(): pl.pallas_call(near_kernel, in_specs=[SMEM] + [ANY] * 5, out_specs=[VMEM]...  5.64 us
    ppermute x4, starting transfers between devices, in_ring(): lax.ppermute(value, axis, [(source, (source + 1) % count) for source in r...  5.63 us
    pallas_call x1, Pallas kernels, far_attention(): pl.pallas_call(far_kernel, in_specs=[SMEM, ANY, ANY] + [VMEM] * 3, out_sp...  3.97 us
    pallas_call x1, Pallas kernels, coarse_attention(): pl.pallas_call(functools.partial(coarse_kernel, sections, seq_count), in_...  2.39 us
    pallas_call x1, Pallas kernels, pool(): pl.pallas_call(pool_kernel, in_specs=[SMEM] + [ANY] * 6, out_specs=[VMEM]...  1.94 us
  transfers between devices with their start and end apart: 14, of which 9 were waited for; matrix products, arithmetic and copies ran while one was open for 0% of the time, Pallas kernels for 22%

profile of v5, /device:TPU:0, one launch (start us, length us, event | category | flops | bytes accessed | tf_op | source)
XLA Modules:
  0.0 54.6 jit_solution(762355758389604058)
XLA Ops:
  0.0 1.9 %shard_map.82 = (bf16[64,768]{1,0:T(8,128)(2,1)S(1)}, bf16[64,768]{1,0:T(8,128)(2,1)S(1)}, bf16[64,768]{1,0:T(8,128)(2,1)S(1)}, bf16[64,768]{1,0:T(8,128)(2,1)S(1)}) custom-call(s32[1]{0:T(128)} %bitcast.my_ref, bf16[256,2048]{1,0:T(8,128)(2,1)} %q_hbm.5, bf16[256,512]{1,0:T(8,128)(2,1)} %k0_hbm.1, bf16[256,512]{1,0:T(8,128)(2,1)} %v0_hbm.1, ...), custom_call_target="tpu_custom_call" | custom-call | flops 1000 | bytes 1000 | tf_op jit(solution)/shard_map/pallas_call | solution.py:108
  1.9 3.0 %collective-permute-start = (bf16[64,768]{1,0:T(8,128)(2,1)S(1)}, bf16[64,768]{1,0:T(8,128)(2,1)S(1)}, u32[]{:S(2)}, u32[]{:S(2)}) collective-permute-start(bf16[64,768]{1,0:T(8,128)(2,1)S(1)} %get-tuple-element.33), channel_id=1, source_target_pairs={{0,8},{8,0},{16,24},{24,16},{1,9},{9,1},{17,25},{25,17},{2,10},{10... | collective-permute-start | bytes 294920 | tf_op jit(solution)/shard_map/pooled_to_heads1/ppermute | solution.py:55
  5.0 1.5 %collective-permute-start.1 = (bf16[64,768]{1,0:T(8,128)(2,1)S(1)}, bf16[64,768]{1,0:T(8,128)(2,1)S(1)}, u32[]{:S(2)}, u32[]{:S(2)}) collective-permute-start(bf16[64,768]{1,0:T(8,128)(2,1)S(1)} %get-tuple-element.34), channel_id=1, source_target_pairs={{0,16},{8,24},{16,0},{24,8},{1,17},{9,25},{17,1},{25,9},{2,18},{10... | collective-permute-start | bytes 294920 | tf_op jit(solution)/shard_map/pooled_to_heads2/ppermute | solution.py:55
  6.5 0.0 collective-permute-start.2
  6.5 2.0 %collective-permute-start.5 = (bf16[256,512]{1,0:T(8,128)(2,1)}, bf16[256,512]{1,0:T(8,128)(2,1)S(1)}, u32[]{:S(2)}, u32[]{:S(2)}) collective-permute-start(bf16[256,512]{1,0:T(8,128)(2,1)} %k0_hbm.1), channel_id=1, source_target_pairs={{0,2},{2,4},{4,6},{6,8},{8,10},{10,12},{12,14},{14,16},{16,18},{18... | collective-permute-start | bytes 786440 | tf_op jit(solution)/shard_map/first_keys/ppermute | solution.py:49
  8.5 0.0 collective-permute-done.refs_1_
  8.5 2.1 %collective-permute-done.1.refs_2_ = bf16[64,768]{1,0:T(8,128)(2,1)S(1)} collective-permute-done((bf16[64,768]{1,0:T(8,128)(2,1)S(1)}, bf16[64,768]{1,0:T(8,128)(2,1)S(1)}, u32[]{:S(2)}, u32[]{:S(2)}) %collective-permute-start.1) | collective-permute-done | bytes 98336 | tf_op jit(solution)/shard_map/pooled_to_heads2/ppermute | solution.py:55
  10.6 1.4 %collective-permute-done.2.refs_3_ = bf16[64,768]{1,0:T(8,128)(2,1)S(1)} collective-permute-done((bf16[64,768]{1,0:T(8,128)(2,1)S(1)}, bf16[64,768]{1,0:T(8,128)(2,1)S(1)}, u32[]{:S(2)}, u32[]{:S(2)}) %collective-permute-start.2) | collective-permute-done | bytes 98336 | tf_op jit(solution)/shard_map/pooled_to_heads3/ppermute | solution.py:55
  12.0 1.6 %collective-permute-start.6 = (bf16[256,512]{1,0:T(8,128)(2,1)}, bf16[256,512]{1,0:T(8,128)(2,1)S(1)}, u32[]{:S(2)}, u32[]{:S(2)}) collective-permute-start(bf16[256,512]{1,0:T(8,128)(2,1)} %v0_hbm.1), channel_id=1, source_target_pairs={{0,2},{2,4},{4,6},{6,8},{8,10},{10,12},{12,14},{14,16},{16,18},{18... | collective-permute-start | bytes 786440 | tf_op jit(solution)/shard_map/first_values/ppermute | solution.py:49
  13.6 1.6 %collective-permute-start.4 = (bf16[272,256]{1,0:T(8,128)(2,1)S(1)}, bf16[272,256]{1,0:T(8,128)(2,1)S(1)}, u32[]{:S(2)}, u32[]{:S(2)}) collective-permute-start(bf16[272,256]{1,0:T(8,128)(2,1)S(1)} %shard_map.83.refs_4_), channel_id=1, source_target_pairs={{0,2},{2,0},{4,6},{6,4},{1,3},{3,1},{5,7},{7,5},{8,10},{10,8},{12,... | collective-permute-start | bytes 417800 | tf_op jit(solution)/shard_map/pooled_near1/ppermute | solution.py:55
  15.2 1.3 %collective-permute-start.3 = (bf16[272,256]{1,0:T(8,128)(2,1)S(1)}, bf16[272,256]{1,0:T(8,128)(2,1)S(1)}, u32[]{:S(2)}, u32[]{:S(2)}) collective-permute-start(bf16[272,256]{1,0:T(8,128)(2,1)S(1)} %shard_map.83.refs_4_), channel_id=1, source_target_pairs={{0,4},{2,6},{4,0},{6,2},{1,5},{3,7},{5,1},{7,3},{8,12},{10,14},{12... | collective-permute-start | bytes 417800 | tf_op jit(solution)/shard_map/pooled_far2/ppermute | solution.py:55
  16.5 3.2 %collective-permute-done.5.k1_hbm = bf16[256,512]{1,0:T(8,128)(2,1)S(1)} collective-permute-done((bf16[256,512]{1,0:T(8,128)(2,1)}, bf16[256,512]{1,0:T(8,128)(2,1)S(1)}, u32[]{:S(2)}, u32[]{:S(2)}) %collective-permute-start.5) | collective-permute-done | bytes 262176 | tf_op jit(solution)/shard_map/first_keys/ppermute | solution.py:49
  19.7 5.6 %collective-permute-done.6.v1_hbm = bf16[256,512]{1,0:T(8,128)(2,1)S(1)} collective-permute-done((bf16[256,512]{1,0:T(8,128)(2,1)}, bf16[256,512]{1,0:T(8,128)(2,1)S(1)}, u32[]{:S(2)}, u32[]{:S(2)}) %collective-permute-start.6) | collective-permute-done | bytes 262176 | tf_op jit(solution)/shard_map/first_values/ppermute | solution.py:49
  25.3 5.6 %shard_map.84 = (f32[256,2048]{1,0:T(8,128)S(1)}, f32[256,2048]{1,0:T(8,128)S(1)}, f32[256,2048]{1,0:T(8,128)S(1)}) custom-call(s32[1]{0:T(128)} %bitcast.1.pos_ref, bf16[256,2048]{1,0:T(8,128)(2,1)} %q_hbm.5, bf16[256,512]{1,0:T(8,128)(2,1)} %k0_hbm.1, bf16[256,512]{1,0:T(8,128)(2,1)S(1)} %collective-permute-done.5.k1_hbm, bf16[256,512]{1,0:T(8,128)(2,1)} %v0_hbm.1, ...), custom_call_target="tpu_custom_call" | custom-call | flops 1073741824 | bytes 4194304 | tf_op jit(solution)/shard_map/pallas_call | solution.py:297
  30.9 0.0 collective-permute-done.3.refs_6_
  31.0 0.1 collective-permute-start.8
  31.0 2.0 %collective-permute-start.7 = (bf16[256,512]{1,0:T(8,128)(2,1)S(1)}, bf16[256,512]{1,0:T(8,128)(2,1)S(1)}, u32[]{:S(2)}, u32[]{:S(2)}) collective-permute-start(bf16[256,512]{1,0:T(8,128)(2,1)S(1)} %collective-permute-done.5.k1_hbm), channel_id=1, source_target_pairs={{0,2},{2,4},{4,6},{6,8},{8,10},{10,12},{12,14},{14,16},{16,18},{18... | collective-permute-start | bytes 786440 | tf_op jit(solution)/shard_map/second_keys/ppermute | solution.py:49
  33.0 5.2 %collective-permute-done.8.refs_7_ = bf16[272,256]{1,0:T(8,128)(2,1)S(1)} collective-permute-done((bf16[272,256]{1,0:T(8,128)(2,1)S(1)}, bf16[272,256]{1,0:T(8,128)(2,1)S(1)}, u32[]{:S(2)}, u32[]{:S(2)}) %collective-permute-start.8) | collective-permute-done | bytes 139296 | tf_op jit(solution)/shard_map/pooled_farther1/ppermute | solution.py:55
  38.2 0.0 collective-permute-start.9
  38.2 0.1 pad_add_fusion.place_ref
  38.3 2.4 %shard_map.86 = (bf16[64,512]{1,0:T(8,128)(2,1)S(1)}, bf16[64,512]{1,0:T(8,128)(2,1)S(1)}, bf16[64,512]{1,0:T(8,128)(2,1)S(1)}, bf16[64,512]{1,0:T(8,128)(2,1)S(1)}) custom-call(s32[2]{0:T(128)S(1)} %pad_add_fusion.place_ref, bf16[64,768]{1,0:T(8,128)(2,1)S(1)} %get-tuple-element.36.refs_0_, bf16[64,768]{1,0:T(8,128)(2,1)S(1)} %collective-permute-done.refs_1_, ...), custom_call_target="tpu_custom_call" | custom-call | flops 536870912 | bytes 1048576 | tf_op jit(solution)/shard_map/pallas_call | solution.py:224
  40.7 0.1 collective-permute-start.10
  40.8 2.4 %collective-permute-start.11 = (bf16[64,512]{1,0:T(8,128)(2,1)S(1)}, bf16[64,512]{1,0:T(8,128)(2,1)S(1)}, u32[]{:S(2)}, u32[]{:S(2)}) collective-permute-start(bf16[64,512]{1,0:T(8,128)(2,1)S(1)} %get-tuple-element.55), channel_id=1, source_target_pairs={{0,16},{8,24},{16,0},{24,8},{1,17},{9,25},{17,1},{25,9},{2,18},{10... | collective-permute-start | bytes 196616 | tf_op jit(solution)/shard_map/coarse_back2/ppermute | solution.py:55
  43.2 1.0 %collective-permute-start.12 = (bf16[64,512]{1,0:T(8,128)(2,1)S(1)}, bf16[64,512]{1,0:T(8,128)(2,1)S(1)}, u32[]{:S(2)}, u32[]{:S(2)}) collective-permute-start(bf16[64,512]{1,0:T(8,128)(2,1)S(1)} %get-tuple-element.56), channel_id=1, source_target_pairs={{0,24},{8,16},{16,8},{24,0},{1,25},{9,17},{17,9},{25,1},{2,26},{10... | collective-permute-start | bytes 196616 | tf_op jit(solution)/shard_map/coarse_back3/ppermute | solution.py:55
  44.2 0.7 %collective-permute-done.7.k2_hbm = bf16[256,512]{1,0:T(8,128)(2,1)S(1)} collective-permute-done((bf16[256,512]{1,0:T(8,128)(2,1)S(1)}, bf16[256,512]{1,0:T(8,128)(2,1)S(1)}, u32[]{:S(2)}, u32[]{:S(2)}) %collective-permute-start.7) | collective-permute-done | bytes 262176 | tf_op jit(solution)/shard_map/second_keys/ppermute | solution.py:49
  45.0 4.0 %shard_map.85 = (f32[256,2048]{1,0:T(8,128)S(1)}, bf16[256,4096]{1,0:T(8,128)(2,1)S(1)}) custom-call(s32[1]{0:T(128)} %bitcast.1.pos_ref, bf16[256,2048]{1,0:T(8,128)(2,1)} %q_hbm.5, bf16[256,512]{1,0:T(8,128)(2,1)S(1)} %collective-permute-done.7.k2_hbm, f32[256,2048]{1,0:T(8,128)S(1)} %get-tuple-element.44.acc_in, ...), custom_call_target="tpu_custom_call" | custom-call | flops 536870912 | bytes 6291456 | tf_op jit(solution)/shard_map/pallas_call | solution.py:359
  48.9 0.2 collective-permute-done.10.refs_1_
  49.2 1.0 %collective-permute-done.11.refs_2_ = bf16[64,512]{1,0:T(8,128)(2,1)S(1)} collective-permute-done((bf16[64,512]{1,0:T(8,128)(2,1)S(1)}, bf16[64,512]{1,0:T(8,128)(2,1)S(1)}, u32[]{:S(2)}, u32[]{:S(2)}) %collective-permute-start.11) | collective-permute-done | bytes 65568 | tf_op jit(solution)/shard_map/coarse_back2/ppermute | solution.py:55
  50.2 1.9 %shard_map.87 = (f32[256,2048]{1,0:T(8,128)S(1)}, f32[256,128]{1,0:T(8,128)S(1)}) custom-call(s32[1]{0:T(128)} %bitcast.my_ref, f32[256,2048]{1,0:T(8,128)S(1)} %get-tuple-element.47.acc_ref, bf16[256,4096]{1,0:T(8,128)(2,1)S(1)} %get-tuple-element.48.last_ref, bf16[256,512]{1,0:T(8,128)(2,1)S(1)} %collective-permute-done.9.v2_hbm, f32[4,2048]{1,0:T(4,128)} %up_hbm.1, ...), custom_call_target="tpu_custom_call" | custom-call | flops 268435456 | bytes 6291456 | tf_op jit(solution)/shard_map/pallas_call | solution.py:424
  52.1 0.1 collective-permute-start.13
  52.2 1.3 %collective-permute-done.13.other_ref = f32[256,128]{1,0:T(8,128)S(1)} collective-permute-done((f32[256,128]{1,0:T(8,128)S(1)}, f32[256,128]{1,0:T(8,128)S(1)}, u32[]{:S(2)}, u32[]{:S(2)}) %collective-permute-start.13) | collective-permute-done | bytes 131104 | tf_op jit(solution)/shard_map/squares1/ppermute | solution.py:55
  53.5 1.1 %shard_map.88 = bf16[256,2048]{1,0:T(8,128)(2,1)} custom-call(f32[256,2048]{1,0:T(8,128)S(1)} %get-tuple-element.57.comb_ref, f32[256,128]{1,0:T(8,128)S(1)} %get-tuple-element.58.mine_ref, f32[256,128]{1,0:T(8,128)S(1)} %collective-permute-done.13.other_ref, f32[1,2048]{1,0:T(1,128)S(1)} %bitcast.4), custom_call_target="tpu_custom_call" | custom-call | flops 1572864 | bytes 3145728 | tf_op jit(solution)/shard_map/pallas_call | solution.py:459
  (6 shorter events, 0.0 us)
Async XLA Ops:
  1.9 6.6 %collective-permute-start = (bf16[64,768]{1,0:T(8,128)(2,1)S(1)}, bf16[64,768]{1,0:T(8,128)(2,1)S(1)}, u32[]{:S(2)}, u32[]{:S(2)}) collective-permute-start(bf16[64,768]{1,0:T(8,128)(2,1)S(1)} %get-tuple-element.33), channel_id=1, source_target_pairs={{0,8},{8,0},{16,24},{24,16},{1,9},{9,1},{17,25},{25,17},{2,10},{10... | collective-permute-start | bytes 294920 | tf_op jit(solution)/shard_map/pooled_to_heads1/ppermute | solution.py:55
  5.0 5.7 %collective-permute-start.1 = (bf16[64,768]{1,0:T(8,128)(2,1)S(1)}, bf16[64,768]{1,0:T(8,128)(2,1)S(1)}, u32[]{:S(2)}, u32[]{:S(2)}) collective-permute-start(bf16[64,768]{1,0:T(8,128)(2,1)S(1)} %get-tuple-element.34), channel_id=1, source_target_pairs={{0,16},{8,24},{16,0},{24,8},{1,17},{9,25},{17,1},{25,9},{2,18},{10... | collective-permute-start | bytes 294920 | tf_op jit(solution)/shard_map/pooled_to_heads2/ppermute | solution.py:55
  6.5 5.5 %collective-permute-start.2 = (bf16[64,768]{1,0:T(8,128)(2,1)S(1)}, bf16[64,768]{1,0:T(8,128)(2,1)S(1)}, u32[]{:S(2)}, u32[]{:S(2)}) collective-permute-start(bf16[64,768]{1,0:T(8,128)(2,1)S(1)} %get-tuple-element.35), channel_id=1, source_target_pairs={{0,24},{8,16},{16,8},{24,0},{1,25},{9,17},{17,9},{25,1},{2,26},{10... | collective-permute-start | bytes 294920 | tf_op jit(solution)/shard_map/pooled_to_heads3/ppermute | solution.py:55
  6.5 13.2 %collective-permute-start.5 = (bf16[256,512]{1,0:T(8,128)(2,1)}, bf16[256,512]{1,0:T(8,128)(2,1)S(1)}, u32[]{:S(2)}, u32[]{:S(2)}) collective-permute-start(bf16[256,512]{1,0:T(8,128)(2,1)} %k0_hbm.1), channel_id=1, source_target_pairs={{0,2},{2,4},{4,6},{6,8},{8,10},{10,12},{12,14},{14,16},{16,18},{18... | collective-permute-start | bytes 786440 | tf_op jit(solution)/shard_map/first_keys/ppermute | solution.py:49
  12.0 13.3 %collective-permute-start.6 = (bf16[256,512]{1,0:T(8,128)(2,1)}, bf16[256,512]{1,0:T(8,128)(2,1)S(1)}, u32[]{:S(2)}, u32[]{:S(2)}) collective-permute-start(bf16[256,512]{1,0:T(8,128)(2,1)} %v0_hbm.1), channel_id=1, source_target_pairs={{0,2},{2,4},{4,6},{6,8},{8,10},{10,12},{12,14},{14,16},{16,18},{18... | collective-permute-start | bytes 786440 | tf_op jit(solution)/shard_map/first_values/ppermute | solution.py:49
  13.6 17.4 %collective-permute-start.4 = (bf16[272,256]{1,0:T(8,128)(2,1)S(1)}, bf16[272,256]{1,0:T(8,128)(2,1)S(1)}, u32[]{:S(2)}, u32[]{:S(2)}) collective-permute-start(bf16[272,256]{1,0:T(8,128)(2,1)S(1)} %shard_map.83.refs_4_), channel_id=1, source_target_pairs={{0,2},{2,0},{4,6},{6,4},{1,3},{3,1},{5,7},{7,5},{8,10},{10,8},{12,... | collective-permute-start | bytes 417800 | tf_op jit(solution)/shard_map/pooled_near1/ppermute | solution.py:55
  15.2 15.7 %collective-permute-start.3 = (bf16[272,256]{1,0:T(8,128)(2,1)S(1)}, bf16[272,256]{1,0:T(8,128)(2,1)S(1)}, u32[]{:S(2)}, u32[]{:S(2)}) collective-permute-start(bf16[272,256]{1,0:T(8,128)(2,1)S(1)} %shard_map.83.refs_4_), channel_id=1, source_target_pairs={{0,4},{2,6},{4,0},{6,2},{1,5},{3,7},{5,1},{7,3},{8,12},{10,14},{12... | collective-permute-start | bytes 417800 | tf_op jit(solution)/shard_map/pooled_far2/ppermute | solution.py:55
  31.0 7.2 %collective-permute-start.8 = (bf16[272,256]{1,0:T(8,128)(2,1)S(1)}, bf16[272,256]{1,0:T(8,128)(2,1)S(1)}, u32[]{:S(2)}, u32[]{:S(2)}) collective-permute-start(bf16[272,256]{1,0:T(8,128)(2,1)S(1)} %collective-permute-done.3.refs_6_), channel_id=1, source_target_pairs={{0,2},{2,0},{4,6},{6,4},{1,3},{3,1},{5,7},{7,5},{8,10},{10,8},{12,... | collective-permute-start | bytes 417800 | tf_op jit(solution)/shard_map/pooled_farther1/ppermute | solution.py:55
  31.0 13.9 %collective-permute-start.7 = (bf16[256,512]{1,0:T(8,128)(2,1)S(1)}, bf16[256,512]{1,0:T(8,128)(2,1)S(1)}, u32[]{:S(2)}, u32[]{:S(2)}) collective-permute-start(bf16[256,512]{1,0:T(8,128)(2,1)S(1)} %collective-permute-done.5.k1_hbm), channel_id=1, source_target_pairs={{0,2},{2,4},{4,6},{6,8},{8,10},{10,12},{12,14},{14,16},{16,18},{18... | collective-permute-start | bytes 786440 | tf_op jit(solution)/shard_map/second_keys/ppermute | solution.py:49
  38.2 11.9 %collective-permute-start.9 = (bf16[256,512]{1,0:T(8,128)(2,1)S(1)}, bf16[256,512]{1,0:T(8,128)(2,1)S(1)}, u32[]{:S(2)}, u32[]{:S(2)}) collective-permute-start(bf16[256,512]{1,0:T(8,128)(2,1)S(1)} %collective-permute-done.6.v1_hbm), channel_id=1, source_target_pairs={{0,2},{2,4},{4,6},{6,8},{8,10},{10,12},{12,14},{14,16},{16,18},{18... | collective-permute-start | bytes 786440 | tf_op jit(solution)/shard_map/second_values/ppermute | solution.py:49
  40.7 8.5 %collective-permute-start.10 = (bf16[64,512]{1,0:T(8,128)(2,1)S(1)}, bf16[64,512]{1,0:T(8,128)(2,1)S(1)}, u32[]{:S(2)}, u32[]{:S(2)}) collective-permute-start(bf16[64,512]{1,0:T(8,128)(2,1)S(1)} %get-tuple-element.54), channel_id=1, source_target_pairs={{0,8},{8,0},{16,24},{24,16},{1,9},{9,1},{17,25},{25,17},{2,10},{10... | collective-permute-start | bytes 196616 | tf_op jit(solution)/shard_map/coarse_back1/ppermute | solution.py:55
  40.8 9.3 %collective-permute-start.11 = (bf16[64,512]{1,0:T(8,128)(2,1)S(1)}, bf16[64,512]{1,0:T(8,128)(2,1)S(1)}, u32[]{:S(2)}, u32[]{:S(2)}) collective-permute-start(bf16[64,512]{1,0:T(8,128)(2,1)S(1)} %get-tuple-element.55), channel_id=1, source_target_pairs={{0,16},{8,24},{16,0},{24,8},{1,17},{9,25},{17,1},{25,9},{2,18},{10... | collective-permute-start | bytes 196616 | tf_op jit(solution)/shard_map/coarse_back2/ppermute | solution.py:55
  43.2 7.0 %collective-permute-start.12 = (bf16[64,512]{1,0:T(8,128)(2,1)S(1)}, bf16[64,512]{1,0:T(8,128)(2,1)S(1)}, u32[]{:S(2)}, u32[]{:S(2)}) collective-permute-start(bf16[64,512]{1,0:T(8,128)(2,1)S(1)} %get-tuple-element.56), channel_id=1, source_target_pairs={{0,24},{8,16},{16,8},{24,0},{1,25},{9,17},{17,9},{25,1},{2,26},{10... | collective-permute-start | bytes 196616 | tf_op jit(solution)/shard_map/coarse_back3/ppermute | solution.py:55
  50.2 3.3 %copy-start = (f32[2048]{0:T(1024)S(1)}, f32[2048]{0:T(1024)}, u32[]{:S(2)}) copy-start(f32[2048]{0:T(1024)} %param.15) | copy-start | bytes 24580
  52.1 1.4 %collective-permute-start.13 = (f32[256,128]{1,0:T(8,128)S(1)}, f32[256,128]{1,0:T(8,128)S(1)}, u32[]{:S(2)}, u32[]{:S(2)}) collective-permute-start(f32[256,128]{1,0:T(8,128)S(1)} %get-tuple-element.58.mine_ref), channel_id=1, source_target_pairs={{0,1},{1,0},{2,3},{3,2},{4,5},{5,4},{6,7},{7,6},{8,9},{9,8},{10,11... | collective-permute-start | bytes 393224 | tf_op jit(solution)/shard_map/squares1/ppermute | solution.py:55
